TPU v7x, 32 devices: a whole 2x2x4 slice. The times are simulated.
32 devices in a mesh: dp: 4 (over y, core), expert: 8 (over z, x).
Axes of the slice: x: 2, y: 2, z: 4, core: 2. Of those that a mesh axis runs over, the one named last changes fastest.
Arguments:
- tokens: bfloat16 [512, 7168], P('expert', 'dp'), may hold values from -6 to 6
- expert_ids: int32 [512, 8], P('expert'), may hold values from 0 to 63, all different within a row; in each aligned block of 64 rows (0 to 63, 64 to 127, ...) at most 10 rows name the same one
- combine_weights: float32 [512, 8], P('expert'), may hold values from 0.05 to 0.6
- w_gate: bfloat16 [64, 7168, 1024], P('expert', 'dp'), may hold values from -0.0625 to 0.0625
- w_up: bfloat16 [64, 7168, 1024], P('expert', 'dp'), may hold values from -0.0625 to 0.0625
- w_down: bfloat16 [64, 1024, 7168], P('expert', None, 'dp'), may hold values from -0.1875 to 0.1875
Outputs:
- combined: bfloat16 [512, 7168], P('expert', 'dp')
Inputs may be any that keep to these rules, and one draw needn't show every extreme that they name: `expert_ids`: each row names 8 different experts. Within the rows of one device (aligned blocks of 64 rows) no expert is named by more than 10 rows, a bound that some block reaches.
All inputs are finite; a program needn't handle non-finite values.
Results may differ from a plain program's by a relative error of at most 0.0057.
Values may be sent and summed in bfloat16 or wider, within the bound.
No kernel may reach another device: no remote copies, remote signals or barrier semaphores. Data moves between devices by JAX's collectives and lax.ppermute only.
A program may use at most 192 MiB of HBM per device.

v0:
```python
import jax
import jax.numpy as jnp
from jax import lax
from jax.sharding import PartitionSpec as P

CAP = 10


def shards(tokens, expert_ids, combine_weights, w_gate, w_up, w_down):
    tok_rows, width_part = tokens.shape
    top_count = expert_ids.shape[1]
    local_experts = w_gate.shape[0]
    owners = lax.axis_size("expert")
    experts = local_experts * owners
    expert_iota = lax.broadcasted_iota(jnp.int32, (1, 1, experts), 2)
    matches = (expert_ids[:, :, None] == expert_iota).astype(jnp.int32)
    per_token = jnp.sum(matches, axis=1)
    before = jnp.cumsum(per_token, axis=0) - per_token
    position = jnp.sum(matches * before[:, None, :], axis=2)
    slot_index = expert_ids * CAP + position
    slot_iota = lax.broadcasted_iota(jnp.int32, (experts * CAP, 1, 1), 0)
    placed = jnp.any(slot_index[None, :, :] == slot_iota, axis=2).astype(jnp.bfloat16)
    outgoing = jnp.dot(placed, tokens, preferred_element_type=jnp.float32).astype(jnp.bfloat16)
    incoming = lax.all_to_all(outgoing, "expert", split_axis=0, concat_axis=0, tiled=True)
    arrived = incoming.reshape(owners, local_experts, CAP, width_part)
    gate_part = jnp.einsum("hecd,edf->hecf", arrived, w_gate, preferred_element_type=jnp.float32)
    up_part = jnp.einsum("hecd,edf->hecf", arrived, w_up, preferred_element_type=jnp.float32)
    gate_sum, up_sum = (
        lax.psum_scatter(gate_part, "dp", scatter_dimension=0, tiled=True),
        lax.psum_scatter(up_part, "dp", scatter_dimension=0, tiled=True),
    )
    shares = (jax.nn.silu(gate_sum) * up_sum).astype(jnp.bfloat16)
    hidden = lax.all_gather(shares, "dp", axis=0, tiled=True)
    outputs = jnp.einsum(
        "hecf,efd->hecd", hidden, w_down, preferred_element_type=jnp.float32
    ).astype(jnp.bfloat16)
    returned = lax.all_to_all(
        outputs.reshape(owners * local_experts * CAP, width_part),
        "expert",
        split_axis=0,
        concat_axis=0,
        tiled=True,
    )
    picked = jnp.take(returned, slot_index.reshape(-1), axis=0).reshape(
        tok_rows, top_count, width_part
    )
    combined = jnp.sum(combine_weights[:, :, None] * picked.astype(jnp.float32), axis=1)
    return combined.astype(jnp.bfloat16)


def solution(mesh):
    placed = (
        P("expert", "dp"),
        P("expert", None),
        P("expert", None),
        P("expert", "dp", None),
        P("expert", "dp", None),
        P("expert", None, "dp"),
    )
    return jax.shard_map(
        shards, mesh=mesh, in_specs=placed, out_specs=P("expert", "dp"), check_vma=False
    )
```

profile of v0, /device:TPU:0, one launch (start us, length us, event | category | flops | bytes accessed | tf_op | source)
XLA Modules:
  0.0 270.6 jit_solution(7474550377380929620)
XLA Ops:
  6.5 0.8 copy.64
  7.4 0.2 convert_reduce_fusion
  7.6 1.2 select_reduce_fusion
  8.9 0.7 compare_and_fusion
  9.7 0.5 fusion.25
  10.2 0.8 convolution_convert_fusion
  11.0 59.6 %all_to_all.21 = bf16[8,80,1792]{2,1,0:T(8,128)(2,1)S(1)} all-to-all(bf16[8,80,1792]{2,1,0:T(8,128)(2,1)S(1)} %bitcast.43), channel_id=1, replica_groups=mesh['dp'=4,'expert'=8] {'expert'}, dimensions={0} | all-to-all | bytes 4587520 | tf_op jit(solution)/shard_map/all_to_all | solution.py:24
  70.6 0.7 copy.68
  71.3 11.5 %fusion.14 = f32[8,8,10,1024]{3,2,0,1:T(8,128)S(1)} fusion(bf16[8,1792,1024]{2,1,0:T(8,128)(2,1)} %param.9, bf16[8,8,10,1792]{3,0,2,1:T(8,128)(2,1)S(1)} %bitcast.41), kind=kOutput, calls=%fused_computation.13 | convolution fusion | flops 2348810240 | bytes 34275328 | tf_op jit(solution)/shard_map/hecd,edf->hecf/dot_general | solution.py:26
  82.8 3.0 %copy.70 = f32[8,8,10,1024]{3,1,2,0:T(8,128)} copy(f32[8,8,10,1024]{3,2,0,1:T(8,128)S(1)} %fusion.14) | data formatting | bytes 5242880 | tf_op jit(solution)/shard_map/hecd,edf->hecf/transpose | solution.py:26
  85.8 12.8 %fusion.19 = f32[8,8,10,1024]{3,2,0,1:T(8,128)S(1)} fusion(bf16[8,1792,1024]{2,1,0:T(8,128)(2,1)} %param.10, bf16[8,8,10,1792]{3,0,2,1:T(8,128)(2,1)S(1)} %bitcast.42), kind=kOutput, calls=%fused_computation.14 | convolution fusion | flops 2348810240 | bytes 34275328 | tf_op jit(solution)/shard_map/hecd,edf->hecf/dot_general | solution.py:27
  98.6 3.0 %copy.72 = f32[8,8,10,1024]{3,1,2,0:T(8,128)} copy(f32[8,8,10,1024]{3,2,0,1:T(8,128)S(1)} %fusion.19) | data formatting | bytes 5242880 | tf_op jit(solution)/shard_map/hecd,edf->hecf/transpose | solution.py:27
  101.7 0.2 all-gather.2.cloned.1.call-start
  101.9 17.6 %reduce-scatter.3.cloned.1.call-done = f32[2,8,10,1024]{3,1,2,0:T(8,128)} async-done(((f32[8,8,10,1024]{3,1,2,0:T(8,128)}), f32[2,8,10,1024]{3,1,2,0:T(8,128)}) %reduce-scatter.3.cloned.1.call-update) | async-done | bytes 655376 | tf_op jit(solution)/shard_map/reduce_scatter | solution.py:29
  119.5 37.4 %reduce-scatter.5.cloned.1.call-done = f32[2,8,10,1024]{3,1,2,0:T(8,128)} async-done(((f32[8,8,10,1024]{3,1,2,0:T(8,128)}), f32[2,8,10,1024]{3,1,2,0:T(8,128)}) %reduce-scatter.5.cloned.1.call-update) | async-done | bytes 655376 | tf_op jit(solution)/shard_map/reduce_scatter | solution.py:30
  156.9 2.2 multiply_convert_fusion
  159.2 18.4 %all-gather.2.cloned.1.call-done = bf16[8,8,10,1024]{3,1,2,0:T(8,128)(2,1)} async-done(((bf16[2,8,10,1024]{3,1,2,0:T(8,128)(2,1)}), bf16[8,8,10,1024]{3,1,2,0:T(8,128)(2,1)}) %all-gather.2.cloned.1.call-update) | async-done | bytes 1310736 | tf_op jit(solution)/shard_map/all_gather | solution.py:33
  177.5 16.5 %fusion.11 = bf16[8,8,10,1792]{3,2,0,1:T(8,128)(2,1)} fusion(bf16[8,1024,1792]{2,1,0:T(8,128)(2,1)} %param.11, bf16[8,8,10,1024]{3,1,2,0:T(8,128)(2,1)} %all-gather.2.cloned.1.call-done), kind=kOutput, calls=%fused_computation.11 | convolution fusion | flops 2349957120 | bytes 32964608 | tf_op jit(solution)/shard_map/hecf,efd->hecd/dot_general | solution.py:34
  194.0 2.7 %copy.74 = bf16[8,8,10,1792]{3,0,2,1:T(8,128)(2,1)S(1)} copy(bf16[8,8,10,1792]{3,2,0,1:T(8,128)(2,1)} %fusion.11) | data formatting | bytes 4587520 | tf_op jit(solution)/shard_map/convert_element_type | solution.py:36
  196.8 1.8 copy.75
  198.5 5.6 %all-to-all-start.1 = ((bf16[8,80,1792]{2,1,0:T(8,128)(2,1)}), bf16[8,80,1792]{2,1,0:T(8,128)(2,1)S(1)}, u32[]{:S(2)}, u32[]{:S(2)}) async-start(bf16[8,80,1792]{2,1,0:T(8,128)(2,1)} %copy.75), calls=%async_computation.3 | async-start | bytes 4587520 | tf_op jit(solution)/shard_map/all_to_all | solution.py:37
  204.5 52.6 %all-to-all-done.1 = bf16[8,80,1792]{2,1,0:T(8,128)(2,1)S(1)} async-done(((bf16[8,80,1792]{2,1,0:T(8,128)(2,1)}), bf16[8,80,1792]{2,1,0:T(8,128)(2,1)S(1)}, u32[]{:S(2)}, u32[]{:S(2)}) %all-to-all-start.1) | async-done | bytes 2293792 | tf_op jit(solution)/shard_map/all_to_all | solution.py:37
  257.0 3.2 %gather_fusion = bf16[512,1792]{1,0:T(8,128)(2,1)} fusion(bf16[640,1792]{1,0:T(8,128)(2,1)S(1)} %bitcast.40, s32[1024]{0:T(1024)S(1)} %pad_clamp_fusion), kind=kCustom, calls=%fused_computation | custom fusion | bytes 3672064 | tf_op jit(solution)/shard_map/jit(_take)/gather | solution.py:44
  260.2 3.8 %multiply_reduce_fusion = bf16[64,1792]{1,0:T(8,128)(2,1)} fusion(bf16[512,1792]{1,0:T(8,128)(2,1)} %gather_fusion, f32[64,8]{1,0:T(8,128)S(1)} %copy.63, pred[64,8]{1,0:T(8,128)(4,1)S(1)} %copy.66), kind=kLoop, calls=%fused_computation.10 | loop fusion | flops 3555328 | bytes 2066944 | tf_op jit(solution)/shard_map/reduce_sum | solution.py:47
  (20 shorter events, 0.6 us)
Async XLA Ops:
  6.5 3.6 %copy-start = (bf16[64,1792]{1,0:T(8,128)(2,1)S(1)}, bf16[64,1792]{1,0:T(8,128)(2,1)}, u32[]{:S(2)}) copy-start(bf16[64,1792]{1,0:T(8,128)(2,1)} %param.6) | copy-start | bytes 688132
  6.5 113.0 %reduce-scatter.3.cloned.1.call-start = ((), (), s32[]{:S(2)}) async-start(), calls=%async_computation.4 | async-start | bytes 3276800 | tf_op jit(solution)/shard_map/reduce_scatter | solution.py:29
  85.8 71.2 %reduce-scatter.5.cloned.1.call-start = ((), (), s32[]{:S(2)}) async-start(), calls=%async_computation.5 | async-start | bytes 3276800 | tf_op jit(solution)/shard_map/reduce_scatter | solution.py:30
  101.7 75.8 %all-gather.2.cloned.1.call-start = ((), (), s32[]{:S(2)}) async-start(), calls=%async_computation.6 | async-start | bytes 1638400 | tf_op jit(solution)/shard_map/all_gather | solution.py:33
  198.5 5.8 %copy-start.2 = (f32[64,8]{0,1:T(8,128)S(1)}, f32[64,8]{0,1:T(8,128)}, u32[]{:S(2)}) copy-start(f32[64,8]{0,1:T(8,128)} %param.8) | copy-start | bytes 6148
  198.5 58.5 %all-to-all-start.1 = ((bf16[8,80,1792]{2,1,0:T(8,128)(2,1)}), bf16[8,80,1792]{2,1,0:T(8,128)(2,1)S(1)}, u32[]{:S(2)}, u32[]{:S(2)}) async-start(bf16[8,80,1792]{2,1,0:T(8,128)(2,1)} %copy.75), calls=%async_computation.3 | async-start | bytes 4587520 | tf_op jit(solution)/shard_map/all_to_all | solution.py:37
  257.0 7.0 %copy-start.1 = (bf16[64,1792]{1,0:T(8,128)(2,1)S(1)}, bf16[64,1792]{1,0:T(8,128)(2,1)}, u32[]{:S(2)}) copy-start(bf16[64,1792]{1,0:T(8,128)(2,1)} %param.6) | copy-start | bytes 688132
Sparse Core Ops, SparseCore 0:
  85.9 33.6 reduce-scatter.2
  122.2 34.6 reduce-scatter.4
  159.3 18.2 all-gather.1
where the time goes:
time: 271 us
  waiting for transfers between devices  126 us (46%)
  blocking collectives  59.6 us (22%)
  matrix products  41.6 us (15%)
  local copies, waits for them, and re-layouts  15.6 us (6%)
  between operations  13.2 us (5%)
  other arithmetic  8.67 us (3%)
  starting transfers between devices  5.91 us (2%)
    all_to_all x1, blocking collectives, shards(): lax.all_to_all(outgoing, 'expert', split_axis=0, concat_axis=0, tiled=True)  59.6 us
    all_to_all x1, waiting for transfers between devices, shards(): lax.all_to_all(outputs.reshape(owners * local_experts * CAP, width_part),...  52.6 us
    reduce_scatter x1, waiting for transfers between devices, shards(): lax.psum_scatter(up_part, 'dp', scatter_dimension=0, tiled=True)  37.4 us
    all_gather x1, waiting for transfers between devices, shards(): hidden = lax.all_gather(shares, 'dp', axis=0, tiled=True)  18.4 us
    reduce_scatter x1, waiting for transfers between devices, shards(): lax.psum_scatter(gate_part, 'dp', scatter_dimension=0, tiled=True)  17.6 us
    dot_general x1, matrix products, shards(): jnp.einsum('hecf,efd->hecd', hidden, w_down, preferred_element_type=jnp.f...  16.5 us
    dot_general x1, matrix products, shards(): jnp.einsum('hecd,edf->hecf', arrived, w_up, preferred_element_type=jnp.fl...  12.8 us
    dot_general x1, matrix products, shards(): jnp.einsum('hecd,edf->hecf', arrived, w_gate, preferred_element_type=jnp....  11.5 us
  transfers between devices with their start and end apart: 4, of which 4 were waited for; matrix products, arithmetic and copies ran while one was open for 6% of the time, Pallas kernels for 0%

commit v1 on v0

--- a/solution.py
+++ b/solution.py
@@ -1,12 +1,19 @@
+import functools
+
 import jax
 import jax.numpy as jnp
 from jax import lax
+from jax.experimental import pallas as pl
+from jax.experimental.pallas import tpu as pltpu
 from jax.sharding import PartitionSpec as P
 
 CAP = 10
-
-
-def shards(tokens, expert_ids, combine_weights, w_gate, w_up, w_down):
+NEAR = 4
+LANES = 128
+COLUMN_PARTS = 2
+
+
+def plain_shards(tokens, expert_ids, combine_weights, w_gate, w_up, w_down):
     tok_rows, width_part = tokens.shape
     top_count = expert_ids.shape[1]
     local_experts = w_gate.shape[0]
@@ -48,6 +55,311 @@
     return combined.astype(jnp.bfloat16)
 
 
+def swap(value, axis, distance):
+    size = lax.axis_size(axis)
+    return lax.ppermute(value, axis, [(i, i ^ distance) for i in range(size)])
+
+
+def project_kernel(top, group, rows, place, *refs):
+    blocks = refs[: -7 - group // 2]
+    w_gate, w_up, send = refs[-7 - group // 2 : -4 - group // 2]
+    keeps = refs[-4 - group // 2 : -4]
+    scale, slots, held, picked = refs[-4:]
+    step = pl.program_id(0)
+    member, first = place[0], place[1]
+    depth = w_gate.shape[1]
+    ff = w_gate.shape[2]
+    tok_rows = blocks[0].shape[0]
+    total = held.shape[0]
+
+    @pl.when(step == 0)
+    def _():
+        for k, block in enumerate(blocks):
+            held[k * tok_rows : (k + 1) * tok_rows, :] = block[...]
+        meta = held[:, depth:].astype(jnp.float32)
+        lane = lax.broadcasted_iota(jnp.int32, (1, LANES), 1)
+        named = jnp.where(lane < group, first + (lane ^ member), -1).astype(jnp.float32)
+        match = jnp.zeros((total, LANES), jnp.float32)
+        for k in range(top):
+            match = match + jnp.where(meta[:, k : k + 1] == named, 1.0, 0.0)
+        row = lax.broadcasted_iota(jnp.int32, (total, total), 0)
+        col = lax.broadcasted_iota(jnp.int32, (total, total), 1)
+        earlier = jnp.where(row > col, 1.0, 0.0).astype(jnp.bfloat16)
+        position = jnp.dot(
+            earlier, match.astype(jnp.bfloat16), preferred_element_type=jnp.float32
+        )
+        position = jnp.where(match > 0.0, position, -1.0).astype(jnp.bfloat16)
+        width = group * rows
+        wide_row = lax.broadcasted_iota(jnp.int32, (LANES, width), 0)
+        wide_col = lax.broadcasted_iota(jnp.int32, (LANES, width), 1)
+        inside = (wide_col >= wide_row * rows) & (wide_col < (wide_row + 1) * rows)
+        spread = jnp.where(inside, 1.0, 0.0).astype(jnp.bfloat16)
+        wide = jnp.dot(position, spread, preferred_element_type=jnp.float32)
+        slot = lax.broadcasted_iota(jnp.int32, (1, width), 1)
+        for j in range(1, group):
+            slot = slot - jnp.where(
+                lax.broadcasted_iota(jnp.int32, (1, width), 1) >= j * rows, rows, 0
+            )
+        one_hot = jnp.where(wide == slot.astype(jnp.float32), 1.0, 0.0).astype(jnp.bfloat16)
+        slots[...] = one_hot
+        picked[...] = lax.dot_general(
+            one_hot,
+            held[...],
+            (((0,), (0,)), ((), ())),
+            preferred_element_type=jnp.float32,
+        ).astype(jnp.bfloat16)
+        own = picked[:rows, depth:].astype(jnp.float32)
+        weight = (
+            own[:, top : 2 * top] + own[:, 2 * top : 3 * top]
+        ) + own[:, 3 * top : 4 * top]
+        mine = (first + member).astype(jnp.float32)
+        weight = jnp.sum(
+            jnp.where(own[:, :top] == mine, weight, 0.0), axis=1, keepdims=True
+        )
+        scale[...] = jnp.broadcast_to(weight, scale.shape)
+
+    half = group // 2
+    relative = jnp.where(step < half, 2 * step + 1, 2 * (group - 1 - step))
+    start = pl.multiple_of(relative * rows, 16)
+    x = picked[pl.ds(start, rows), :depth]
+    gate = jnp.dot(x, w_gate[0], preferred_element_type=jnp.float32)
+    up = jnp.dot(x, w_up[0], preferred_element_type=jnp.float32)
+
+    @pl.when(step < half)
+    def _():
+        send[pl.ds(step, 1), :, :ff] = gate.astype(send.dtype)[None]
+        send[pl.ds(step, 1), :, ff:] = up.astype(send.dtype)[None]
+
+    for j in range(half):
+
+        @pl.when(step == group - 1 - j)
+        def _(j=j):
+            keeps[j][:, :ff] = gate
+            keeps[j][:, ff:] = up
+
+
+def project(blocks, place, w_gate, w_up, top, group, rows):
+    depth, ff = w_gate.shape[1:]
+    tok_rows, wide = blocks[0].shape
+    total = tok_rows * len(blocks)
+    half = group // 2
+
+    def weight_index(step, place):
+        relative = jnp.where(step < half, 2 * step + 1, 2 * (group - 1 - step))
+        return place[2] + (relative ^ place[0]), 0, 0
+
+    def whole(step, place):
+        return 0, 0
+
+    out_shape = (
+        [jax.ShapeDtypeStruct((half, rows, 2 * ff), jnp.bfloat16)]
+        + [jax.ShapeDtypeStruct((rows, 2 * ff), jnp.float32)] * half
+        + [
+            jax.ShapeDtypeStruct((rows, LANES), jnp.float32),
+            jax.ShapeDtypeStruct((total, group * rows), jnp.bfloat16),
+        ]
+    )
+    outs = pl.pallas_call(
+        functools.partial(project_kernel, top, group, rows),
+        out_shape=out_shape,
+        grid_spec=pltpu.PrefetchScalarGridSpec(
+            num_scalar_prefetch=1,
+            grid=(group,),
+            in_specs=[pl.BlockSpec((tok_rows, wide), whole)] * len(blocks)
+            + [pl.BlockSpec((1, depth, ff), weight_index)] * 2,
+            out_specs=[pl.BlockSpec((half, rows, 2 * ff), lambda step, place: (0, 0, 0))]
+            + [pl.BlockSpec(s.shape, whole) for s in out_shape[1:]],
+            scratch_shapes=[
+                pltpu.VMEM((total, wide), jnp.bfloat16),
+                pltpu.VMEM((group * rows, wide), jnp.bfloat16),
+            ],
+        ),
+        compiler_params=pltpu.CompilerParams(vmem_limit_bytes=48 * 2**20),
+        cost_estimate=pl.CostEstimate(
+            flops=4 * group * rows * depth * ff,
+            bytes_accessed=4 * group * depth * ff,
+            transcendentals=0,
+        ),
+        name="project",
+    )(place, *blocks, w_gate, w_up)
+    return outs[0], outs[1 : 1 + half], outs[-2], outs[-1]
+
+
+def down_kernel(count, chunks, rows, place, *refs):
+    hidden = refs[:count]
+    slots = refs[count : count + chunks]
+    w_down = refs[count + chunks]
+    outs = refs[count + chunks + 1 : -2]
+    held, result = refs[-2:]
+    step = pl.program_id(0)
+
+    @pl.when(step == 0)
+    def _():
+        for k, part in enumerate(hidden):
+            held[k * rows : (k + 1) * rows, :] = part[...]
+
+    start = pl.multiple_of(step * rows, 16)
+    result[pl.ds(start, rows), :] = jnp.dot(
+        held[pl.ds(start, rows), :], w_down[0], preferred_element_type=jnp.float32
+    ).astype(jnp.bfloat16)
+
+    @pl.when(step == count - 1)
+    def _():
+        span = count * rows // chunks
+        total = jnp.dot(slots[0][...], result[:span, :], preferred_element_type=jnp.float32)
+        for c in range(1, chunks):
+            total = total + jnp.dot(
+                slots[c][...],
+                result[c * span : (c + 1) * span, :],
+                preferred_element_type=jnp.float32,
+            )
+        tok_rows = outs[0].shape[0]
+        for k, out in enumerate(outs):
+            out[...] = total[k * tok_rows : (k + 1) * tok_rows, :].astype(out.dtype)
+
+
+def down(hidden, slots, place, w_down, part, columns, owners, group):
+    rows, ff = hidden[0].shape
+    count = len(hidden)
+    total = slots[0].shape[0]
+    tok_rows = total // owners
+
+    def weight_index(step, place):
+        return (step // group) * group + ((step % group) ^ place[0]), 0, part
+
+    def whole(step, place):
+        return 0, 0
+
+    out_shape = [
+        jax.ShapeDtypeStruct(
+            (tok_rows, columns), jnp.float32 if k % NEAR == 0 else jnp.bfloat16
+        )
+        for k in range(owners)
+    ]
+    return pl.pallas_call(
+        functools.partial(down_kernel, count, len(slots), rows),
+        out_shape=out_shape,
+        grid_spec=pltpu.PrefetchScalarGridSpec(
+            num_scalar_prefetch=1,
+            grid=(count,),
+            in_specs=[pl.BlockSpec((rows, ff), whole)] * count
+            + [pl.BlockSpec(s.shape, whole) for s in slots]
+            + [pl.BlockSpec((1, ff, columns), weight_index)],
+            out_specs=[pl.BlockSpec((tok_rows, columns), whole)] * owners,
+            scratch_shapes=[
+                pltpu.VMEM((count * rows, ff), jnp.bfloat16),
+                pltpu.VMEM((count * rows, columns), jnp.bfloat16),
+            ],
+        ),
+        compiler_params=pltpu.CompilerParams(vmem_limit_bytes=48 * 2**20),
+        cost_estimate=pl.CostEstimate(
+            flops=2 * count * rows * columns * (ff + total),
+            bytes_accessed=2 * count * ff * columns,
+            transcendentals=0,
+        ),
+        name="down",
+    )(place, *hidden, *slots, w_down)
+
+
+def split_three(value):
+    high = value.astype(jnp.bfloat16)
+    rest = value - high.astype(jnp.float32)
+    middle = rest.astype(jnp.bfloat16)
+    low = (rest - middle.astype(jnp.float32)).astype(jnp.bfloat16)
+    return high, middle, low
+
+
+def shards(tokens, expert_ids, combine_weights, w_gate, w_up, w_down):
+    tok_rows, depth = tokens.shape
+    top = expert_ids.shape[1]
+    local_experts = w_gate.shape[0]
+    ff = w_gate.shape[2]
+    owners = lax.axis_size("expert")
+    group = lax.axis_size("dp")
+    rows = owners * CAP
+    chunks = local_experts // group
+    member = lax.axis_index("dp")
+    first = lax.axis_index("expert") * local_experts
+    places = [
+        jnp.stack([member, first + c * group, jnp.int32(c * group)]) for c in range(chunks)
+    ]
+
+    meta = jnp.concatenate(
+        (expert_ids.astype(jnp.bfloat16),) + split_three(combine_weights), axis=1
+    )
+    meta = jnp.pad(meta, ((0, 0), (0, LANES - meta.shape[1])))
+    own = jnp.concatenate((tokens, meta), axis=1)
+    blocks = {0: own}
+    for far in range(NEAR, owners, NEAR):
+        blocks[far] = swap(own, "expert", far)
+    for far in range(0, owners, NEAR):
+        for near in range(1, NEAR):
+            blocks[far + near] = swap(blocks[far], "expert", near)
+    ordered = [blocks[k] for k in range(owners)]
+
+    hidden, slots = [], []
+    for c in range(chunks):
+        send, keeps, scale, one_hot = project(
+            ordered, places[c], w_gate, w_up, top, group, rows
+        )
+        slots.append(one_hot)
+        received = swap(send, "dp", 1).astype(jnp.float32)
+        both = keeps[0] + received[0]
+        for j in range(1, group // 2):
+            part = (keeps[j] + received[j]).astype(jnp.bfloat16)
+            both = both + swap(part, "dp", 2 * j).astype(jnp.float32)
+        shares = jax.nn.silu(both[:, :ff]) * both[:, ff:] * scale[:, :1]
+        gathered = {0: shares.astype(jnp.bfloat16)}
+        for j in range(1, group // 2):
+            gathered[2 * j] = swap(gathered[0], "dp", 2 * j)
+        for j in range(group // 2):
+            gathered[2 * j + 1] = swap(gathered[2 * j], "dp", 1)
+        hidden += [gathered[k] for k in range(group)]
+
+    columns = depth // COLUMN_PARTS
+    done = []
+    for part in range(COLUMN_PARTS):
+        partial = down(hidden, slots, places[0], w_down, part, columns, owners, group)
+        total = partial[0]
+        sums = {}
+        for far in range(NEAR, owners, NEAR):
+            sums[far] = partial[far]
+            for near in range(1, NEAR):
+                sums[far] = sums[far] + swap(partial[far + near], "expert", near).astype(
+                    jnp.float32
+                )
+        for near in range(1, NEAR):
+            total = total + swap(partial[near], "expert", near).astype(jnp.float32)
+        for far in range(NEAR, owners, NEAR):
+            total = total + swap(sums[far].astype(jnp.bfloat16), "expert", far).astype(
+                jnp.float32
+            )
+        done.append(total.astype(jnp.bfloat16))
+    return jnp.concatenate(done, axis=1)
+
+
+def fits(owners, group, tokens, expert_ids, w_gate):
+    powers = all(k & (k - 1) == 0 for k in (owners, group))
+    return (
+        powers
+        and owners >= NEAR
+        and group >= 2
+        and w_gate.shape[0] % group == 0
+        and tokens.shape[0] % 16 == 0
+        and (owners * CAP) % 16 == 0
+        and owners * CAP < 256
+        and owners * w_gate.shape[0] <= 256
+        and 4 * expert_ids.shape[1] <= LANES
+        and tokens.shape[1] % (COLUMN_PARTS * LANES) == 0
+    )
+
+
+def layer(tokens, expert_ids, combine_weights, w_gate, w_up, w_down):
+    owners, group = lax.axis_size("expert"), lax.axis_size("dp")
+    chosen = shards if fits(owners, group, tokens, expert_ids, w_gate) else plain_shards
+    return chosen(tokens, expert_ids, combine_weights, w_gate, w_up, w_down)
+
+
 def solution(mesh):
     placed = (
         P("expert", "dp"),
@@ -58,5 +370,5 @@
         P("expert", None, "dp"),
     )
     return jax.shard_map(
-        shards, mesh=mesh, in_specs=placed, out_specs=P("expert", "dp"), check_vma=False
-    )
+        layer, mesh=mesh, in_specs=placed, out_specs=P("expert", "dp"), check_vma=False
+    )

time: 271 us -> 141 us (0.52)
  waiting for transfers between devices: 126 us -> 46.7 us
  blocking collectives: 59.6 us -> 0 us
  Pallas kernels: 0 us -> 49.3 us
  matrix products: 41.6 us -> 0 us
  starting transfers between devices: 5.91 us -> 38.6 us
  local copies, waits for them, and re-layouts: 15.6 us -> 1.28 us
  between operations: 13.2 us -> 0.18 us
  other arithmetic: 8.67 us -> 4.5 us
    all_to_all x1 -> x0, blocking collectives: 59.6 us -> none  [shards(): lax.all_to_all(outgoing, 'expert', split_axis=0, concat_axis=0, tiled=True)]
    reduce_scatter x2 -> x0, waiting for transfers between devices: 55 us -> none  [the longest x1 37.4 us: shards(): lax.psum_scatter(up_part, 'dp', scatter_dimension=0, tiled=True)]
    all_to_all x1 -> x0, waiting for transfers between devices: 52.6 us -> none  [shards(): lax.all_to_all(outputs.reshape(owners * local_experts * CAP, width_part),...]
    pallas_call x0 -> x4, Pallas kernels: none -> 49.3 us  [the longest x2 28.1 us: project(): pl.pallas_call(functools.partial(project_kernel, top, group, rows), out_s...]
    ppermute x0 -> x31, waiting for transfers between devices: none -> 46.7 us  [swap(): return lax.ppermute(value, axis, [(i, i ^ distance) for i in range(size)])]
    dot_general x4 -> x0, matrix products: 41.6 us -> none  [the longest x1 16.5 us: shards(): jnp.einsum('hecf,efd->hecd', hidden, w_down, preferred_element_type=jnp.f...]
    ppermute x0 -> x31, starting transfers between devices: none -> 38.6 us  [swap(): return lax.ppermute(value, axis, [(i, i ^ distance) for i in range(size)])]
    all_gather x1 -> x0, waiting for transfers between devices: 18.4 us -> none  [shards(): hidden = lax.all_gather(shares, 'dp', axis=0, tiled=True)]
  transfers between devices with their start and end apart: 4 -> 31, of which waited for: 4 -> 15; matrix products, arithmetic and copies ran while one was open for 6% -> 1% of each run, Pallas kernels for 0% -> 18%
where the time goes in v1:
time: 141 us; the launch traced here: 140 us
  Pallas kernels  49.3 us (35%)
  waiting for transfers between devices  46.7 us (33%)
  starting transfers between devices  38.6 us (27%)
  other arithmetic  4.5 us (3%)
    ppermute x31, waiting for transfers between devices, swap(): return lax.ppermute(value, axis, [(i, i ^ distance) for i in range(size)])  46.7 us
    ppermute x31, starting transfers between devices, swap(): return lax.ppermute(value, axis, [(i, i ^ distance) for i in range(size)])  38.6 us
    pallas_call x2, Pallas kernels, project(): pl.pallas_call(functools.partial(project_kernel, top, group, rows), out_s...  28.1 us
    pallas_call x2, Pallas kernels, down(): pl.pallas_call(functools.partial(down_kernel, count, len(slots), rows), o...  21.2 us
  transfers between devices with their start and end apart: 31, of which 15 were waited for; matrix products, arithmetic and copies ran while one was open for 1% of the time, Pallas kernels for 18%

profile of v1, /device:TPU:0, one launch (start us, length us, event | category | flops | bytes accessed | tf_op | source)
XLA Modules:
  0.0 140.5 jit_solution(6009681464188575300)
XLA Ops:
  3.5 4.1 %collective-permute-start.3 = (bf16[64,1920]{1,0:T(8,128)(2,1)S(1)}, bf16[64,1920]{1,0:T(8,128)(2,1)S(1)}, u32[]{:S(2)}, u32[]{:S(2)}) collective-permute-start(bf16[64,1920]{1,0:T(8,128)(2,1)S(1)} %pad_maximum_fusion.refs_0_), channel_id=1, source_target_pairs={{0,4},{1,5},{2,6},{3,7},{4,0},{5,1},{6,2},{7,3},{8,12},{9,13},{10,... | collective-permute-start | bytes 737288 | tf_op jit(solution)/shard_map/ppermute | solution.py:60
  9.1 1.6 %collective-permute-start.1 = (bf16[64,1920]{1,0:T(8,128)(2,1)S(1)}, bf16[64,1920]{1,0:T(8,128)(2,1)S(1)}, u32[]{:S(2)}, u32[]{:S(2)}) collective-permute-start(bf16[64,1920]{1,0:T(8,128)(2,1)S(1)} %pad_maximum_fusion.refs_0_), channel_id=1, source_target_pairs={{0,2},{1,3},{2,0},{3,1},{4,6},{5,7},{6,4},{7,5},{8,10},{9,11},{10,... | collective-permute-start | bytes 737288 | tf_op jit(solution)/shard_map/ppermute | solution.py:60
  11.1 7.8 %collective-permute-done.3.refs_4_ = bf16[64,1920]{1,0:T(8,128)(2,1)S(1)} collective-permute-done((bf16[64,1920]{1,0:T(8,128)(2,1)S(1)}, bf16[64,1920]{1,0:T(8,128)(2,1)S(1)}, u32[]{:S(2)}, u32[]{:S(2)}) %collective-permute-start.3) | collective-permute-done | bytes 245792 | tf_op jit(solution)/shard_map/ppermute | solution.py:60
  22.5 4.9 %collective-permute-done.2.refs_3_ = bf16[64,1920]{1,0:T(8,128)(2,1)S(1)} collective-permute-done((bf16[64,1920]{1,0:T(8,128)(2,1)S(1)}, bf16[64,1920]{1,0:T(8,128)(2,1)S(1)}, u32[]{:S(2)}, u32[]{:S(2)}) %collective-permute-start.2) | collective-permute-done | bytes 245792 | tf_op jit(solution)/shard_map/ppermute | solution.py:60
  27.4 3.8 %collective-permute-done.4.refs_5_ = bf16[64,1920]{1,0:T(8,128)(2,1)S(1)} collective-permute-done((bf16[64,1920]{1,0:T(8,128)(2,1)S(1)}, bf16[64,1920]{1,0:T(8,128)(2,1)S(1)}, u32[]{:S(2)}, u32[]{:S(2)}) %collective-permute-start.4) | collective-permute-done | bytes 245792 | tf_op jit(solution)/shard_map/ppermute | solution.py:60
  32.7 3.5 %collective-permute-done.6.refs_7_ = bf16[64,1920]{1,0:T(8,128)(2,1)S(1)} collective-permute-done((bf16[64,1920]{1,0:T(8,128)(2,1)S(1)}, bf16[64,1920]{1,0:T(8,128)(2,1)S(1)}, u32[]{:S(2)}, u32[]{:S(2)}) %collective-permute-start.6) | collective-permute-done | bytes 245792 | tf_op jit(solution)/shard_map/ppermute | solution.py:60
  36.2 14.0 %project.3 = (bf16[2,80,2048]{2,1,0:T(8,128)(2,1)S(1)}, f32[80,2048]{1,0:T(8,128)S(1)}, f32[80,2048]{1,0:T(8,128)S(1)}, f32[80,128]{1,0:T(8,128)S(1)}, bf16[512,320]{1,0:T(8,128)(2,1)S(1)}) custom-call(s32[3]{0:T(128)S(1)} %pad_add_fusion.1.place, bf16[64,1920]{1,0:T(8,128)(2,1)S(1)} %pad_maximum_fusion.refs_0_, ...), custom_call_target="tpu_custom_call" | custom-call | flops 2348810240 | bytes 29360128 | tf_op jit(solution)/shard_map/project/pallas_call | solution.py:162
  50.4 14.0 %project.2 = (bf16[2,80,2048]{2,1,0:T(8,128)(2,1)S(1)}, f32[80,2048]{1,0:T(8,128)S(1)}, f32[80,2048]{1,0:T(8,128)S(1)}, f32[80,128]{1,0:T(8,128)S(1)}, bf16[512,320]{1,0:T(8,128)(2,1)S(1)}) custom-call(s32[3]{0:T(128)S(1)} %pad_add_fusion.place, bf16[64,1920]{1,0:T(8,128)(2,1)S(1)} %pad_maximum_fusion.refs_0_, ...), custom_call_target="tpu_custom_call" | custom-call | flops 2348810240 | bytes 29360128 | tf_op jit(solution)/shard_map/project/pallas_call | solution.py:162
  65.5 1.6 %collective-permute-start.13 = (bf16[80,2048]{1,0:T(8,128)(2,1)S(1)}, bf16[80,2048]{1,0:T(8,128)(2,1)S(1)}, u32[]{:S(2)}, u32[]{:S(2)}) collective-permute-start(bf16[80,2048]{1,0:T(8,128)(2,1)S(1)} %fusion.1), channel_id=1, source_target_pairs={{0,16},{8,24},{16,0},{24,8},{1,17},{9,25},{17,1},{25,9},{2,18},{10... | collective-permute-start | bytes 983048 | tf_op jit(solution)/shard_map/ppermute | solution.py:60
  68.6 7.5 %collective-permute-done.13 = bf16[80,2048]{1,0:T(8,128)(2,1)S(1)} collective-permute-done((bf16[80,2048]{1,0:T(8,128)(2,1)S(1)}, bf16[80,2048]{1,0:T(8,128)(2,1)S(1)}, u32[]{:S(2)}, u32[]{:S(2)}) %collective-permute-start.13) | collective-permute-done | bytes 327712 | tf_op jit(solution)/shard_map/ppermute | solution.py:60
  76.4 1.6 %collective-permute-start.15 = (bf16[80,1024]{1,0:T(8,128)(2,1)S(1)}, bf16[80,1024]{1,0:T(8,128)(2,1)S(1)}, u32[]{:S(2)}, u32[]{:S(2)}) collective-permute-start(bf16[80,1024]{1,0:T(8,128)(2,1)S(1)} %fusion.9.refs_4_), channel_id=1, source_target_pairs={{0,16},{8,24},{16,0},{24,8},{1,17},{9,25},{17,1},{25,9},{2,18},{10... | collective-permute-start | bytes 491528 | tf_op jit(solution)/shard_map/ppermute | solution.py:60
  78.0 5.2 %collective-permute-done.8 = bf16[80,2048]{1,0:T(8,128)(2,1)S(1)} collective-permute-done((bf16[80,2048]{1,0:T(8,128)(2,1)S(1)}, bf16[80,2048]{1,0:T(8,128)(2,1)S(1)}, u32[]{:S(2)}, u32[]{:S(2)}) %collective-permute-start.8) | collective-permute-done | bytes 327712 | tf_op jit(solution)/shard_map/ppermute | solution.py:60
  83.4 1.6 %collective-permute-start.10 = (bf16[80,1024]{1,0:T(8,128)(2,1)S(1)}, bf16[80,1024]{1,0:T(8,128)(2,1)S(1)}, u32[]{:S(2)}, u32[]{:S(2)}) collective-permute-start(bf16[80,1024]{1,0:T(8,128)(2,1)S(1)} %fusion.11.refs_0_), channel_id=1, source_target_pairs={{0,16},{8,24},{16,0},{24,8},{1,17},{9,25},{17,1},{25,9},{2,18},{10... | collective-permute-start | bytes 491528 | tf_op jit(solution)/shard_map/ppermute | solution.py:60
  86.7 2.6 %collective-permute-done.10.refs_2_ = bf16[80,1024]{1,0:T(8,128)(2,1)S(1)} collective-permute-done((bf16[80,1024]{1,0:T(8,128)(2,1)S(1)}, bf16[80,1024]{1,0:T(8,128)(2,1)S(1)}, u32[]{:S(2)}, u32[]{:S(2)}) %collective-permute-start.10) | collective-permute-done | bytes 163872 | tf_op jit(solution)/shard_map/ppermute | solution.py:60
  90.6 10.6 %down.2 = (f32[64,896]{1,0:T(8,128)S(1)}, bf16[64,896]{1,0:T(8,128)(2,1)S(1)}, bf16[64,896]{1,0:T(8,128)(2,1)S(1)}, bf16[64,896]{1,0:T(8,128)(2,1)S(1)}, f32[64,...) custom-call(s32[3]{0:T(128)S(1)} %pad_add_fusion.place, ...), custom_call_target="tpu_custom_call" | custom-call | flops 1761607680 | bytes 14680064 | tf_op jit(solution)/shard_map/down/pallas_call | solution.py:239
  103.0 1.8 %collective-permute-start.22 = (bf16[64,896]{1,0:T(8,128)(2,1)S(1)}, bf16[64,896]{1,0:T(8,128)(2,1)S(1)}, u32[]{:S(2)}, u32[]{:S(2)}) collective-permute-start(bf16[64,896]{1,0:T(8,128)(2,1)S(1)} %get-tuple-element.48), channel_id=1, source_target_pairs={{0,3},{1,2},{2,1},{3,0},{4,7},{5,6},{6,5},{7,4},{8,11},{9,10},{10,... | collective-permute-start | bytes 344072 | tf_op jit(solution)/shard_map/ppermute | solution.py:60
  106.5 10.6 %down.3 = (f32[64,896]{1,0:T(8,128)S(1)}, bf16[64,896]{1,0:T(8,128)(2,1)S(1)}, bf16[64,896]{1,0:T(8,128)(2,1)S(1)}, bf16[64,896]{1,0:T(8,128)(2,1)S(1)}, f32[64,...) custom-call(s32[3]{0:T(128)S(1)} %pad_add_fusion.place, ...), custom_call_target="tpu_custom_call" | custom-call | flops 1761607680 | bytes 14680064 | tf_op jit(solution)/shard_map/down/pallas_call | solution.py:239
  120.7 2.6 %collective-permute-done.27 = bf16[64,896]{1,0:T(8,128)(2,1)S(1)} collective-permute-done((bf16[64,896]{1,0:T(8,128)(2,1)S(1)}, bf16[64,896]{1,0:T(8,128)(2,1)S(1)}, u32[]{:S(2)}, u32[]{:S(2)}) %collective-permute-start.27) | collective-permute-done | bytes 114720 | tf_op jit(solution)/shard_map/ppermute | solution.py:60
  123.3 1.8 %collective-permute-start.19 = (bf16[64,896]{1,0:T(8,128)(2,1)S(1)}, bf16[64,896]{1,0:T(8,128)(2,1)S(1)}, u32[]{:S(2)}, u32[]{:S(2)}) collective-permute-start(bf16[64,896]{1,0:T(8,128)(2,1)S(1)} %get-tuple-element.44), channel_id=1, source_target_pairs={{0,3},{1,2},{2,1},{3,0},{4,7},{5,6},{6,5},{7,4},{8,11},{9,10},{10,... | collective-permute-start | bytes 344072 | tf_op jit(solution)/shard_map/ppermute | solution.py:60
  125.1 1.6 %collective-permute-start.24 = (bf16[64,896]{1,0:T(8,128)(2,1)S(1)}, bf16[64,896]{1,0:T(8,128)(2,1)S(1)}, u32[]{:S(2)}, u32[]{:S(2)}) collective-permute-start(bf16[64,896]{1,0:T(8,128)(2,1)S(1)} %get-tuple-element.50), channel_id=1, source_target_pairs={{0,1},{1,0},{2,3},{3,2},{4,5},{5,4},{6,7},{7,6},{8,9},{9,8},{10,11... | collective-permute-start | bytes 344072 | tf_op jit(solution)/shard_map/ppermute | solution.py:60
  126.7 2.4 %collective-permute-start.23 = (bf16[64,896]{1,0:T(8,128)(2,1)S(1)}, bf16[64,896]{1,0:T(8,128)(2,1)S(1)}, u32[]{:S(2)}, u32[]{:S(2)}) collective-permute-start(bf16[64,896]{1,0:T(8,128)(2,1)S(1)} %add_convert_fusion.3), channel_id=1, source_target_pairs={{0,4},{1,5},{2,6},{3,7},{4,0},{5,1},{6,2},{7,3},{8,12},{9,13},{10,... | collective-permute-start | bytes 344072 | tf_op jit(solution)/shard_map/ppermute | solution.py:60
  129.2 3.5 %collective-permute-start.25 = (bf16[64,896]{1,0:T(8,128)(2,1)S(1)}, bf16[64,896]{1,0:T(8,128)(2,1)S(1)}, u32[]{:S(2)}, u32[]{:S(2)}) collective-permute-start(bf16[64,896]{1,0:T(8,128)(2,1)S(1)} %get-tuple-element.51), channel_id=1, source_target_pairs={{0,2},{1,3},{2,0},{3,1},{4,6},{5,7},{6,4},{7,5},{8,10},{9,11},{10,... | collective-permute-start | bytes 344072 | tf_op jit(solution)/shard_map/ppermute | solution.py:60
  132.7 2.2 %collective-permute-start.30 = (bf16[64,896]{1,0:T(8,128)(2,1)S(1)}, bf16[64,896]{1,0:T(8,128)(2,1)S(1)}, u32[]{:S(2)}, u32[]{:S(2)}) collective-permute-start(bf16[64,896]{1,0:T(8,128)(2,1)S(1)} %add_convert_fusion.1), channel_id=1, source_target_pairs={{0,4},{1,5},{2,6},{3,7},{4,0},{5,1},{6,2},{7,3},{8,12},{9,13},{10,... | collective-permute-start | bytes 344072 | tf_op jit(solution)/shard_map/ppermute | solution.py:60
  136.2 3.5 %collective-permute-done.26 = bf16[64,896]{1,0:T(8,128)(2,1)S(1)} collective-permute-done((bf16[64,896]{1,0:T(8,128)(2,1)S(1)}, bf16[64,896]{1,0:T(8,128)(2,1)S(1)}, u32[]{:S(2)}, u32[]{:S(2)}) %collective-permute-start.26) | collective-permute-done | bytes 114720 | tf_op jit(solution)/shard_map/ppermute | solution.py:60
  (68 shorter events, 25.9 us)
Async XLA Ops:
  3.5 15.4 %collective-permute-start.3 = (bf16[64,1920]{1,0:T(8,128)(2,1)S(1)}, bf16[64,1920]{1,0:T(8,128)(2,1)S(1)}, u32[]{:S(2)}, u32[]{:S(2)}) collective-permute-start(bf16[64,1920]{1,0:T(8,128)(2,1)S(1)} %pad_maximum_fusion.refs_0_), channel_id=1, source_target_pairs={{0,4},{1,5},{2,6},{3,7},{4,0},{5,1},{6,2},{7,3},{8,12},{9,13},{10,... | collective-permute-start | bytes 737288 | tf_op jit(solution)/shard_map/ppermute | solution.py:60
  7.6 13.5 %collective-permute-start = (bf16[64,1920]{1,0:T(8,128)(2,1)S(1)}, bf16[64,1920]{1,0:T(8,128)(2,1)S(1)}, u32[]{:S(2)}, u32[]{:S(2)}) collective-permute-start(bf16[64,1920]{1,0:T(8,128)(2,1)S(1)} %pad_maximum_fusion.refs_0_), channel_id=1, source_target_pairs={{0,1},{1,0},{2,3},{3,2},{4,5},{5,4},{6,7},{7,6},{8,9},{9,8},{10,11... | collective-permute-start | bytes 737288 | tf_op jit(solution)/shard_map/ppermute | solution.py:60
  9.1 13.4 %collective-permute-start.1 = (bf16[64,1920]{1,0:T(8,128)(2,1)S(1)}, bf16[64,1920]{1,0:T(8,128)(2,1)S(1)}, u32[]{:S(2)}, u32[]{:S(2)}) collective-permute-start(bf16[64,1920]{1,0:T(8,128)(2,1)S(1)} %pad_maximum_fusion.refs_0_), channel_id=1, source_target_pairs={{0,2},{1,3},{2,0},{3,1},{4,6},{5,7},{6,4},{7,5},{8,10},{9,11},{10,... | collective-permute-start | bytes 737288 | tf_op jit(solution)/shard_map/ppermute | solution.py:60
  10.7 16.8 %collective-permute-start.2 = (bf16[64,1920]{1,0:T(8,128)(2,1)S(1)}, bf16[64,1920]{1,0:T(8,128)(2,1)S(1)}, u32[]{:S(2)}, u32[]{:S(2)}) collective-permute-start(bf16[64,1920]{1,0:T(8,128)(2,1)S(1)} %pad_maximum_fusion.refs_0_), channel_id=1, source_target_pairs={{0,3},{1,2},{2,1},{3,0},{4,7},{5,6},{6,5},{7,4},{8,11},{9,10},{10,... | collective-permute-start | bytes 737288 | tf_op jit(solution)/shard_map/ppermute | solution.py:60
  18.9 12.3 %collective-permute-start.4 = (bf16[64,1920]{1,0:T(8,128)(2,1)S(1)}, bf16[64,1920]{1,0:T(8,128)(2,1)S(1)}, u32[]{:S(2)}, u32[]{:S(2)}) collective-permute-start(bf16[64,1920]{1,0:T(8,128)(2,1)S(1)} %collective-permute-done.3.refs_4_), channel_id=1, source_target_pairs={{0,1},{1,0},{2,3},{3,2},{4,5},{5,4},{6,7},{7,6},{8,9},{9,8},{10,11... | collective-permute-start | bytes 737288 | tf_op jit(solution)/shard_map/ppermute | solution.py:60
  20.5 12.2 %collective-permute-start.5 = (bf16[64,1920]{1,0:T(8,128)(2,1)S(1)}, bf16[64,1920]{1,0:T(8,128)(2,1)S(1)}, u32[]{:S(2)}, u32[]{:S(2)}) collective-permute-start(bf16[64,1920]{1,0:T(8,128)(2,1)S(1)} %collective-permute-done.3.refs_4_), channel_id=1, source_target_pairs={{0,2},{1,3},{2,0},{3,1},{4,6},{5,7},{6,4},{7,5},{8,10},{9,11},{10,... | collective-permute-start | bytes 737288 | tf_op jit(solution)/shard_map/ppermute | solution.py:60
  21.1 15.1 %collective-permute-start.6 = (bf16[64,1920]{1,0:T(8,128)(2,1)S(1)}, bf16[64,1920]{1,0:T(8,128)(2,1)S(1)}, u32[]{:S(2)}, u32[]{:S(2)}) collective-permute-start(bf16[64,1920]{1,0:T(8,128)(2,1)S(1)} %collective-permute-done.3.refs_4_), channel_id=1, source_target_pairs={{0,3},{1,2},{2,1},{3,0},{4,7},{5,6},{6,5},{7,4},{8,11},{9,10},{10,... | collective-permute-start | bytes 737288 | tf_op jit(solution)/shard_map/ppermute | solution.py:60
  50.3 15.0 %collective-permute-start.12 = (bf16[2,80,2048]{2,1,0:T(8,128)(2,1)S(1)}, bf16[2,80,2048]{2,1,0:T(8,128)(2,1)S(1)}, u32[]{:S(2)}, u32[]{:S(2)}) collective-permute-start(bf16[2,80,2048]{2,1,0:T(8,128)(2,1)S(1)} %get-tuple-element.36), channel_id=1, source_target_pairs={{0,8},{8,0},{16,24},{24,16},{1,9},{9,1},{17,25},{25,17},{2,10},{10... | collective-permute-start | bytes 1966088 | tf_op jit(solution)/shard_map/ppermute | solution.py:60
  65.5 10.6 %collective-permute-start.13 = (bf16[80,2048]{1,0:T(8,128)(2,1)S(1)}, bf16[80,2048]{1,0:T(8,128)(2,1)S(1)}, u32[]{:S(2)}, u32[]{:S(2)}) collective-permute-start(bf16[80,2048]{1,0:T(8,128)(2,1)S(1)} %fusion.1), channel_id=1, source_target_pairs={{0,16},{8,24},{16,0},{24,8},{1,17},{9,25},{17,1},{25,9},{2,18},{10... | collective-permute-start | bytes 983048 | tf_op jit(solution)/shard_map/ppermute | solution.py:60
  67.3 15.8 %collective-permute-start.8 = (bf16[80,2048]{1,0:T(8,128)(2,1)S(1)}, bf16[80,2048]{1,0:T(8,128)(2,1)S(1)}, u32[]{:S(2)}, u32[]{:S(2)}) collective-permute-start(bf16[80,2048]{1,0:T(8,128)(2,1)S(1)} %fusion.5), channel_id=1, source_target_pairs={{0,16},{8,24},{16,0},{24,8},{1,17},{9,25},{17,1},{25,9},{2,18},{10... | collective-permute-start | bytes 983048 | tf_op jit(solution)/shard_map/ppermute | solution.py:60
  76.4 10.3 %collective-permute-start.15 = (bf16[80,1024]{1,0:T(8,128)(2,1)S(1)}, bf16[80,1024]{1,0:T(8,128)(2,1)S(1)}, u32[]{:S(2)}, u32[]{:S(2)}) collective-permute-start(bf16[80,1024]{1,0:T(8,128)(2,1)S(1)} %fusion.9.refs_4_), channel_id=1, source_target_pairs={{0,16},{8,24},{16,0},{24,8},{1,17},{9,25},{17,1},{25,9},{2,18},{10... | collective-permute-start | bytes 491528 | tf_op jit(solution)/shard_map/ppermute | solution.py:60
  101.2 15.9 %collective-permute-start.20 = (bf16[64,896]{1,0:T(8,128)(2,1)S(1)}, bf16[64,896]{1,0:T(8,128)(2,1)S(1)}, u32[]{:S(2)}, u32[]{:S(2)}) collective-permute-start(bf16[64,896]{1,0:T(8,128)(2,1)S(1)} %get-tuple-element.46), channel_id=1, source_target_pairs={{0,1},{1,0},{2,3},{3,2},{4,5},{5,4},{6,7},{7,6},{8,9},{9,8},{10,11... | collective-permute-start | bytes 344072 | tf_op jit(solution)/shard_map/ppermute | solution.py:60
  102.7 15.9 %collective-permute-start.21 = (bf16[64,896]{1,0:T(8,128)(2,1)S(1)}, bf16[64,896]{1,0:T(8,128)(2,1)S(1)}, u32[]{:S(2)}, u32[]{:S(2)}) collective-permute-start(bf16[64,896]{1,0:T(8,128)(2,1)S(1)} %get-tuple-element.47), channel_id=1, source_target_pairs={{0,2},{1,3},{2,0},{3,1},{4,6},{5,7},{6,4},{7,5},{8,10},{9,11},{10,... | collective-permute-start | bytes 344072 | tf_op jit(solution)/shard_map/ppermute | solution.py:60
  103.0 16.5 %collective-permute-start.22 = (bf16[64,896]{1,0:T(8,128)(2,1)S(1)}, bf16[64,896]{1,0:T(8,128)(2,1)S(1)}, u32[]{:S(2)}, u32[]{:S(2)}) collective-permute-start(bf16[64,896]{1,0:T(8,128)(2,1)S(1)} %get-tuple-element.48), channel_id=1, source_target_pairs={{0,3},{1,2},{2,1},{3,0},{4,7},{5,6},{6,5},{7,4},{8,11},{9,10},{10,... | collective-permute-start | bytes 344072 | tf_op jit(solution)/shard_map/ppermute | solution.py:60
  104.8 24.4 %collective-permute-start.17 = (bf16[64,896]{1,0:T(8,128)(2,1)S(1)}, bf16[64,896]{1,0:T(8,128)(2,1)S(1)}, u32[]{:S(2)}, u32[]{:S(2)}) collective-permute-start(bf16[64,896]{1,0:T(8,128)(2,1)S(1)} %get-tuple-element.42), channel_id=1, source_target_pairs={{0,1},{1,0},{2,3},{3,2},{4,5},{5,4},{6,7},{7,6},{8,9},{9,8},{10,11... | collective-permute-start | bytes 344072 | tf_op jit(solution)/shard_map/ppermute | solution.py:60
  106.2 26.5 %collective-permute-start.18 = (bf16[64,896]{1,0:T(8,128)(2,1)S(1)}, bf16[64,896]{1,0:T(8,128)(2,1)S(1)}, u32[]{:S(2)}, u32[]{:S(2)}) collective-permute-start(bf16[64,896]{1,0:T(8,128)(2,1)S(1)} %get-tuple-element.43), channel_id=1, source_target_pairs={{0,2},{1,3},{2,0},{3,1},{4,6},{5,7},{6,4},{7,5},{8,10},{9,11},{10,... | collective-permute-start | bytes 344072 | tf_op jit(solution)/shard_map/ppermute | solution.py:60
  118.7 6.5 %collective-permute-start.28 = (bf16[64,896]{1,0:T(8,128)(2,1)S(1)}, bf16[64,896]{1,0:T(8,128)(2,1)S(1)}, u32[]{:S(2)}, u32[]{:S(2)}) collective-permute-start(bf16[64,896]{1,0:T(8,128)(2,1)S(1)} %get-tuple-element.55), channel_id=1, source_target_pairs={{0,2},{1,3},{2,0},{3,1},{4,6},{5,7},{6,4},{7,5},{8,10},{9,11},{10,... | collective-permute-start | bytes 344072 | tf_op jit(solution)/shard_map/ppermute | solution.py:60
  119.5 7.2 %collective-permute-start.29 = (bf16[64,896]{1,0:T(8,128)(2,1)S(1)}, bf16[64,896]{1,0:T(8,128)(2,1)S(1)}, u32[]{:S(2)}, u32[]{:S(2)}) collective-permute-start(bf16[64,896]{1,0:T(8,128)(2,1)S(1)} %get-tuple-element.56), channel_id=1, source_target_pairs={{0,3},{1,2},{2,1},{3,0},{4,7},{5,6},{6,5},{7,4},{8,11},{9,10},{10,... | collective-permute-start | bytes 344072 | tf_op jit(solution)/shard_map/ppermute | solution.py:60
  123.3 9.4 %collective-permute-start.19 = (bf16[64,896]{1,0:T(8,128)(2,1)S(1)}, bf16[64,896]{1,0:T(8,128)(2,1)S(1)}, u32[]{:S(2)}, u32[]{:S(2)}) collective-permute-start(bf16[64,896]{1,0:T(8,128)(2,1)S(1)} %get-tuple-element.44), channel_id=1, source_target_pairs={{0,3},{1,2},{2,1},{3,0},{4,7},{5,6},{6,5},{7,4},{8,11},{9,10},{10,... | collective-permute-start | bytes 344072 | tf_op jit(solution)/shard_map/ppermute | solution.py:60
  125.1 10.5 %collective-permute-start.24 = (bf16[64,896]{1,0:T(8,128)(2,1)S(1)}, bf16[64,896]{1,0:T(8,128)(2,1)S(1)}, u32[]{:S(2)}, u32[]{:S(2)}) collective-permute-start(bf16[64,896]{1,0:T(8,128)(2,1)S(1)} %get-tuple-element.50), channel_id=1, source_target_pairs={{0,1},{1,0},{2,3},{3,2},{4,5},{5,4},{6,7},{7,6},{8,9},{9,8},{10,11... | collective-permute-start | bytes 344072 | tf_op jit(solution)/shard_map/ppermute | solution.py:60
  126.7 8.8 %collective-permute-start.23 = (bf16[64,896]{1,0:T(8,128)(2,1)S(1)}, bf16[64,896]{1,0:T(8,128)(2,1)S(1)}, u32[]{:S(2)}, u32[]{:S(2)}) collective-permute-start(bf16[64,896]{1,0:T(8,128)(2,1)S(1)} %add_convert_fusion.3), channel_id=1, source_target_pairs={{0,4},{1,5},{2,6},{3,7},{4,0},{5,1},{6,2},{7,3},{8,12},{9,13},{10,... | collective-permute-start | bytes 344072 | tf_op jit(solution)/shard_map/ppermute | solution.py:60
  129.2 6.9 %collective-permute-start.25 = (bf16[64,896]{1,0:T(8,128)(2,1)S(1)}, bf16[64,896]{1,0:T(8,128)(2,1)S(1)}, u32[]{:S(2)}, u32[]{:S(2)}) collective-permute-start(bf16[64,896]{1,0:T(8,128)(2,1)S(1)} %get-tuple-element.51), channel_id=1, source_target_pairs={{0,2},{1,3},{2,0},{3,1},{4,6},{5,7},{6,4},{7,5},{8,10},{9,11},{10,... | collective-permute-start | bytes 344072 | tf_op jit(solution)/shard_map/ppermute | solution.py:60
  132.7 6.9 %collective-permute-start.26 = (bf16[64,896]{1,0:T(8,128)(2,1)S(1)}, bf16[64,896]{1,0:T(8,128)(2,1)S(1)}, u32[]{:S(2)}, u32[]{:S(2)}) collective-permute-start(bf16[64,896]{1,0:T(8,128)(2,1)S(1)} %get-tuple-element.52), channel_id=1, source_target_pairs={{0,3},{1,2},{2,1},{3,0},{4,7},{5,6},{6,5},{7,4},{8,11},{9,10},{10,... | collective-permute-start | bytes 344072 | tf_op jit(solution)/shard_map/ppermute | solution.py:60
  132.7 7.0 %collective-permute-start.30 = (bf16[64,896]{1,0:T(8,128)(2,1)S(1)}, bf16[64,896]{1,0:T(8,128)(2,1)S(1)}, u32[]{:S(2)}, u32[]{:S(2)}) collective-permute-start(bf16[64,896]{1,0:T(8,128)(2,1)S(1)} %add_convert_fusion.1), channel_id=1, source_target_pairs={{0,4},{1,5},{2,6},{3,7},{4,0},{5,1},{6,2},{7,3},{8,12},{9,13},{10,... | collective-permute-start | bytes 344072 | tf_op jit(solution)/shard_map/ppermute | solution.py:60
  (7 other events, 27.1 us)

commit v2 on v0

--- a/solution.py
+++ b/solution.py
@@ -1,12 +1,20 @@
+import functools
+import math
+
 import jax
 import jax.numpy as jnp
 from jax import lax
+from jax.experimental import pallas as pl
+from jax.experimental.pallas import tpu as pltpu
 from jax.sharding import PartitionSpec as P
 
 CAP = 10
-
-
-def shards(tokens, expert_ids, combine_weights, w_gate, w_up, w_down):
+NEAR = 4
+LANES = 128
+COLUMN_PARTS = 2
+
+
+def plain_shards(tokens, expert_ids, combine_weights, w_gate, w_up, w_down):
     tok_rows, width_part = tokens.shape
     top_count = expert_ids.shape[1]
     local_experts = w_gate.shape[0]
@@ -48,6 +56,457 @@
     return combined.astype(jnp.bfloat16)
 
 
+def swap(value, axis, distance):
+    size = lax.axis_size(axis)
+    return lax.ppermute(value, axis, [(i, i ^ distance) for i in range(size)])
+
+
+def resident(value):
+    return pltpu.with_memory_space_constraint(value, pltpu.VMEM)
+
+
+def distant(value):
+    return pltpu.with_memory_space_constraint(value, pltpu.HBM)
+
+
+def in_vmem(count):
+    return [pl.BlockSpec(memory_space=pltpu.VMEM)] * count
+
+
+def anywhere(count):
+    return [pl.BlockSpec(memory_space=pl.ANY)] * count
+
+
+def in_hbm(count):
+    return [pl.BlockSpec(memory_space=pltpu.HBM)] * count
+
+
+def pack_kernel(tokens, ids, weights, packed):
+    depth = tokens.shape[1]
+    weight = weights[...]
+    high = weight.astype(jnp.bfloat16).astype(jnp.float32)
+    middle = (weight - high).astype(jnp.bfloat16).astype(jnp.float32)
+    low = weight - high - middle
+    rows = jnp.concatenate((ids[...].astype(jnp.float32), high, middle, low), axis=0)
+    count = rows.shape[0]
+    row = lax.broadcasted_iota(jnp.int32, (count, LANES), 0)
+    col = lax.broadcasted_iota(jnp.int32, (count, LANES), 1)
+    eye = jnp.where(row == col, 1.0, 0.0).astype(jnp.bfloat16)
+    packed[:, :depth] = tokens[...]
+    packed[:, depth:] = lax.dot_general(
+        rows.astype(jnp.bfloat16),
+        eye,
+        (((0,), (0,)), ((), ())),
+        preferred_element_type=jnp.float32,
+    ).astype(jnp.bfloat16)
+
+
+def pack(tokens, expert_ids, combine_weights):
+    rows, depth = tokens.shape
+    return pl.pallas_call(
+        pack_kernel,
+        out_shape=jax.ShapeDtypeStruct((rows, depth + LANES), jnp.bfloat16),
+        in_specs=in_vmem(3),
+        out_specs=pl.BlockSpec(memory_space=pltpu.VMEM),
+        name="pack",
+    )(tokens, expert_ids.T, combine_weights.T)
+
+
+def visiting(group):
+    return list(range(1, group, 2)) + list(range(0, group, 2))[::-1]
+
+
+def load_kernel(starts, orders, place, *refs):
+    count = len(starts)
+    sources, targets = refs[:count], refs[count + 1 : 2 * count + 1]
+    token, done = refs[-2:]
+    copies = []
+    for k in range(max(map(len, orders))):
+        for i in range(count):
+            if k < len(orders[i]):
+                copies.append(
+                    pltpu.make_async_copy(
+                        sources[i].at[starts[i] + (orders[i][k] ^ place[0])],
+                        targets[i].at[k],
+                        done.at[i, k],
+                    )
+                )
+                copies[-1].start()
+    token[...] = jnp.zeros_like(token)
+    for copy in copies:
+        copy.wait()
+
+
+def load(weights, starts, orders, place, after):
+    count = len(weights)
+    shapes = [
+        pltpu.VMEM((len(order),) + w.shape[1:], w.dtype) for w, order in zip(weights, orders)
+    ]
+    size = sum(2 * math.prod(shape.shape) for shape in shapes)
+    *loaded, token = pl.pallas_call(
+        functools.partial(load_kernel, starts, orders),
+        out_shape=shapes + [jax.ShapeDtypeStruct((8, LANES), jnp.float32)],
+        in_specs=[pl.BlockSpec(memory_space=pltpu.SMEM)] + in_hbm(count) + anywhere(1),
+        out_specs=in_vmem(count + 1),
+        scratch_shapes=[pltpu.SemaphoreType.DMA((count, max(map(len, orders))))],
+        compiler_params=pltpu.CompilerParams(vmem_limit_bytes=2 * 2**20),
+        cost_estimate=pl.CostEstimate(flops=0, bytes_accessed=size, transcendentals=0),
+        name="load",
+    )(place, *map(distant, weights), after)
+    return loaded, token
+
+
+def merge_kernel(half, *refs):
+    received, keeps, parts, base = refs[0], refs[1 : 1 + half], refs[1 + half : -1], refs[-1]
+    base[...] = keeps[0][...] + received[0].astype(jnp.float32)
+    for j, part in enumerate(parts):
+        part[...] = (keeps[j + 1][...] + received[j + 1].astype(jnp.float32)).astype(part.dtype)
+
+
+def merge(received, keeps):
+    half = len(keeps)
+    shape = keeps[0].shape
+    *parts, base = pl.pallas_call(
+        functools.partial(merge_kernel, half),
+        out_shape=[jax.ShapeDtypeStruct(shape, jnp.bfloat16)] * (half - 1)
+        + [jax.ShapeDtypeStruct(shape, jnp.float32)],
+        in_specs=in_vmem(1 + half),
+        out_specs=in_vmem(half),
+        compiler_params=pltpu.CompilerParams(vmem_limit_bytes=4 * 2**20),
+        name="merge",
+    )(received, *keeps)
+    return parts, base
+
+
+def route(blocks, held, picked, scale, slots, place, top, group, rows):
+    depth = held.shape[1] - LANES
+    tok_rows = blocks[0].shape[0]
+    total = held.shape[0]
+    member, first = place[0], place[1]
+    for k, block in enumerate(blocks):
+        held[k * tok_rows : (k + 1) * tok_rows, :] = block[...]
+    meta = held[:, depth:].astype(jnp.float32)
+    lane = lax.broadcasted_iota(jnp.int32, (1, LANES), 1)
+    named = jnp.where(lane < group, first + (lane ^ member), -1).astype(jnp.float32)
+    match = jnp.zeros((total, LANES), jnp.float32)
+    for k in range(top):
+        match = match + jnp.where(meta[:, k : k + 1] == named, 1.0, 0.0)
+    row = lax.broadcasted_iota(jnp.int32, (total, total), 0)
+    col = lax.broadcasted_iota(jnp.int32, (total, total), 1)
+    earlier = jnp.where(row > col, 1.0, 0.0).astype(jnp.bfloat16)
+    position = jnp.dot(earlier, match.astype(jnp.bfloat16), preferred_element_type=jnp.float32)
+    position = jnp.where(match > 0.0, position, -1.0).astype(jnp.bfloat16)
+    width = group * rows
+    wide_row = lax.broadcasted_iota(jnp.int32, (LANES, width), 0)
+    wide_col = lax.broadcasted_iota(jnp.int32, (LANES, width), 1)
+    inside = (wide_col >= wide_row * rows) & (wide_col < (wide_row + 1) * rows)
+    spread = jnp.where(inside, 1.0, 0.0).astype(jnp.bfloat16)
+    wide = jnp.dot(position, spread, preferred_element_type=jnp.float32)
+    number = lax.broadcasted_iota(jnp.int32, (1, width), 1)
+    slot = number
+    for j in range(1, group):
+        slot = slot - jnp.where(number >= j * rows, rows, 0)
+    one_hot = jnp.where(wide == slot.astype(jnp.float32), 1.0, 0.0).astype(jnp.bfloat16)
+    slots[...] = one_hot
+    picked[...] = lax.dot_general(
+        one_hot, held[...], (((0,), (0,)), ((), ())), preferred_element_type=jnp.float32
+    ).astype(jnp.bfloat16)
+    own = picked[:rows, depth:].astype(jnp.float32)
+    weight = (own[:, top : 2 * top] + own[:, 2 * top : 3 * top]) + own[:, 3 * top : 4 * top]
+    mine = (first + member).astype(jnp.float32)
+    weight = jnp.sum(jnp.where(own[:, :top] == mine, weight, 0.0), axis=1, keepdims=True)
+    scale[...] = jnp.broadcast_to(weight, scale.shape)
+
+
+def project_kernel(top, group, rows, owners, ready, place, *refs):
+    half = group // 2
+    blocks = refs[:owners]
+    near = refs[owners : owners + 2] if ready else ()
+    refs = refs[owners + len(near) :]
+    far, send, keeps = refs[:2], refs[3], refs[4 : 4 + half]
+    scale, slots, held, picked = refs[4 + half : 8 + half]
+    order = visiting(group)
+    copies = {}
+    if ready < group:
+        *buffers, done = refs[8 + half :]
+        for k in range(ready, group):
+            for i in range(2):
+                copies[i, k] = pltpu.make_async_copy(
+                    far[i].at[place[2] + (order[k] ^ place[0])],
+                    buffers[i].at[k - ready],
+                    done.at[i, k - ready],
+                )
+                copies[i, k].start()
+    route(blocks, held, picked, scale, slots, place, top, group, rows)
+    depth, ff = far[0].shape[1:]
+    for k, number in enumerate(order):
+        for i in range(2):
+            if k >= ready:
+                copies[i, k].wait()
+            part = jnp.dot(
+                picked[number * rows : (number + 1) * rows, :depth],
+                near[i][k] if k < ready else buffers[i][k - ready],
+                preferred_element_type=jnp.float32,
+            )
+            if number % 2:
+                send[number // 2, :, i * ff : (i + 1) * ff] = part.astype(send.dtype)
+            else:
+                keeps[number // 2][:, i * ff : (i + 1) * ff] = part
+
+
+def project(blocks, place, near, weights, after, top, group, rows):
+    ready = near[0].shape[0] if near else 0
+    depth, ff = weights[0].shape[1:]
+    tok_rows, wide = blocks[0].shape
+    owners = len(blocks)
+    total = tok_rows * owners
+    half = group // 2
+    out_shape = (
+        [jax.ShapeDtypeStruct((half, rows, 2 * ff), jnp.bfloat16)]
+        + [jax.ShapeDtypeStruct((rows, 2 * ff), jnp.float32)] * half
+        + [
+            jax.ShapeDtypeStruct((rows, LANES), jnp.float32),
+            jax.ShapeDtypeStruct((total, group * rows), jnp.bfloat16),
+        ]
+    )
+    scratch = [
+        pltpu.VMEM((total, wide), jnp.bfloat16),
+        pltpu.VMEM((group * rows, wide), jnp.bfloat16),
+    ]
+    streamed = group - ready
+    if streamed:
+        scratch += [pltpu.VMEM((streamed, depth, ff), jnp.bfloat16)] * 2
+        scratch += [pltpu.SemaphoreType.DMA((2, streamed))]
+    outs = pl.pallas_call(
+        functools.partial(project_kernel, top, group, rows, owners, ready),
+        out_shape=out_shape,
+        in_specs=[pl.BlockSpec(memory_space=pltpu.SMEM)]
+        + in_vmem(owners + len(near))
+        + in_hbm(2)
+        + anywhere(1),
+        out_specs=in_vmem(len(out_shape)),
+        scratch_shapes=scratch,
+        compiler_params=pltpu.CompilerParams(
+            vmem_limit_bytes=8 * 2**20 + streamed * depth * ff * 4
+        ),
+        cost_estimate=pl.CostEstimate(
+            flops=4 * group * rows * depth * ff,
+            bytes_accessed=4 * group * depth * ff,
+            transcendentals=0,
+        ),
+        name="project",
+    )(place, *blocks, *map(resident, near), *map(distant, weights), after)
+    return outs[0], outs[1 : 1 + half], outs[-2], outs[-1]
+
+
+def down_kernel(*refs):
+    *hidden, weights, slots, _, total, result = refs
+    rows = hidden[0].shape[0]
+    for k, part in enumerate(hidden):
+        result[k * rows : (k + 1) * rows, :] = jnp.dot(
+            part[...], weights[k], preferred_element_type=jnp.float32
+        ).astype(jnp.bfloat16)
+    total[...] = jnp.dot(slots[...], result[...], preferred_element_type=jnp.float32)
+
+
+def down(hidden, weights, slots, after):
+    rows, ff = hidden[0].shape
+    count, columns = len(hidden), weights.shape[2]
+    total = slots.shape[0]
+    return pl.pallas_call(
+        down_kernel,
+        out_shape=jax.ShapeDtypeStruct((total, columns), jnp.float32),
+        in_specs=in_vmem(count + 2) + anywhere(1),
+        out_specs=pl.BlockSpec(memory_space=pltpu.VMEM),
+        scratch_shapes=[pltpu.VMEM((count * rows, columns), jnp.bfloat16)],
+        compiler_params=pltpu.CompilerParams(vmem_limit_bytes=8 * 2**20),
+        cost_estimate=pl.CostEstimate(
+            flops=2 * count * rows * columns * (ff + total),
+            bytes_accessed=2 * count * ff * columns,
+            transcendentals=0,
+        ),
+        name="down",
+    )(*hidden, resident(weights), slots, after)
+
+
+def finish_kernel(count, chunks, start, columns, *refs):
+    hidden, weights, slots = refs[:count], refs[count], refs[count + 1]
+    others = refs[count + 2 : count + 1 + chunks]
+    outs, result = refs[count + 1 + chunks : -1], refs[-1]
+    rows = hidden[0].shape[0]
+    for k, part in enumerate(hidden):
+        result[k * rows : (k + 1) * rows, :] = jnp.dot(
+            part[...],
+            weights[k, :, start : start + columns],
+            preferred_element_type=jnp.float32,
+        ).astype(jnp.bfloat16)
+    total = jnp.dot(slots[...], result[...], preferred_element_type=jnp.float32)
+    for other in others:
+        total = total + other[:, start : start + columns]
+    tok_rows = outs[0].shape[0]
+    for k, out in enumerate(outs):
+        out[...] = total[k * tok_rows : (k + 1) * tok_rows, :].astype(out.dtype)
+
+
+def finish(hidden, weights, slots, others, start, columns, owners):
+    rows, ff = hidden[0].shape
+    count = len(hidden)
+    total = slots.shape[0]
+    out_shape = [
+        jax.ShapeDtypeStruct(
+            (total // owners, columns), jnp.float32 if k % NEAR == 0 else jnp.bfloat16
+        )
+        for k in range(owners)
+    ]
+    return pl.pallas_call(
+        functools.partial(finish_kernel, count, len(others) + 1, start, columns),
+        out_shape=out_shape,
+        in_specs=in_vmem(count + 2 + len(others)),
+        out_specs=in_vmem(owners),
+        scratch_shapes=[pltpu.VMEM((count * rows, columns), jnp.bfloat16)],
+        compiler_params=pltpu.CompilerParams(vmem_limit_bytes=8 * 2**20),
+        cost_estimate=pl.CostEstimate(
+            flops=2 * count * rows * columns * (ff + total),
+            bytes_accessed=2 * count * ff * columns,
+            transcendentals=0,
+        ),
+        name="finish",
+    )(*hidden, resident(weights), slots, *others)
+
+
+def activate_kernel(*refs):
+    *sums, scale, out = refs
+    both = sums[0][...]
+    for part in sums[1:]:
+        both = both + part[...].astype(jnp.float32)
+    ff = out.shape[1]
+    out[...] = (jax.nn.silu(both[:, :ff]) * both[:, ff:] * scale[:, :1]).astype(out.dtype)
+
+
+def activate(base, arrived, scale):
+    rows, wide = base.shape
+    return pl.pallas_call(
+        activate_kernel,
+        out_shape=jax.ShapeDtypeStruct((rows, wide // 2), jnp.bfloat16),
+        in_specs=in_vmem(2 + len(arrived)),
+        out_specs=pl.BlockSpec(memory_space=pltpu.VMEM),
+        compiler_params=pltpu.CompilerParams(vmem_limit_bytes=4 * 2**20),
+        name="activate",
+    )(base, *arrived, scale)
+
+
+def spread(own, group):
+    gathered = {0: own, 1: swap(own, "dp", 1)}
+    for j in range(2, group, 2):
+        gathered[j] = swap(own, "dp", j)
+    return gathered
+
+
+def complete(gathered, group):
+    for j in range(2, group, 2):
+        gathered[j + 1] = swap(gathered[j], "dp", 1)
+    return [gathered[k] for k in range(group)]
+
+
+def shards(tokens, expert_ids, combine_weights, w_gate, w_up, w_down):
+    tok_rows, depth = tokens.shape
+    top = expert_ids.shape[1]
+    local_experts = w_gate.shape[0]
+    ff = w_gate.shape[2]
+    owners = lax.axis_size("expert")
+    group = lax.axis_size("dp")
+    rows = owners * CAP
+    chunks = local_experts // group
+    member = lax.axis_index("dp")
+    first = lax.axis_index("expert") * local_experts
+    places = [
+        jnp.stack([member, first + c * group, jnp.int32(c * group)]) for c in range(chunks)
+    ]
+
+    order = visiting(group)
+    own = pack(tokens, expert_ids, combine_weights)
+    far_blocks = {far: swap(own, "expert", far) for far in range(NEAR, owners, NEAR)}
+    near_blocks = {near: swap(own, "expert", near) for near in range(1, NEAR)}
+    (gate_ready,), token = load((w_gate,), (0,), (order,), places[0], own)
+    far_blocks, token = lax.optimization_barrier((far_blocks, token))
+    blocks = {0: own} | near_blocks | far_blocks
+    for far in far_blocks:
+        for near in range(1, NEAR):
+            blocks[far + near] = swap(blocks[far], "expert", near)
+    ordered = [blocks[k] for k in range(owners)]
+    (up_ready,), _ = load((w_up,), (0,), (order,), places[0], token)
+
+    hidden, slots = [], []
+    after = token
+    for c in range(chunks):
+        near = (gate_ready, up_ready) if c == 0 else ()
+        send, keeps, scale, one_hot = project(
+            ordered, places[c], near, (w_gate, w_up), after, top, group, rows
+        )
+        slots.append(one_hot)
+        if c > 0:
+            send, arrived = lax.optimization_barrier((send, arrived))
+            hidden.append(spread(activate(base, arrived, old_scale), group))
+        parts, base = merge(swap(send, "dp", 1), keeps)
+        old_scale = scale
+        arrived = [swap(part, "dp", 2 * j) for j, part in enumerate(parts, 1)]
+        after = parts[0] if parts else base
+    starts = tuple(range(0, local_experts, group))
+    members = (list(range(group)),) * chunks
+    down_weights, token = load((w_down,) * chunks, starts, members, places[0], after)
+    arrived, hidden, token = lax.optimization_barrier((arrived, hidden, token))
+    last = spread(activate(base, arrived, old_scale), group)
+    hidden = [complete(gathered, group) for gathered in hidden]
+    others = [down(hidden[c], down_weights[c], slots[c], token) for c in range(chunks - 1)]
+    if others:
+        last, others = lax.optimization_barrier((last, others))
+    hidden.append(complete(last, group))
+    columns = depth // COLUMN_PARTS
+    done = []
+    for start in range(0, depth, columns):
+        partial = finish(
+            hidden[-1], down_weights[-1], slots[-1], others, start, columns, owners
+        )
+        total = partial[0]
+        sums = {}
+        for far in range(NEAR, owners, NEAR):
+            sums[far] = partial[far]
+            for near in range(1, NEAR):
+                sums[far] = sums[far] + swap(partial[far + near], "expert", near).astype(
+                    jnp.float32
+                )
+        for near in range(1, NEAR):
+            total = total + swap(partial[near], "expert", near).astype(jnp.float32)
+        for far in range(NEAR, owners, NEAR):
+            total = total + swap(sums[far].astype(jnp.bfloat16), "expert", far).astype(
+                jnp.float32
+            )
+        done.append(total.astype(jnp.bfloat16))
+    return jnp.concatenate(done, axis=1)
+
+
+def fits(owners, group, tokens, expert_ids, w_gate):
+    powers = all(k & (k - 1) == 0 for k in (owners, group))
+    return (
+        powers
+        and owners >= NEAR
+        and group >= 2
+        and w_gate.shape[0] % group == 0
+        and tokens.shape[0] % 16 == 0
+        and (owners * CAP) % 16 == 0
+        and owners * CAP < 256
+        and owners * w_gate.shape[0] <= 256
+        and 4 * expert_ids.shape[1] <= LANES
+        and tokens.shape[1] % (COLUMN_PARTS * LANES) == 0
+    )
+
+
+def layer(tokens, expert_ids, combine_weights, w_gate, w_up, w_down):
+    owners, group = lax.axis_size("expert"), lax.axis_size("dp")
+    chosen = shards if fits(owners, group, tokens, expert_ids, w_gate) else plain_shards
+    return chosen(tokens, expert_ids, combine_weights, w_gate, w_up, w_down)
+
+
 def solution(mesh):
     placed = (
         P("expert", "dp"),
@@ -58,5 +517,5 @@
         P("expert", None, "dp"),
     )
     return jax.shard_map(
-        shards, mesh=mesh, in_specs=placed, out_specs=P("expert", "dp"), check_vma=False
-    )
+        layer, mesh=mesh, in_specs=placed, out_specs=P("expert", "dp"), check_vma=False
+    )

time: 271 us -> 116 us (0.43)
  waiting for transfers between devices: 126 us -> 26.8 us
  blocking collectives: 59.6 us -> 0 us
  Pallas kernels: 0 us -> 53 us
  matrix products: 41.6 us -> 0 us
  starting transfers between devices: 5.91 us -> 33 us
  local copies, waits for them, and re-layouts: 15.6 us -> 1.74 us
  between operations: 13.2 us -> 0.18 us
  other arithmetic: 8.67 us -> 1.11 us
    all_to_all x1 -> x0, blocking collectives: 59.6 us -> none  [shards(): lax.all_to_all(outgoing, 'expert', split_axis=0, concat_axis=0, tiled=True)]
    reduce_scatter x2 -> x0, waiting for transfers between devices: 55 us -> none  [the longest x1 37.4 us: shards(): lax.psum_scatter(up_part, 'dp', scatter_dimension=0, tiled=True)]
    pallas_call x0 -> x13, Pallas kernels: none -> 53 us  [the longest x3 22.3 us: load(): pl.pallas_call(functools.partial(load_kernel, starts, orders), out_shape=...]
    all_to_all x1 -> x0, waiting for transfers between devices: 52.6 us -> none  [shards(): lax.all_to_all(outputs.reshape(owners * local_experts * CAP, width_part),...]
    dot_general x4 -> x0, matrix products: 41.6 us -> none  [the longest x1 16.5 us: shards(): jnp.einsum('hecf,efd->hecd', hidden, w_down, preferred_element_type=jnp.f...]
    ppermute x0 -> x31, starting transfers between devices: none -> 33 us  [swap(): return lax.ppermute(value, axis, [(i, i ^ distance) for i in range(size)])]
    ppermute x0 -> x31, waiting for transfers between devices: none -> 26.8 us  [swap(): return lax.ppermute(value, axis, [(i, i ^ distance) for i in range(size)])]
    all_gather x1 -> x0, waiting for transfers between devices: 18.4 us -> none  [shards(): hidden = lax.all_gather(shares, 'dp', axis=0, tiled=True)]
  transfers between devices with their start and end apart: 4 -> 31, of which waited for: 4 -> 15; matrix products, arithmetic and copies ran while one was open for 6% -> 0% of each run, Pallas kernels for 0% -> 35%
where the time goes in v2:
time: 116 us
  Pallas kernels  53 us (46%)
  starting transfers between devices  33 us (28%)
  waiting for transfers between devices  26.8 us (23%)
  local copies, waits for them, and re-layouts  1.74 us (2%)
    ppermute x31, starting transfers between devices, swap(): return lax.ppermute(value, axis, [(i, i ^ distance) for i in range(size)])  33 us
    ppermute x31, waiting for transfers between devices, swap(): return lax.ppermute(value, axis, [(i, i ^ distance) for i in range(size)])  26.8 us
    pallas_call x3, Pallas kernels, load(): pl.pallas_call(functools.partial(load_kernel, starts, orders), out_shape=...  22.3 us
    pallas_call x2, Pallas kernels, project(): pl.pallas_call(functools.partial(project_kernel, top, group, rows, owners...  20 us
    pallas_call x1, Pallas kernels, down(): pl.pallas_call(down_kernel, out_shape=jax.ShapeDtypeStruct((total, column...  3.63 us
    pallas_call x2, Pallas kernels, finish(): pl.pallas_call(functools.partial(finish_kernel, count, len(others) + 1, s...  3.53 us
  transfers between devices with their start and end apart: 31, of which 15 were waited for; matrix products, arithmetic and copies ran while one was open for 0% of the time, Pallas kernels for 35%

profile of v2, /device:TPU:0, one launch (start us, length us, event | category | flops | bytes accessed | tf_op | source)
XLA Modules:
  0.0 115.8 jit_solution(9448257026196118288)
XLA Ops:
  0.0 1.8 %pack.1.refs_1_.refs_0_ = bf16[64,1920]{1,0:T(8,128)(2,1)} custom-call(bf16[64,1792]{1,0:T(8,128)(2,1)} %tokens.1, s32[8,64]{1,0:T(8,128)} %bitcast.5, f32[8,64]{1,0:T(8,128)} %bitcast.6), custom_call_target="tpu_custom_call" | custom-call | tf_op jit(solution)/shard_map/pack/pallas_call | solution.py:106
  1.8 4.0 %collective-permute-start.3 = (bf16[64,1920]{1,0:T(8,128)(2,1)}, bf16[64,1920]{1,0:T(8,128)(2,1)S(1)}, u32[]{:S(2)}, u32[]{:S(2)}) collective-permute-start(bf16[64,1920]{1,0:T(8,128)(2,1)} %pack.1.refs_1_.refs_0_), channel_id=1, source_target_pairs={{0,4},{1,5},{2,6},{3,7},{4,0},{5,1},{6,2},{7,3},{8,12},{9,13},{10,... | collective-permute-start | bytes 737288 | tf_op jit(solution)/shard_map/ppermute | solution.py:61
  5.9 2.5 %collective-permute-start.2 = (bf16[64,1920]{1,0:T(8,128)(2,1)}, bf16[64,1920]{1,0:T(8,128)(2,1)S(1)}, u32[]{:S(2)}, u32[]{:S(2)}) collective-permute-start(bf16[64,1920]{1,0:T(8,128)(2,1)} %pack.1.refs_1_.refs_0_), channel_id=1, source_target_pairs={{0,3},{1,2},{2,1},{3,0},{4,7},{5,6},{6,5},{7,4},{8,11},{9,10},{10,... | collective-permute-start | bytes 737288 | tf_op jit(solution)/shard_map/ppermute | solution.py:61
  10.4 5.8 %load.3 = (bf16[4,1792,1024]{2,1,0:T(8,128)(2,1)S(1)}, f32[8,128]{1,0:T(8,128)S(1)}) custom-call(s32[3]{0:T(128)S(1)} %pad_add_fusion.1.place, bf16[8,1792,1024]{2,1,0:T(8,128)(2,1)} %refs_8_.1, bf16[64,1920]{1,0:T(8,128)(2,1)S(1)} %copy-done), custom_call_target="tpu_custom_call" | custom-call | bytes 14680064 | tf_op jit(solution)/shard_map/load/pallas_call | solution.py:146
  17.4 1.7 %collective-permute-start.6 = (bf16[64,1920]{1,0:T(8,128)(2,1)S(1)}, bf16[64,1920]{1,0:T(8,128)(2,1)S(1)}, u32[]{:S(2)}, u32[]{:S(2)}) collective-permute-start(bf16[64,1920]{1,0:T(8,128)(2,1)S(1)} %collective-permute-done.3.refs_4_), channel_id=1, source_target_pairs={{0,3},{1,2},{2,1},{3,0},{4,7},{5,6},{6,5},{7,4},{8,11},{9,10},{10,... | collective-permute-start | bytes 737288 | tf_op jit(solution)/shard_map/ppermute | solution.py:61
  21.5 6.4 %load.4 = (bf16[4,1792,1024]{2,1,0:T(8,128)(2,1)S(1)}, f32[8,128]{1,0:T(8,128)}) custom-call(s32[3]{0:T(128)S(1)} %pad_add_fusion.1.place, bf16[8,1792,1024]{2,1,0:T(8,128)(2,1)} %refs_9_.1, f32[8,128]{1,0:T(8,128)S(1)} %get-tuple-element.57.refs_1_.refs_12_), custom_call_target="tpu_custom_call" | custom-call | bytes 14680064 | tf_op jit(solution)/shard_map/load/pallas_call | solution.py:146
  27.9 2.7 %collective-permute-done.6.refs_7_ = bf16[64,1920]{1,0:T(8,128)(2,1)S(1)} collective-permute-done((bf16[64,1920]{1,0:T(8,128)(2,1)S(1)}, bf16[64,1920]{1,0:T(8,128)(2,1)S(1)}, u32[]{:S(2)}, u32[]{:S(2)}) %collective-permute-start.6) | collective-permute-done | bytes 245792 | tf_op jit(solution)/shard_map/ppermute | solution.py:61
  30.6 3.8 %collective-permute-done.5.refs_6_ = bf16[64,1920]{1,0:T(8,128)(2,1)S(1)} collective-permute-done((bf16[64,1920]{1,0:T(8,128)(2,1)S(1)}, bf16[64,1920]{1,0:T(8,128)(2,1)S(1)}, u32[]{:S(2)}, u32[]{:S(2)}) %collective-permute-start.5) | collective-permute-done | bytes 245792 | tf_op jit(solution)/shard_map/ppermute | solution.py:61
  34.4 7.7 %project.2 = (bf16[2,80,2048]{2,1,0:T(8,128)(2,1)}, f32[80,2048]{1,0:T(8,128)S(1)}, f32[80,2048]{1,0:T(8,128)S(1)}, f32[80,128]{1,0:T(8,128)S(1)}, bf16[512,320]{1,0:T(8,128)(2,1)S(1)}) custom-call(s32[3]{0:T(128)S(1)} %pad_add_fusion.1.place, bf16[64,1920]{1,0:T(8,128)(2,1)S(1)} %copy-done.1, bf16[64,1920]{1,0:T(8,128)(2,1)S(1)} %collective-permute-done.refs_1_, ...), custom_call_target="tpu_custom_call" | custom-call | flops 2348810240 | bytes 29360128 | tf_op jit(solution)/shard_map/project/pallas_call | solution.py:280
  42.9 2.4 %collective-permute-done.7.refs_0_ = bf16[2,80,2048]{2,1,0:T(8,128)(2,1)} collective-permute-done((bf16[2,80,2048]{2,1,0:T(8,128)(2,1)}, bf16[2,80,2048]{2,1,0:T(8,128)(2,1)}, u32[]{:S(2)}, u32[]{:S(2)}) %collective-permute-start.7) | collective-permute-done | bytes 655392 | tf_op jit(solution)/shard_map/ppermute | solution.py:61
  46.6 1.6 %collective-permute-start.8 = (bf16[80,2048]{1,0:T(8,128)(2,1)S(1)}, bf16[80,2048]{1,0:T(8,128)(2,1)S(1)}, u32[]{:S(2)}, u32[]{:S(2)}) collective-permute-start(bf16[80,2048]{1,0:T(8,128)(2,1)S(1)} %get-tuple-element.62.refs_10_), channel_id=1, source_target_pairs={{0,16},{8,24},{16,0},{24,8},{1,17},{9,25},{17,1},{25,9},{2,18},{10... | collective-permute-start | bytes 983048 | tf_op jit(solution)/shard_map/ppermute | solution.py:61
  48.3 12.3 %project.3 = (bf16[2,80,2048]{2,1,0:T(8,128)(2,1)S(1)}, f32[80,2048]{1,0:T(8,128)S(1)}, f32[80,2048]{1,0:T(8,128)S(1)}, f32[80,128]{1,0:T(8,128)S(1)}, bf16[512,320]{1,0:T(8,128)(2,1)S(1)}) custom-call(s32[3]{0:T(128)S(1)} %pad_add_fusion.place, bf16[64,1920]{1,0:T(8,128)(2,1)S(1)} %copy-done.1, bf16[64,1920]{1,0:T(8,128)(2,1)S(1)} %collective-permute-done.refs_1_, ...), custom_call_target="tpu_custom_call" | custom-call | flops 2348810240 | bytes 29360128 | tf_op jit(solution)/shard_map/project/pallas_call | solution.py:280
  60.7 2.1 %collective-permute-done.9.refs_0_ = bf16[2,80,2048]{2,1,0:T(8,128)(2,1)S(1)} collective-permute-done((bf16[2,80,2048]{2,1,0:T(8,128)(2,1)S(1)}, bf16[2,80,2048]{2,1,0:T(8,128)(2,1)S(1)}, u32[]{:S(2)}, u32[]{:S(2)}) %collective-permute-start.9) | collective-permute-done | bytes 655392 | tf_op jit(solution)/shard_map/ppermute | solution.py:61
  63.7 1.6 %collective-permute-start.12 = (bf16[80,1024]{1,0:T(8,128)(2,1)S(1)}, bf16[80,1024]{1,0:T(8,128)(2,1)S(1)}, u32[]{:S(2)}, u32[]{:S(2)}) collective-permute-start(bf16[80,1024]{1,0:T(8,128)(2,1)S(1)} %activate.2.refs_0_), channel_id=1, source_target_pairs={{0,16},{8,24},{16,0},{24,8},{1,17},{9,25},{17,1},{25,9},{2,18},{10... | collective-permute-start | bytes 491528 | tf_op jit(solution)/shard_map/ppermute | solution.py:61
  65.3 10.0 %load.5 = (bf16[4,1024,1792]{2,1,0:T(8,128)(2,1)S(1)}, bf16[4,1024,1792]{2,1,0:T(8,128)(2,1)S(1)}, f32[8,128]{1,0:T(8,128)S(1)}) custom-call(s32[3]{0:T(128)S(1)} %pad_add_fusion.1.place, bf16[8,1024,1792]{2,1,0:T(8,128)(2,1)} %refs_1_.1, bf16[8,1024,1792]{2,1,0:T(8,128)(2,1)} %refs_1_.1, bf16[80,2048]{1,0:T(8,128)(2,1)S(1)} %get-tuple-element.68.refs_2_), custom_call_target="tpu_custom_call" | custom-call | bytes 29360128 | tf_op jit(solution)/shard_map/load/pallas_call | solution.py:146
  77.8 3.6 %down.1.refs_6_ = f32[512,1792]{1,0:T(8,128)S(1)} custom-call(bf16[80,1024]{1,0:T(8,128)(2,1)S(1)} %activate.2.refs_0_, bf16[80,1024]{1,0:T(8,128)(2,1)S(1)} %collective-permute-done.11.refs_1_, bf16[80,1024]{1,0:T(8,128)(2,1)S(1)} %collective-permute-done.12.refs_2_, bf16[80,1024]{1,0:T(8,128)(2,1)S(1)} %collective-permute-done.15.refs_3_, ...), custom_call_target="tpu_custom_call" | custom-call | flops 1761607680 | bytes 14680064 | tf_op jit(solution)/shard_map/down/pallas_call | solution.py:316
  81.4 1.8 %collective-permute-done.14.refs_2_ = bf16[80,1024]{1,0:T(8,128)(2,1)S(1)} collective-permute-done((bf16[80,1024]{1,0:T(8,128)(2,1)S(1)}, bf16[80,1024]{1,0:T(8,128)(2,1)S(1)}, u32[]{:S(2)}, u32[]{:S(2)}) %collective-permute-start.14) | collective-permute-done | bytes 163872 | tf_op jit(solution)/shard_map/ppermute | solution.py:61
  84.6 1.8 %finish.3 = (f32[64,896]{1,0:T(8,128)S(1)}, bf16[64,896]{1,0:T(8,128)(2,1)S(1)}, bf16[64,896]{1,0:T(8,128)(2,1)S(1)}, bf16[64,896]{1,0:T(8,128)(2,1)S(1)}, f32[6...) custom-call(bf16[80,1024]{1,0:T(8,128)(2,1)S(1)} %activate.3.refs_0_,, ...), custom_call_target="tpu_custom_call" | custom-call | flops 880803840 | bytes 7340032 | tf_op jit(solution)/shard_map/finish/pallas_call | solution.py:361
  91.9 1.8 %finish.2 = (f32[64,896]{1,0:T(8,128)S(1)}, bf16[64,896]{1,0:T(8,128)(2,1)S(1)}, bf16[64,896]{1,0:T(8,128)(2,1)S(1)}, bf16[64,896]{1,0:T(8,128)(2,1)S(1)}, f32[6...) custom-call(bf16[80,1024]{1,0:T(8,128)(2,1)S(1)} %activate.3.refs_0_,, ...), custom_call_target="tpu_custom_call" | custom-call | flops 880803840 | bytes 7340032 | tf_op jit(solution)/shard_map/finish/pallas_call | solution.py:361
  94.3 1.5 %collective-permute-start.21 = (bf16[64,896]{1,0:T(8,128)(2,1)S(1)}, bf16[64,896]{1,0:T(8,128)(2,1)S(1)}, u32[]{:S(2)}, u32[]{:S(2)}) collective-permute-start(bf16[64,896]{1,0:T(8,128)(2,1)S(1)} %get-tuple-element.93), channel_id=1, source_target_pairs={{0,2},{1,3},{2,0},{3,1},{4,6},{5,7},{6,4},{7,5},{8,10},{9,11},{10,... | collective-permute-start | bytes 344072 | tf_op jit(solution)/shard_map/ppermute | solution.py:61
  101.8 1.6 %collective-permute-done.22 = bf16[64,896]{1,0:T(8,128)(2,1)S(1)} collective-permute-done((bf16[64,896]{1,0:T(8,128)(2,1)S(1)}, bf16[64,896]{1,0:T(8,128)(2,1)S(1)}, u32[]{:S(2)}, u32[]{:S(2)}) %collective-permute-start.22) | collective-permute-done | bytes 114720 | tf_op jit(solution)/shard_map/ppermute | solution.py:61
  104.7 1.9 %collective-permute-start.18 = (bf16[64,896]{1,0:T(8,128)(2,1)S(1)}, bf16[64,896]{1,0:T(8,128)(2,1)S(1)}, u32[]{:S(2)}, u32[]{:S(2)}) collective-permute-start(bf16[64,896]{1,0:T(8,128)(2,1)S(1)} %get-tuple-element.89), channel_id=1, source_target_pairs={{0,2},{1,3},{2,0},{3,1},{4,6},{5,7},{6,4},{7,5},{8,10},{9,11},{10,... | collective-permute-start | bytes 344072 | tf_op jit(solution)/shard_map/ppermute | solution.py:61
  108.5 2.9 %collective-permute-done.30 = bf16[64,896]{1,0:T(8,128)(2,1)S(1)} collective-permute-done((bf16[64,896]{1,0:T(8,128)(2,1)S(1)}, bf16[64,896]{1,0:T(8,128)(2,1)S(1)}, u32[]{:S(2)}, u32[]{:S(2)}) %collective-permute-start.30) | collective-permute-done | bytes 114720 | tf_op jit(solution)/shard_map/ppermute | solution.py:61
  111.5 2.3 %collective-permute-done.18 = bf16[64,896]{1,0:T(8,128)(2,1)S(1)} collective-permute-done((bf16[64,896]{1,0:T(8,128)(2,1)S(1)}, bf16[64,896]{1,0:T(8,128)(2,1)S(1)}, u32[]{:S(2)}, u32[]{:S(2)}) %collective-permute-start.18) | collective-permute-done | bytes 114720 | tf_op jit(solution)/shard_map/ppermute | solution.py:61
  (66 shorter events, 29.9 us)
Async XLA Ops:
  1.8 15.6 %collective-permute-start.3 = (bf16[64,1920]{1,0:T(8,128)(2,1)}, bf16[64,1920]{1,0:T(8,128)(2,1)S(1)}, u32[]{:S(2)}, u32[]{:S(2)}) collective-permute-start(bf16[64,1920]{1,0:T(8,128)(2,1)} %pack.1.refs_1_.refs_0_), channel_id=1, source_target_pairs={{0,4},{1,5},{2,6},{3,7},{4,0},{5,1},{6,2},{7,3},{8,12},{9,13},{10,... | collective-permute-start | bytes 737288 | tf_op jit(solution)/shard_map/ppermute | solution.py:61
  5.9 14.5 %collective-permute-start.2 = (bf16[64,1920]{1,0:T(8,128)(2,1)}, bf16[64,1920]{1,0:T(8,128)(2,1)S(1)}, u32[]{:S(2)}, u32[]{:S(2)}) collective-permute-start(bf16[64,1920]{1,0:T(8,128)(2,1)} %pack.1.refs_1_.refs_0_), channel_id=1, source_target_pairs={{0,3},{1,2},{2,1},{3,0},{4,7},{5,6},{6,5},{7,4},{8,11},{9,10},{10,... | collective-permute-start | bytes 737288 | tf_op jit(solution)/shard_map/ppermute | solution.py:61
  8.4 19.5 %collective-permute-start.1 = (bf16[64,1920]{1,0:T(8,128)(2,1)}, bf16[64,1920]{1,0:T(8,128)(2,1)S(1)}, u32[]{:S(2)}, u32[]{:S(2)}) collective-permute-start(bf16[64,1920]{1,0:T(8,128)(2,1)} %pack.1.refs_1_.refs_0_), channel_id=1, source_target_pairs={{0,2},{1,3},{2,0},{3,1},{4,6},{5,7},{6,4},{7,5},{8,10},{9,11},{10,... | collective-permute-start | bytes 737288 | tf_op jit(solution)/shard_map/ppermute | solution.py:61
  8.8 19.1 %collective-permute-start = (bf16[64,1920]{1,0:T(8,128)(2,1)}, bf16[64,1920]{1,0:T(8,128)(2,1)S(1)}, u32[]{:S(2)}, u32[]{:S(2)}) collective-permute-start(bf16[64,1920]{1,0:T(8,128)(2,1)} %pack.1.refs_1_.refs_0_), channel_id=1, source_target_pairs={{0,1},{1,0},{2,3},{3,2},{4,5},{5,4},{6,7},{7,6},{8,9},{9,8},{10,11... | collective-permute-start | bytes 737288 | tf_op jit(solution)/shard_map/ppermute | solution.py:61
  17.4 13.2 %collective-permute-start.6 = (bf16[64,1920]{1,0:T(8,128)(2,1)S(1)}, bf16[64,1920]{1,0:T(8,128)(2,1)S(1)}, u32[]{:S(2)}, u32[]{:S(2)}) collective-permute-start(bf16[64,1920]{1,0:T(8,128)(2,1)S(1)} %collective-permute-done.3.refs_4_), channel_id=1, source_target_pairs={{0,3},{1,2},{2,1},{3,0},{4,7},{5,6},{6,5},{7,4},{8,11},{9,10},{10,... | collective-permute-start | bytes 737288 | tf_op jit(solution)/shard_map/ppermute | solution.py:61
  19.1 15.3 %collective-permute-start.5 = (bf16[64,1920]{1,0:T(8,128)(2,1)S(1)}, bf16[64,1920]{1,0:T(8,128)(2,1)S(1)}, u32[]{:S(2)}, u32[]{:S(2)}) collective-permute-start(bf16[64,1920]{1,0:T(8,128)(2,1)S(1)} %collective-permute-done.3.refs_4_), channel_id=1, source_target_pairs={{0,2},{1,3},{2,0},{3,1},{4,6},{5,7},{6,4},{7,5},{8,10},{9,11},{10,... | collective-permute-start | bytes 737288 | tf_op jit(solution)/shard_map/ppermute | solution.py:61
  20.4 14.0 %collective-permute-start.4 = (bf16[64,1920]{1,0:T(8,128)(2,1)S(1)}, bf16[64,1920]{1,0:T(8,128)(2,1)S(1)}, u32[]{:S(2)}, u32[]{:S(2)}) collective-permute-start(bf16[64,1920]{1,0:T(8,128)(2,1)S(1)} %collective-permute-done.3.refs_4_), channel_id=1, source_target_pairs={{0,1},{1,0},{2,3},{3,2},{4,5},{5,4},{6,7},{7,6},{8,9},{9,8},{10,11... | collective-permute-start | bytes 737288 | tf_op jit(solution)/shard_map/ppermute | solution.py:61
  46.6 14.0 %collective-permute-start.8 = (bf16[80,2048]{1,0:T(8,128)(2,1)S(1)}, bf16[80,2048]{1,0:T(8,128)(2,1)S(1)}, u32[]{:S(2)}, u32[]{:S(2)}) collective-permute-start(bf16[80,2048]{1,0:T(8,128)(2,1)S(1)} %get-tuple-element.62.refs_10_), channel_id=1, source_target_pairs={{0,16},{8,24},{16,0},{24,8},{1,17},{9,25},{17,1},{25,9},{2,18},{10... | collective-permute-start | bytes 983048 | tf_op jit(solution)/shard_map/ppermute | solution.py:61
  63.0 13.3 %collective-permute-start.10 = (bf16[80,2048]{1,0:T(8,128)(2,1)S(1)}, bf16[80,2048]{1,0:T(8,128)(2,1)S(1)}, u32[]{:S(2)}, u32[]{:S(2)}) collective-permute-start(bf16[80,2048]{1,0:T(8,128)(2,1)S(1)} %get-tuple-element.68.refs_2_), channel_id=1, source_target_pairs={{0,16},{8,24},{16,0},{24,8},{1,17},{9,25},{17,1},{25,9},{2,18},{10... | collective-permute-start | bytes 983048 | tf_op jit(solution)/shard_map/ppermute | solution.py:61
  63.7 12.7 %collective-permute-start.12 = (bf16[80,1024]{1,0:T(8,128)(2,1)S(1)}, bf16[80,1024]{1,0:T(8,128)(2,1)S(1)}, u32[]{:S(2)}, u32[]{:S(2)}) collective-permute-start(bf16[80,1024]{1,0:T(8,128)(2,1)S(1)} %activate.2.refs_0_), channel_id=1, source_target_pairs={{0,16},{8,24},{16,0},{24,8},{1,17},{9,25},{17,1},{25,9},{2,18},{10... | collective-permute-start | bytes 491528 | tf_op jit(solution)/shard_map/ppermute | solution.py:61
  65.3 11.0 %collective-permute-start.11 = (bf16[80,1024]{1,0:T(8,128)(2,1)S(1)}, bf16[80,1024]{1,0:T(8,128)(2,1)S(1)}, u32[]{:S(2)}, u32[]{:S(2)}) collective-permute-start(bf16[80,1024]{1,0:T(8,128)(2,1)S(1)} %activate.2.refs_0_), channel_id=1, source_target_pairs={{0,8},{8,0},{16,24},{24,16},{1,9},{9,1},{17,25},{25,17},{2,10},{10... | collective-permute-start | bytes 491528 | tf_op jit(solution)/shard_map/ppermute | solution.py:61
  76.5 6.7 %collective-permute-start.14 = (bf16[80,1024]{1,0:T(8,128)(2,1)S(1)}, bf16[80,1024]{1,0:T(8,128)(2,1)S(1)}, u32[]{:S(2)}, u32[]{:S(2)}) collective-permute-start(bf16[80,1024]{1,0:T(8,128)(2,1)S(1)} %activate.3.refs_0_), channel_id=1, source_target_pairs={{0,16},{8,24},{16,0},{24,8},{1,17},{9,25},{17,1},{25,9},{2,18},{10... | collective-permute-start | bytes 491528 | tf_op jit(solution)/shard_map/ppermute | solution.py:61
  86.3 7.3 %collective-permute-start.27 = (bf16[64,896]{1,0:T(8,128)(2,1)S(1)}, bf16[64,896]{1,0:T(8,128)(2,1)S(1)}, u32[]{:S(2)}, u32[]{:S(2)}) collective-permute-start(bf16[64,896]{1,0:T(8,128)(2,1)S(1)} %get-tuple-element.100), channel_id=1, source_target_pairs={{0,1},{1,0},{2,3},{3,2},{4,5},{5,4},{6,7},{7,6},{8,9},{9,8},{10,11... | collective-permute-start | bytes 344072 | tf_op jit(solution)/shard_map/ppermute | solution.py:61
  86.9 7.3 %collective-permute-start.28 = (bf16[64,896]{1,0:T(8,128)(2,1)S(1)}, bf16[64,896]{1,0:T(8,128)(2,1)S(1)}, u32[]{:S(2)}, u32[]{:S(2)}) collective-permute-start(bf16[64,896]{1,0:T(8,128)(2,1)S(1)} %get-tuple-element.101), channel_id=1, source_target_pairs={{0,2},{1,3},{2,0},{3,1},{4,6},{5,7},{6,4},{7,5},{8,10},{9,11},{10,... | collective-permute-start | bytes 344072 | tf_op jit(solution)/shard_map/ppermute | solution.py:61
  88.4 7.9 %collective-permute-start.29 = (bf16[64,896]{1,0:T(8,128)(2,1)S(1)}, bf16[64,896]{1,0:T(8,128)(2,1)S(1)}, u32[]{:S(2)}, u32[]{:S(2)}) collective-permute-start(bf16[64,896]{1,0:T(8,128)(2,1)S(1)} %get-tuple-element.102), channel_id=1, source_target_pairs={{0,3},{1,2},{2,1},{3,0},{4,7},{5,6},{6,5},{7,4},{8,11},{9,10},{10,... | collective-permute-start | bytes 344072 | tf_op jit(solution)/shard_map/ppermute | solution.py:61
  89.9 14.8 %collective-permute-start.24 = (bf16[64,896]{1,0:T(8,128)(2,1)S(1)}, bf16[64,896]{1,0:T(8,128)(2,1)S(1)}, u32[]{:S(2)}, u32[]{:S(2)}) collective-permute-start(bf16[64,896]{1,0:T(8,128)(2,1)S(1)} %get-tuple-element.96), channel_id=1, source_target_pairs={{0,1},{1,0},{2,3},{3,2},{4,5},{5,4},{6,7},{7,6},{8,9},{9,8},{10,11... | collective-permute-start | bytes 344072 | tf_op jit(solution)/shard_map/ppermute | solution.py:61
  90.4 16.1 %collective-permute-start.25 = (bf16[64,896]{1,0:T(8,128)(2,1)S(1)}, bf16[64,896]{1,0:T(8,128)(2,1)S(1)}, u32[]{:S(2)}, u32[]{:S(2)}) collective-permute-start(bf16[64,896]{1,0:T(8,128)(2,1)S(1)} %get-tuple-element.97), channel_id=1, source_target_pairs={{0,2},{1,3},{2,0},{3,1},{4,6},{5,7},{6,4},{7,5},{8,10},{9,11},{10,... | collective-permute-start | bytes 344072 | tf_op jit(solution)/shard_map/ppermute | solution.py:61
  96.4 7.1 %collective-permute-start.22 = (bf16[64,896]{1,0:T(8,128)(2,1)S(1)}, bf16[64,896]{1,0:T(8,128)(2,1)S(1)}, u32[]{:S(2)}, u32[]{:S(2)}) collective-permute-start(bf16[64,896]{1,0:T(8,128)(2,1)S(1)} %get-tuple-element.94), channel_id=1, source_target_pairs={{0,3},{1,2},{2,1},{3,0},{4,7},{5,6},{6,5},{7,4},{8,11},{9,10},{10,... | collective-permute-start | bytes 344072 | tf_op jit(solution)/shard_map/ppermute | solution.py:61
  99.2 8.0 %collective-permute-start.26 = (bf16[64,896]{1,0:T(8,128)(2,1)S(1)}, bf16[64,896]{1,0:T(8,128)(2,1)S(1)}, u32[]{:S(2)}, u32[]{:S(2)}) collective-permute-start(bf16[64,896]{1,0:T(8,128)(2,1)S(1)} %get-tuple-element.98), channel_id=1, source_target_pairs={{0,3},{1,2},{2,1},{3,0},{4,7},{5,6},{6,5},{7,4},{8,11},{9,10},{10,... | collective-permute-start | bytes 344072 | tf_op jit(solution)/shard_map/ppermute | solution.py:61
  100.7 10.8 %collective-permute-start.17 = (bf16[64,896]{1,0:T(8,128)(2,1)S(1)}, bf16[64,896]{1,0:T(8,128)(2,1)S(1)}, u32[]{:S(2)}, u32[]{:S(2)}) collective-permute-start(bf16[64,896]{1,0:T(8,128)(2,1)S(1)} %get-tuple-element.88), channel_id=1, source_target_pairs={{0,1},{1,0},{2,3},{3,2},{4,5},{5,4},{6,7},{7,6},{8,9},{9,8},{10,11... | collective-permute-start | bytes 344072 | tf_op jit(solution)/shard_map/ppermute | solution.py:61
  103.5 8.0 %collective-permute-start.30 = (bf16[64,896]{1,0:T(8,128)(2,1)S(1)}, bf16[64,896]{1,0:T(8,128)(2,1)S(1)}, u32[]{:S(2)}, u32[]{:S(2)}) collective-permute-start(bf16[64,896]{1,0:T(8,128)(2,1)S(1)} %add_convert_fusion.1), channel_id=1, source_target_pairs={{0,4},{1,5},{2,6},{3,7},{4,0},{5,1},{6,2},{7,3},{8,12},{9,13},{10,... | collective-permute-start | bytes 344072 | tf_op jit(solution)/shard_map/ppermute | solution.py:61
  104.7 9.1 %collective-permute-start.18 = (bf16[64,896]{1,0:T(8,128)(2,1)S(1)}, bf16[64,896]{1,0:T(8,128)(2,1)S(1)}, u32[]{:S(2)}, u32[]{:S(2)}) collective-permute-start(bf16[64,896]{1,0:T(8,128)(2,1)S(1)} %get-tuple-element.89), channel_id=1, source_target_pairs={{0,2},{1,3},{2,0},{3,1},{4,6},{5,7},{6,4},{7,5},{8,10},{9,11},{10,... | collective-permute-start | bytes 344072 | tf_op jit(solution)/shard_map/ppermute | solution.py:61
  106.6 8.4 %collective-permute-start.19 = (bf16[64,896]{1,0:T(8,128)(2,1)S(1)}, bf16[64,896]{1,0:T(8,128)(2,1)S(1)}, u32[]{:S(2)}, u32[]{:S(2)}) collective-permute-start(bf16[64,896]{1,0:T(8,128)(2,1)S(1)} %get-tuple-element.90), channel_id=1, source_target_pairs={{0,3},{1,2},{2,1},{3,0},{4,7},{5,6},{6,5},{7,4},{8,11},{9,10},{10,... | collective-permute-start | bytes 344072 | tf_op jit(solution)/shard_map/ppermute | solution.py:61
  107.2 7.9 %collective-permute-start.23 = (bf16[64,896]{1,0:T(8,128)(2,1)S(1)}, bf16[64,896]{1,0:T(8,128)(2,1)S(1)}, u32[]{:S(2)}, u32[]{:S(2)}) collective-permute-start(bf16[64,896]{1,0:T(8,128)(2,1)S(1)} %add_convert_fusion.3), channel_id=1, source_target_pairs={{0,4},{1,5},{2,6},{3,7},{4,0},{5,1},{6,2},{7,3},{8,12},{9,13},{10,... | collective-permute-start | bytes 344072 | tf_op jit(solution)/shard_map/ppermute | solution.py:61
  (11 other events, 58.2 us)

commit v3 on v2

--- a/solution.py
+++ b/solution.py
@@ -11,6 +11,8 @@
 CAP = 10
 NEAR = 4
 LANES = 128
+PIECES = 4
+BASE_VMEM = 5 * 2**20
 COLUMN_PARTS = 2
 
 
@@ -124,14 +126,17 @@
     for k in range(max(map(len, orders))):
         for i in range(count):
             if k < len(orders[i]):
-                copies.append(
-                    pltpu.make_async_copy(
-                        sources[i].at[starts[i] + (orders[i][k] ^ place[0])],
-                        targets[i].at[k],
-                        done.at[i, k],
+                expert = starts[i] + (orders[i][k] ^ place[0])
+                rows = targets[i].shape[1] // PIECES
+                for j in range(PIECES):
+                    copies.append(
+                        pltpu.make_async_copy(
+                            sources[i].at[expert, pl.ds(j * rows, rows)],
+                            targets[i].at[k, pl.ds(j * rows, rows)],
+                            done.at[i, k, j],
+                        )
                     )
-                )
-                copies[-1].start()
+                    copies[-1].start()
     token[...] = jnp.zeros_like(token)
     for copy in copies:
         copy.wait()
@@ -148,7 +153,7 @@
         out_shape=shapes + [jax.ShapeDtypeStruct((8, LANES), jnp.float32)],
         in_specs=[pl.BlockSpec(memory_space=pltpu.SMEM)] + in_hbm(count) + anywhere(1),
         out_specs=in_vmem(count + 1),
-        scratch_shapes=[pltpu.SemaphoreType.DMA((count, max(map(len, orders))))],
+        scratch_shapes=[pltpu.SemaphoreType.DMA((count, max(map(len, orders)), PIECES))],
         compiler_params=pltpu.CompilerParams(vmem_limit_bytes=2 * 2**20),
         cost_estimate=pl.CostEstimate(flops=0, bytes_accessed=size, transcendentals=0),
         name="load",
@@ -208,9 +213,15 @@
         slot = slot - jnp.where(number >= j * rows, rows, 0)
     one_hot = jnp.where(wide == slot.astype(jnp.float32), 1.0, 0.0).astype(jnp.bfloat16)
     slots[...] = one_hot
-    picked[...] = lax.dot_general(
-        one_hot, held[...], (((0,), (0,)), ((), ())), preferred_element_type=jnp.float32
-    ).astype(jnp.bfloat16)
+    step = 3 * LANES
+    for begin in range(0, held.shape[1], step):
+        end = min(begin + step, held.shape[1])
+        picked[:, begin:end] = lax.dot_general(
+            one_hot,
+            held[:, begin:end],
+            (((0,), (0,)), ((), ())),
+            preferred_element_type=jnp.float32,
+        ).astype(jnp.bfloat16)
     own = picked[:rows, depth:].astype(jnp.float32)
     weight = (own[:, top : 2 * top] + own[:, 2 * top : 3 * top]) + own[:, 3 * top : 4 * top]
     mine = (first + member).astype(jnp.float32)
@@ -218,89 +229,118 @@
     scale[...] = jnp.broadcast_to(weight, scale.shape)
 
 
-def project_kernel(top, group, rows, owners, ready, place, *refs):
+def project_kernel(top, group, rows, numbers, owners, stream, ahead, place, *refs):
+    refs = list(refs)
+
+    def take(count):
+        taken, refs[:count] = refs[:count], []
+        return taken
+
+    blocks, weights = take(owners), take(2)
+    near = weights[0].shape[0]
+    streamed = len(numbers) - near
+    far = take(2) if streamed or ahead else []
+    take(1)
     half = group // 2
-    blocks = refs[:owners]
-    near = refs[owners : owners + 2] if ready else ()
-    refs = refs[owners + len(near) :]
-    far, send, keeps = refs[:2], refs[3], refs[4 : 4 + half]
-    scale, slots, held, picked = refs[4 + half : 8 + half]
-    order = visiting(group)
+    send, keeps = take(1)[0], take(half)
+    scale, slots = take(2)
+    targets = take(2) if ahead else []
+    held, picked = take(2)
     copies = {}
-    if ready < group:
-        *buffers, done = refs[8 + half :]
-        for k in range(ready, group):
+    if streamed:
+        buffers, arrivals = take(2), take(1)[0]
+        for k in range(streamed):
             for i in range(2):
                 copies[i, k] = pltpu.make_async_copy(
-                    far[i].at[place[2] + (order[k] ^ place[0])],
-                    buffers[i].at[k - ready],
-                    done.at[i, k - ready],
+                    far[i].at[stream + (numbers[near + k] ^ place[0])],
+                    buffers[i].at[k],
+                    arrivals.at[i, k],
                 )
                 copies[i, k].start()
-    route(blocks, held, picked, scale, slots, place, top, group, rows)
-    depth, ff = far[0].shape[1:]
-    for k, number in enumerate(order):
+    waiting = []
+    if ahead:
+        fetched = take(1)[0]
         for i in range(2):
-            if k >= ready:
-                copies[i, k].wait()
-            part = jnp.dot(
-                picked[number * rows : (number + 1) * rows, :depth],
-                near[i][k] if k < ready else buffers[i][k - ready],
-                preferred_element_type=jnp.float32,
-            )
-            if number % 2:
-                send[number // 2, :, i * ff : (i + 1) * ff] = part.astype(send.dtype)
-            else:
-                keeps[number // 2][:, i * ff : (i + 1) * ff] = part
-
-
-def project(blocks, place, near, weights, after, top, group, rows):
-    ready = near[0].shape[0] if near else 0
+            for k in range(ahead):
+                waiting.append(
+                    pltpu.make_async_copy(
+                        far[i].at[stream + group + (numbers[k] ^ place[0])],
+                        targets[i].at[k],
+                        fetched.at[i, k],
+                    )
+                )
+                waiting[-1].start()
     depth, ff = weights[0].shape[1:]
+
+    @pl.when(place[0] >= 0)
+    def _():
+        route(blocks, held, picked, scale, slots, place, top, group, rows)
+        for k, number in enumerate(numbers):
+            for i in range(2):
+                if k >= near:
+                    copies[i, k - near].wait()
+                part = jnp.dot(
+                    picked[number * rows : (number + 1) * rows, :depth],
+                    weights[i][k] if k < near else buffers[i][k - near],
+                    preferred_element_type=jnp.float32,
+                )
+                if number % 2:
+                    send[number // 2, :, i * ff : (i + 1) * ff] = part.astype(send.dtype)
+                else:
+                    keeps[number // 2][:, i * ff : (i + 1) * ff] = part
+
+    for copy in waiting:
+        copy.wait()
+
+
+def project(blocks, place, weights, pair, stream, numbers, ahead, after, top, group, rows):
+    depth, ff = weights[0].shape[1:]
+    owners = len(blocks)
     tok_rows, wide = blocks[0].shape
-    owners = len(blocks)
     total = tok_rows * owners
     half = group // 2
-    out_shape = (
-        [jax.ShapeDtypeStruct((half, rows, 2 * ff), jnp.bfloat16)]
-        + [jax.ShapeDtypeStruct((rows, 2 * ff), jnp.float32)] * half
-        + [
-            jax.ShapeDtypeStruct((rows, LANES), jnp.float32),
-            jax.ShapeDtypeStruct((total, group * rows), jnp.bfloat16),
-        ]
-    )
+    streamed = len(numbers) - weights[0].shape[0]
+    pair = list(pair) if streamed or ahead else []
+    out_shape = [jax.ShapeDtypeStruct((half, rows, 2 * ff), jnp.bfloat16)]
+    out_shape += [jax.ShapeDtypeStruct((rows, 2 * ff), jnp.float32)] * half
+    out_shape += [
+        jax.ShapeDtypeStruct((rows, LANES), jnp.float32),
+        jax.ShapeDtypeStruct((total, group * rows), jnp.bfloat16),
+    ]
+    out_shape += [pltpu.VMEM((ahead, depth, ff), jnp.bfloat16)] * (2 * (ahead > 0))
     scratch = [
         pltpu.VMEM((total, wide), jnp.bfloat16),
         pltpu.VMEM((group * rows, wide), jnp.bfloat16),
     ]
-    streamed = group - ready
     if streamed:
         scratch += [pltpu.VMEM((streamed, depth, ff), jnp.bfloat16)] * 2
         scratch += [pltpu.SemaphoreType.DMA((2, streamed))]
-    outs = pl.pallas_call(
-        functools.partial(project_kernel, top, group, rows, owners, ready),
+    if ahead:
+        scratch += [pltpu.SemaphoreType.DMA((2, ahead))]
+    return pl.pallas_call(
+        functools.partial(project_kernel, top, group, rows, numbers, owners, stream, ahead),
         out_shape=out_shape,
         in_specs=[pl.BlockSpec(memory_space=pltpu.SMEM)]
-        + in_vmem(owners + len(near))
-        + in_hbm(2)
+        + in_vmem(owners + 2)
+        + in_hbm(len(pair))
         + anywhere(1),
         out_specs=in_vmem(len(out_shape)),
         scratch_shapes=scratch,
         compiler_params=pltpu.CompilerParams(
-            vmem_limit_bytes=8 * 2**20 + streamed * depth * ff * 4
+            vmem_limit_bytes=BASE_VMEM + streamed * depth * ff * 4
         ),
         cost_estimate=pl.CostEstimate(
-            flops=4 * group * rows * depth * ff,
-            bytes_accessed=4 * group * depth * ff,
+            flops=4 * len(numbers) * rows * depth * ff,
+            bytes_accessed=4 * len(numbers) * depth * ff,
             transcendentals=0,
         ),
         name="project",
-    )(place, *blocks, *map(resident, near), *map(distant, weights), after)
-    return outs[0], outs[1 : 1 + half], outs[-2], outs[-1]
-
-
-def down_kernel(*refs):
-    *hidden, weights, slots, _, total, result = refs
+    )(place, *blocks, *map(resident, weights), *map(distant, pair), after)
+
+
+def down_kernel(count, *refs):
+    hidden, weights, slots = refs[:count], refs[count], refs[count + 1]
+    total, result = refs[-2:]
     rows = hidden[0].shape[0]
     for k, part in enumerate(hidden):
         result[k * rows : (k + 1) * rows, :] = jnp.dot(
@@ -314,19 +354,19 @@
     count, columns = len(hidden), weights.shape[2]
     total = slots.shape[0]
     return pl.pallas_call(
-        down_kernel,
+        functools.partial(down_kernel, count),
         out_shape=jax.ShapeDtypeStruct((total, columns), jnp.float32),
-        in_specs=in_vmem(count + 2) + anywhere(1),
+        in_specs=in_vmem(count + 2) + anywhere(len(after)),
         out_specs=pl.BlockSpec(memory_space=pltpu.VMEM),
         scratch_shapes=[pltpu.VMEM((count * rows, columns), jnp.bfloat16)],
-        compiler_params=pltpu.CompilerParams(vmem_limit_bytes=8 * 2**20),
+        compiler_params=pltpu.CompilerParams(vmem_limit_bytes=6 * 2**20),
         cost_estimate=pl.CostEstimate(
             flops=2 * count * rows * columns * (ff + total),
             bytes_accessed=2 * count * ff * columns,
             transcendentals=0,
         ),
         name="down",
-    )(*hidden, resident(weights), slots, after)
+    )(*hidden, resident(weights), slots, *after)
 
 
 def finish_kernel(count, chunks, start, columns, *refs):
@@ -364,7 +404,7 @@
         in_specs=in_vmem(count + 2 + len(others)),
         out_specs=in_vmem(owners),
         scratch_shapes=[pltpu.VMEM((count * rows, columns), jnp.bfloat16)],
-        compiler_params=pltpu.CompilerParams(vmem_limit_bytes=8 * 2**20),
+        compiler_params=pltpu.CompilerParams(vmem_limit_bytes=6 * 2**20),
         cost_estimate=pl.CostEstimate(
             flops=2 * count * rows * columns * (ff + total),
             bytes_accessed=2 * count * ff * columns,
@@ -427,60 +467,80 @@
     own = pack(tokens, expert_ids, combine_weights)
     far_blocks = {far: swap(own, "expert", far) for far in range(NEAR, owners, NEAR)}
     near_blocks = {near: swap(own, "expert", near) for near in range(1, NEAR)}
-    (gate_ready,), token = load((w_gate,), (0,), (order,), places[0], own)
+    pair = (w_gate, w_up)
+    (gate_ready,), token = load((w_gate,), (0,), (order[:-1],), places[0], own)
     far_blocks, token = lax.optimization_barrier((far_blocks, token))
     blocks = {0: own} | near_blocks | far_blocks
     for far in far_blocks:
         for near in range(1, NEAR):
             blocks[far + near] = swap(blocks[far], "expert", near)
     ordered = [blocks[k] for k in range(owners)]
-    (up_ready,), _ = load((w_up,), (0,), (order,), places[0], token)
+    (up_ready,), token = load((w_up,), (0,), (order[:-1],), places[0], token)
+    weights = [gate_ready, up_ready]
 
     hidden, slots = [], []
+    natural = list(range(group))
     after = token
+    sends, keeps, scales = [], [], []
     for c in range(chunks):
-        near = (gate_ready, up_ready) if c == 0 else ()
-        send, keeps, scale, one_hot = project(
-            ordered, places[c], near, (w_gate, w_up), after, top, group, rows
+        ahead = 1 if c + 1 < chunks else 0
+        outs = project(
+            ordered, places[c], weights, pair, c * group, order, ahead, after, top, group, rows
         )
+        send, *kept, scale, one_hot = outs[: 3 + group // 2]
+        weights = outs[3 + group // 2 :]
+        sends.append(send)
+        keeps.append(kept)
+        scales.append(scale)
         slots.append(one_hot)
-        if c > 0:
-            send, arrived = lax.optimization_barrier((send, arrived))
-            hidden.append(spread(activate(base, arrived, old_scale), group))
-        parts, base = merge(swap(send, "dp", 1), keeps)
-        old_scale = scale
-        arrived = [swap(part, "dp", 2 * j) for j, part in enumerate(parts, 1)]
-        after = parts[0] if parts else base
-    starts = tuple(range(0, local_experts, group))
-    members = (list(range(group)),) * chunks
-    down_weights, token = load((w_down,) * chunks, starts, members, places[0], after)
-    arrived, hidden, token = lax.optimization_barrier((arrived, hidden, token))
-    last = spread(activate(base, arrived, old_scale), group)
+        after = scale
+    received = [swap(send, "dp", 1) for send in sends]
+    bases, arrived = [], []
+    for c in range(chunks):
+        parts, base = merge(received[c], keeps[c])
+        bases.append(base)
+        arrived.append([swap(part, "dp", 2 * j) for j, part in enumerate(parts, 1)])
+    after = parts[0] if parts else base
+    natural = list(range(group))
+    down_weights, tokens = [], []
+    for c in range(chunks):
+        loaded, token = load((w_down,), (c * group,), (natural,), places[0], after)
+        arrived[c], hidden, token = lax.optimization_barrier((arrived[c], hidden, token))
+        after = activate(bases[c], arrived[c], scales[c])
+        hidden.append(spread(after, group))
+        down_weights += loaded
+        tokens.append(token)
+    last = hidden.pop()
     hidden = [complete(gathered, group) for gathered in hidden]
-    others = [down(hidden[c], down_weights[c], slots[c], token) for c in range(chunks - 1)]
+    others = [down(hidden[c], down_weights[c], slots[c], tokens) for c in range(chunks - 1)]
     if others:
         last, others = lax.optimization_barrier((last, others))
     hidden.append(complete(last, group))
     columns = depth // COLUMN_PARTS
+    fars = range(NEAR, owners, NEAR)
+    nears = range(1, NEAR)
+    partials = [
+        finish(hidden[-1], down_weights[-1], slots[-1], others, start, columns, owners)
+        for start in range(0, depth, columns)
+    ]
+    passing = [
+        {far: [swap(partial[far + near], "expert", near) for near in nears] for far in fars}
+        for partial in partials
+    ]
+    own_parts, _ = lax.optimization_barrier(
+        ([partial[:NEAR] for partial in partials], partials[-1][NEAR:])
+    )
     done = []
-    for start in range(0, depth, columns):
-        partial = finish(
-            hidden[-1], down_weights[-1], slots[-1], others, start, columns, owners
-        )
-        total = partial[0]
-        sums = {}
-        for far in range(NEAR, owners, NEAR):
-            sums[far] = partial[far]
-            for near in range(1, NEAR):
-                sums[far] = sums[far] + swap(partial[far + near], "expert", near).astype(
-                    jnp.float32
-                )
-        for near in range(1, NEAR):
-            total = total + swap(partial[near], "expert", near).astype(jnp.float32)
-        for far in range(NEAR, owners, NEAR):
-            total = total + swap(sums[far].astype(jnp.bfloat16), "expert", far).astype(
-                jnp.float32
-            )
+    for partial, mine, received in zip(partials, own_parts, passing):
+        total = mine[0]
+        for near in nears:
+            total = total + swap(mine[near], "expert", near).astype(jnp.float32)
+        for far in fars:
+            part = partial[far]
+            for block in received[far]:
+                part = part + block.astype(jnp.float32)
+            part = swap(part.astype(jnp.bfloat16), "expert", far)
+            total = total + part.astype(jnp.float32)
         done.append(total.astype(jnp.bfloat16))
     return jnp.concatenate(done, axis=1)
 
@@ -498,6 +558,9 @@
         and owners * w_gate.shape[0] <= 256
         and 4 * expert_ids.shape[1] <= LANES
         and tokens.shape[1] % (COLUMN_PARTS * LANES) == 0
+        and tokens.shape[1] % (16 * PIECES) == 0
+        and w_gate.shape[2] % LANES == 0
+        and w_gate.shape[2] % (16 * PIECES) == 0
     )
 
 

time: 116 us -> 112 us (0.966)
  Pallas kernels: 53 us -> 47.8 us
  local copies, waits for them, and re-layouts: 1.74 us -> 5.11 us
  waiting for transfers between devices: 26.8 us -> 24.1 us
    unnamed x8, local copies, waits for them, and re-layouts: 1.74 us -> 5.11 us
    pallas_call x3, Pallas kernels: 23.6 us -> 20.4 us  [the longest x2 16.8 us: project(): pl.pallas_call(functools.partial(project_kernel, top, group, rows, number...]
    ppermute x31, waiting for transfers between devices: 26.8 us -> 24.1 us  [swap(): return lax.ppermute(value, axis, [(i, i ^ distance) for i in range(size)])]
    pallas_call x2, Pallas kernels: 1.48 us -> 0.3 us  [merge(): pl.pallas_call(functools.partial(merge_kernel, half), out_shape=[jax.Shap...]
    pallas_call x3 -> x4, Pallas kernels: 22.3 us -> 21.5 us  [load(): pl.pallas_call(functools.partial(load_kernel, starts, orders), out_shape=...]
  transfers between devices with their start and end apart: 31 -> 31, of which waited for: 15 -> 14; matrix products, arithmetic and copies ran while one was open for 0% -> 0% of each run, Pallas kernels for 35% -> 33%
where the time goes in v3:
time: 112 us
  Pallas kernels  47.8 us (43%)
  starting transfers between devices  33.6 us (30%)
  waiting for transfers between devices  24.1 us (22%)
  local copies, waits for them, and re-layouts  5.11 us (5%)
    ppermute x31, starting transfers between devices, swap(): return lax.ppermute(value, axis, [(i, i ^ distance) for i in range(size)])  33.6 us
    ppermute x31, waiting for transfers between devices, swap(): return lax.ppermute(value, axis, [(i, i ^ distance) for i in range(size)])  24.1 us
    pallas_call x4, Pallas kernels, load(): pl.pallas_call(functools.partial(load_kernel, starts, orders), out_shape=...  21.5 us
    pallas_call x2, Pallas kernels, project(): pl.pallas_call(functools.partial(project_kernel, top, group, rows, number...  16.8 us
    unnamed x8, local copies, waits for them, and re-layouts  5.11 us
    pallas_call x1, Pallas kernels, down(): pl.pallas_call(functools.partial(down_kernel, count), out_shape=jax.Shape...  3.62 us
    pallas_call x2, Pallas kernels, finish(): pl.pallas_call(functools.partial(finish_kernel, count, len(others) + 1, s...  3.53 us
  transfers between devices with their start and end apart: 31, of which 14 were waited for; matrix products, arithmetic and copies ran while one was open for 0% of the time, Pallas kernels for 33%

profile of v3, /device:TPU:0, one launch (start us, length us, event | category | flops | bytes accessed | tf_op | source)
XLA Modules:
  0.0 112.0 jit_solution(13625314699489965699)
XLA Ops:
  0.0 1.8 %pack.1.refs_1_.refs_0_ = bf16[64,1920]{1,0:T(8,128)(2,1)} custom-call(bf16[64,1792]{1,0:T(8,128)(2,1)} %tokens.1, s32[8,64]{1,0:T(8,128)} %bitcast.5, f32[8,64]{1,0:T(8,128)} %bitcast.6), custom_call_target="tpu_custom_call" | custom-call | tf_op jit(solution)/shard_map/pack/pallas_call | solution.py:108
  1.8 4.0 %collective-permute-start.3 = (bf16[64,1920]{1,0:T(8,128)(2,1)}, bf16[64,1920]{1,0:T(8,128)(2,1)S(1)}, u32[]{:S(2)}, u32[]{:S(2)}) collective-permute-start(bf16[64,1920]{1,0:T(8,128)(2,1)} %pack.1.refs_1_.refs_0_), channel_id=1, source_target_pairs={{0,4},{1,5},{2,6},{3,7},{4,0},{5,1},{6,2},{7,3},{8,12},{9,13},{10,... | collective-permute-start | bytes 737288 | tf_op jit(solution)/shard_map/ppermute | solution.py:63
  5.9 2.5 %collective-permute-start.2 = (bf16[64,1920]{1,0:T(8,128)(2,1)}, bf16[64,1920]{1,0:T(8,128)(2,1)S(1)}, u32[]{:S(2)}, u32[]{:S(2)}) collective-permute-start(bf16[64,1920]{1,0:T(8,128)(2,1)} %pack.1.refs_1_.refs_0_), channel_id=1, source_target_pairs={{0,3},{1,2},{2,1},{3,0},{4,7},{5,6},{6,5},{7,4},{8,11},{9,10},{10,... | collective-permute-start | bytes 737288 | tf_op jit(solution)/shard_map/ppermute | solution.py:63
  10.4 4.8 %load.4 = (bf16[3,1792,1024]{2,1,0:T(8,128)(2,1)S(1)}, f32[8,128]{1,0:T(8,128)S(1)}) custom-call(s32[3]{0:T(128)S(1)} %pad_add_fusion.1.place, bf16[8,1792,1024]{2,1,0:T(8,128)(2,1)} %refs_10_.3, bf16[64,1920]{1,0:T(8,128)(2,1)S(1)} %copy-done.2), custom_call_target="tpu_custom_call" | custom-call | bytes 11010048 | tf_op jit(solution)/shard_map/load/pallas_call | solution.py:151
  15.2 4.2 %copy-done = bf16[3,1792,1024]{2,1,0:T(8,128)(2,1)} copy-done((bf16[3,1792,1024]{2,1,0:T(8,128)(2,1)}, bf16[3,1792,1024]{2,1,0:T(8,128)(2,1)S(1)}, u32[]{:S(2)}) %copy-start) | copy-done | bytes 11010072
  19.4 2.5 %collective-permute-start.6 = (bf16[64,1920]{1,0:T(8,128)(2,1)S(1)}, bf16[64,1920]{1,0:T(8,128)(2,1)S(1)}, u32[]{:S(2)}, u32[]{:S(2)}) collective-permute-start(bf16[64,1920]{1,0:T(8,128)(2,1)S(1)} %collective-permute-done.3.refs_4_), channel_id=1, source_target_pairs={{0,3},{1,2},{2,1},{3,0},{4,7},{5,6},{6,5},{7,4},{8,11},{9,10},{10,... | collective-permute-start | bytes 737288 | tf_op jit(solution)/shard_map/ppermute | solution.py:63
  22.9 5.0 %load.5 = (bf16[3,1792,1024]{2,1,0:T(8,128)(2,1)S(1)}, f32[8,128]{1,0:T(8,128)S(1)}) custom-call(s32[3]{0:T(128)S(1)} %pad_add_fusion.1.place, bf16[8,1792,1024]{2,1,0:T(8,128)(2,1)} %refs_11_.3, f32[8,128]{1,0:T(8,128)S(1)} %get-tuple-element.69.refs_1_), custom_call_target="tpu_custom_call" | custom-call | bytes 11010048 | tf_op jit(solution)/shard_map/load/pallas_call | solution.py:151
  28.0 2.7 %collective-permute-done.6.refs_7_ = bf16[64,1920]{1,0:T(8,128)(2,1)S(1)} collective-permute-done((bf16[64,1920]{1,0:T(8,128)(2,1)S(1)}, bf16[64,1920]{1,0:T(8,128)(2,1)S(1)}, u32[]{:S(2)}, u32[]{:S(2)}) %collective-permute-start.6) | collective-permute-done | bytes 245792 | tf_op jit(solution)/shard_map/ppermute | solution.py:63
  30.6 3.8 %collective-permute-done.5.refs_6_ = bf16[64,1920]{1,0:T(8,128)(2,1)S(1)} collective-permute-done((bf16[64,1920]{1,0:T(8,128)(2,1)S(1)}, bf16[64,1920]{1,0:T(8,128)(2,1)S(1)}, u32[]{:S(2)}, u32[]{:S(2)}) %collective-permute-start.5) | collective-permute-done | bytes 245792 | tf_op jit(solution)/shard_map/ppermute | solution.py:63
  34.4 7.6 %project.2 = (bf16[2,80,2048]{2,1,0:T(8,128)(2,1)S(1)}, f32[80,2048]{1,0:T(8,128)S(1)}, f32[80,2048]{1,0:T(8,128)S(1)}, f32[80,128]{1,0:T(8,128)S(1)}, bf16[512,...) custom-call(s32[3]{0:T(128)S(1)} %pad_add_fusion.1.place, ...), custom_call_target="tpu_custom_call" | custom-call | flops 2348810240 | bytes 29360128 | tf_op jit(solution)/shard_map/project/pallas_call | solution.py:320
  42.1 9.2 %project.3 = (bf16[2,80,2048]{2,1,0:T(8,128)(2,1)S(1)}, f32[80,2048]{1,0:T(8,128)S(1)}, f32[80,2048]{1,0:T(8,128)S(1)}, f32[80,128]{1,0:T(8,128)S(1)}, bf16[512,320]{1,0:T(8,128)(2,1)S(1)}) custom-call(s32[3]{0:T(128)S(1)} %pad_add_fusion.place, bf16[64,1920]{1,0:T(8,128)(2,1)S(1)} %copy-done.3, bf16[64,1920]{1,0:T(8,128)(2,1)S(1)} %collective-permute-done.refs_1_, ...), custom_call_target="tpu_custom_call" | custom-call | flops 2348810240 | bytes 29360128 | tf_op jit(solution)/shard_map/project/pallas_call | solution.py:320
  51.8 1.6 %collective-permute-start.10 = (bf16[80,2048]{1,0:T(8,128)(2,1)S(1)}, bf16[80,2048]{1,0:T(8,128)(2,1)S(1)}, u32[]{:S(2)}, u32[]{:S(2)}) collective-permute-start(bf16[80,2048]{1,0:T(8,128)(2,1)S(1)} %get-tuple-element.84), channel_id=1, source_target_pairs={{0,16},{8,24},{16,0},{24,8},{1,17},{9,25},{17,1},{25,9},{2,18},{10... | collective-permute-start | bytes 983048 | tf_op jit(solution)/shard_map/ppermute | solution.py:63
  53.6 1.5 %collective-permute-start.8 = (bf16[80,2048]{1,0:T(8,128)(2,1)S(1)}, bf16[80,2048]{1,0:T(8,128)(2,1)S(1)}, u32[]{:S(2)}, u32[]{:S(2)}) collective-permute-start(bf16[80,2048]{1,0:T(8,128)(2,1)S(1)} %get-tuple-element.79.refs_1_), channel_id=1, source_target_pairs={{0,16},{8,24},{16,0},{24,8},{1,17},{9,25},{17,1},{25,9},{2,18},{10... | collective-permute-start | bytes 983048 | tf_op jit(solution)/shard_map/ppermute | solution.py:63
  55.2 5.9 %load.6 = (bf16[4,1024,1792]{2,1,0:T(8,128)(2,1)S(1)}, f32[8,128]{1,0:T(8,128)S(1)}) custom-call(s32[3]{0:T(128)S(1)} %pad_add_fusion.1.place, bf16[8,1024,1792]{2,1,0:T(8,128)(2,1)} %refs_0_.7, bf16[80,2048]{1,0:T(8,128)(2,1)S(1)} %get-tuple-element.79.refs_1_), custom_call_target="tpu_custom_call" | custom-call | bytes 14680064 | tf_op jit(solution)/shard_map/load/pallas_call | solution.py:151
  62.5 1.7 %collective-permute-start.12 = (bf16[80,1024]{1,0:T(8,128)(2,1)S(1)}, bf16[80,1024]{1,0:T(8,128)(2,1)S(1)}, u32[]{:S(2)}, u32[]{:S(2)}) collective-permute-start(bf16[80,1024]{1,0:T(8,128)(2,1)S(1)} %activate.2.refs_1_.refs_0_), channel_id=1, source_target_pairs={{0,16},{8,24},{16,0},{24,8},{1,17},{9,25},{17,1},{25,9},{2,18},{10... | collective-permute-start | bytes 491528 | tf_op jit(solution)/shard_map/ppermute | solution.py:63
  64.2 5.9 %load.7 = (bf16[4,1024,1792]{2,1,0:T(8,128)(2,1)S(1)}, f32[8,128]{1,0:T(8,128)S(1)}) custom-call(s32[3]{0:T(128)S(1)} %pad_add_fusion.1.place, bf16[8,1024,1792]{2,1,0:T(8,128)(2,1)} %refs_0_.7, bf16[80,1024]{1,0:T(8,128)(2,1)S(1)} %activate.2.refs_1_.refs_0_), custom_call_target="tpu_custom_call" | custom-call | bytes 14680064 | tf_op jit(solution)/shard_map/load/pallas_call | solution.py:151
  70.1 2.2 %collective-permute-done.12.refs_2_ = bf16[80,1024]{1,0:T(8,128)(2,1)S(1)} collective-permute-done((bf16[80,1024]{1,0:T(8,128)(2,1)S(1)}, bf16[80,1024]{1,0:T(8,128)(2,1)S(1)}, u32[]{:S(2)}, u32[]{:S(2)}) %collective-permute-start.12) | collective-permute-done | bytes 163872 | tf_op jit(solution)/shard_map/ppermute | solution.py:63
  74.1 3.6 %down.1.refs_6_ = f32[512,1792]{1,0:T(8,128)S(1)} custom-call(bf16[80,1024]{1,0:T(8,128)(2,1)S(1)} %activate.2.refs_1_.refs_0_, bf16[80,1024]{1,0:T(8,128)(2,1)S(1)} %collective-permute-done.11.refs_1_, bf16[80,1024]{1,0:T(8,128)(2,1)S(1)} %collective-permute-done.12.refs_2_, bf16[80,1024]{1,0:T(8,128)(2,1)S(1)} %collective-permute-done.15.refs_3_, ...), custom_call_target="tpu_custom_call" | custom-call | flops 1761607680 | bytes 14680064 | tf_op jit(solution)/shard_map/down/pallas_call | solution.py:356
  80.5 1.8 %finish.2 = (f32[64,896]{1,0:T(8,128)S(1)}, bf16[64,896]{1,0:T(8,128)(2,1)S(1)}, bf16[64,896]{1,0:T(8,128)(2,1)S(1)}, bf16[64,896]{1,0:T(8,128)(2,1)S(1)}, f32[6...) custom-call(bf16[80,1024]{1,0:T(8,128)(2,1)S(1)} %activate.3.refs_0_,, ...), custom_call_target="tpu_custom_call" | custom-call | flops 880803840 | bytes 7340032 | tf_op jit(solution)/shard_map/finish/pallas_call | solution.py:401
  85.8 1.8 %finish.3 = (f32[64,896]{1,0:T(8,128)S(1)}, bf16[64,896]{1,0:T(8,128)(2,1)S(1)}, bf16[64,896]{1,0:T(8,128)(2,1)S(1)}, bf16[64,896]{1,0:T(8,128)(2,1)S(1)}, f32[6...) custom-call(bf16[80,1024]{1,0:T(8,128)(2,1)S(1)} %activate.3.refs_0_,, ...), custom_call_target="tpu_custom_call" | custom-call | flops 880803840 | bytes 7340032 | tf_op jit(solution)/shard_map/finish/pallas_call | solution.py:401
  93.3 1.9 %collective-permute-done.27 = bf16[64,896]{1,0:T(8,128)(2,1)S(1)} collective-permute-done((bf16[64,896]{1,0:T(8,128)(2,1)S(1)}, bf16[64,896]{1,0:T(8,128)(2,1)S(1)}, u32[]{:S(2)}, u32[]{:S(2)}) %collective-permute-start.27) | collective-permute-done | bytes 114720 | tf_op jit(solution)/shard_map/ppermute | solution.py:63
  97.4 2.2 %collective-permute-start.23 = (bf16[64,896]{1,0:T(8,128)(2,1)S(1)}, bf16[64,896]{1,0:T(8,128)(2,1)S(1)}, u32[]{:S(2)}, u32[]{:S(2)}) collective-permute-start(bf16[64,896]{1,0:T(8,128)(2,1)S(1)} %add_convert_fusion.3), channel_id=1, source_target_pairs={{0,4},{1,5},{2,6},{3,7},{4,0},{5,1},{6,2},{7,3},{8,12},{9,13},{10,... | collective-permute-start | bytes 344072 | tf_op jit(solution)/shard_map/ppermute | solution.py:63
  104.9 2.6 %collective-permute-done.25 = bf16[64,896]{1,0:T(8,128)(2,1)S(1)} collective-permute-done((bf16[64,896]{1,0:T(8,128)(2,1)S(1)}, bf16[64,896]{1,0:T(8,128)(2,1)S(1)}, u32[]{:S(2)}, u32[]{:S(2)}) %collective-permute-start.25) | collective-permute-done | bytes 114720 | tf_op jit(solution)/shard_map/ppermute | solution.py:63
  107.5 3.3 %collective-permute-done.26 = bf16[64,896]{1,0:T(8,128)(2,1)S(1)} collective-permute-done((bf16[64,896]{1,0:T(8,128)(2,1)S(1)}, bf16[64,896]{1,0:T(8,128)(2,1)S(1)}, u32[]{:S(2)}, u32[]{:S(2)}) %collective-permute-start.26) | collective-permute-done | bytes 114720 | tf_op jit(solution)/shard_map/ppermute | solution.py:63
  (67 shorter events, 27.8 us)
Async XLA Ops:
  1.8 17.5 %collective-permute-start.3 = (bf16[64,1920]{1,0:T(8,128)(2,1)}, bf16[64,1920]{1,0:T(8,128)(2,1)S(1)}, u32[]{:S(2)}, u32[]{:S(2)}) collective-permute-start(bf16[64,1920]{1,0:T(8,128)(2,1)} %pack.1.refs_1_.refs_0_), channel_id=1, source_target_pairs={{0,4},{1,5},{2,6},{3,7},{4,0},{5,1},{6,2},{7,3},{8,12},{9,13},{10,... | collective-permute-start | bytes 737288 | tf_op jit(solution)/shard_map/ppermute | solution.py:63
  5.9 16.4 %collective-permute-start.2 = (bf16[64,1920]{1,0:T(8,128)(2,1)}, bf16[64,1920]{1,0:T(8,128)(2,1)S(1)}, u32[]{:S(2)}, u32[]{:S(2)}) collective-permute-start(bf16[64,1920]{1,0:T(8,128)(2,1)} %pack.1.refs_1_.refs_0_), channel_id=1, source_target_pairs={{0,3},{1,2},{2,1},{3,0},{4,7},{5,6},{6,5},{7,4},{8,11},{9,10},{10,... | collective-permute-start | bytes 737288 | tf_op jit(solution)/shard_map/ppermute | solution.py:63
  8.4 19.6 %collective-permute-start.1 = (bf16[64,1920]{1,0:T(8,128)(2,1)}, bf16[64,1920]{1,0:T(8,128)(2,1)S(1)}, u32[]{:S(2)}, u32[]{:S(2)}) collective-permute-start(bf16[64,1920]{1,0:T(8,128)(2,1)} %pack.1.refs_1_.refs_0_), channel_id=1, source_target_pairs={{0,2},{1,3},{2,0},{3,1},{4,6},{5,7},{6,4},{7,5},{8,10},{9,11},{10,... | collective-permute-start | bytes 737288 | tf_op jit(solution)/shard_map/ppermute | solution.py:63
  8.8 19.1 %collective-permute-start = (bf16[64,1920]{1,0:T(8,128)(2,1)}, bf16[64,1920]{1,0:T(8,128)(2,1)S(1)}, u32[]{:S(2)}, u32[]{:S(2)}) collective-permute-start(bf16[64,1920]{1,0:T(8,128)(2,1)} %pack.1.refs_1_.refs_0_), channel_id=1, source_target_pairs={{0,1},{1,0},{2,3},{3,2},{4,5},{5,4},{6,7},{7,6},{8,9},{9,8},{10,11... | collective-permute-start | bytes 737288 | tf_op jit(solution)/shard_map/ppermute | solution.py:63
  19.4 11.3 %collective-permute-start.6 = (bf16[64,1920]{1,0:T(8,128)(2,1)S(1)}, bf16[64,1920]{1,0:T(8,128)(2,1)S(1)}, u32[]{:S(2)}, u32[]{:S(2)}) collective-permute-start(bf16[64,1920]{1,0:T(8,128)(2,1)S(1)} %collective-permute-done.3.refs_4_), channel_id=1, source_target_pairs={{0,3},{1,2},{2,1},{3,0},{4,7},{5,6},{6,5},{7,4},{8,11},{9,10},{10,... | collective-permute-start | bytes 737288 | tf_op jit(solution)/shard_map/ppermute | solution.py:63
  21.9 12.6 %collective-permute-start.5 = (bf16[64,1920]{1,0:T(8,128)(2,1)S(1)}, bf16[64,1920]{1,0:T(8,128)(2,1)S(1)}, u32[]{:S(2)}, u32[]{:S(2)}) collective-permute-start(bf16[64,1920]{1,0:T(8,128)(2,1)S(1)} %collective-permute-done.3.refs_4_), channel_id=1, source_target_pairs={{0,2},{1,3},{2,0},{3,1},{4,6},{5,7},{6,4},{7,5},{8,10},{9,11},{10,... | collective-permute-start | bytes 737288 | tf_op jit(solution)/shard_map/ppermute | solution.py:63
  22.3 12.1 %collective-permute-start.4 = (bf16[64,1920]{1,0:T(8,128)(2,1)S(1)}, bf16[64,1920]{1,0:T(8,128)(2,1)S(1)}, u32[]{:S(2)}, u32[]{:S(2)}) collective-permute-start(bf16[64,1920]{1,0:T(8,128)(2,1)S(1)} %collective-permute-done.3.refs_4_), channel_id=1, source_target_pairs={{0,1},{1,0},{2,3},{3,2},{4,5},{5,4},{6,7},{7,6},{8,9},{9,8},{10,11... | collective-permute-start | bytes 737288 | tf_op jit(solution)/shard_map/ppermute | solution.py:63
  42.1 9.6 %collective-permute-start.9 = (bf16[2,80,2048]{2,1,0:T(8,128)(2,1)S(1)}, bf16[2,80,2048]{2,1,0:T(8,128)(2,1)S(1)}, u32[]{:S(2)}, u32[]{:S(2)}) collective-permute-start(bf16[2,80,2048]{2,1,0:T(8,128)(2,1)S(1)} %get-tuple-element.80), channel_id=1, source_target_pairs={{0,8},{8,0},{16,24},{24,16},{1,9},{9,1},{17,25},{25,17},{2,10},{10... | collective-permute-start | bytes 1966088 | tf_op jit(solution)/shard_map/ppermute | solution.py:63
  51.8 10.6 %collective-permute-start.10 = (bf16[80,2048]{1,0:T(8,128)(2,1)S(1)}, bf16[80,2048]{1,0:T(8,128)(2,1)S(1)}, u32[]{:S(2)}, u32[]{:S(2)}) collective-permute-start(bf16[80,2048]{1,0:T(8,128)(2,1)S(1)} %get-tuple-element.84), channel_id=1, source_target_pairs={{0,16},{8,24},{16,0},{24,8},{1,17},{9,25},{17,1},{25,9},{2,18},{10... | collective-permute-start | bytes 983048 | tf_op jit(solution)/shard_map/ppermute | solution.py:63
  53.6 16.5 %collective-permute-start.8 = (bf16[80,2048]{1,0:T(8,128)(2,1)S(1)}, bf16[80,2048]{1,0:T(8,128)(2,1)S(1)}, u32[]{:S(2)}, u32[]{:S(2)}) collective-permute-start(bf16[80,2048]{1,0:T(8,128)(2,1)S(1)} %get-tuple-element.79.refs_1_), channel_id=1, source_target_pairs={{0,16},{8,24},{16,0},{24,8},{1,17},{9,25},{17,1},{25,9},{2,18},{10... | collective-permute-start | bytes 983048 | tf_op jit(solution)/shard_map/ppermute | solution.py:63
  62.5 9.7 %collective-permute-start.12 = (bf16[80,1024]{1,0:T(8,128)(2,1)S(1)}, bf16[80,1024]{1,0:T(8,128)(2,1)S(1)}, u32[]{:S(2)}, u32[]{:S(2)}) collective-permute-start(bf16[80,1024]{1,0:T(8,128)(2,1)S(1)} %activate.2.refs_1_.refs_0_), channel_id=1, source_target_pairs={{0,16},{8,24},{16,0},{24,8},{1,17},{9,25},{17,1},{25,9},{2,18},{10... | collective-permute-start | bytes 491528 | tf_op jit(solution)/shard_map/ppermute | solution.py:63
  64.2 8.1 %collective-permute-start.11 = (bf16[80,1024]{1,0:T(8,128)(2,1)S(1)}, bf16[80,1024]{1,0:T(8,128)(2,1)S(1)}, u32[]{:S(2)}, u32[]{:S(2)}) collective-permute-start(bf16[80,1024]{1,0:T(8,128)(2,1)S(1)} %activate.2.refs_1_.refs_0_), channel_id=1, source_target_pairs={{0,8},{8,0},{16,24},{24,16},{1,9},{9,1},{17,25},{25,17},{2,10},{10... | collective-permute-start | bytes 491528 | tf_op jit(solution)/shard_map/ppermute | solution.py:63
  82.2 7.5 %collective-permute-start.20 = (bf16[64,896]{1,0:T(8,128)(2,1)S(1)}, bf16[64,896]{1,0:T(8,128)(2,1)S(1)}, u32[]{:S(2)}, u32[]{:S(2)}) collective-permute-start(bf16[64,896]{1,0:T(8,128)(2,1)S(1)} %get-tuple-element.120), channel_id=1, source_target_pairs={{0,1},{1,0},{2,3},{3,2},{4,5},{5,4},{6,7},{7,6},{8,9},{9,8},{10,11... | collective-permute-start | bytes 344072 | tf_op jit(solution)/shard_map/ppermute | solution.py:63
  82.9 8.2 %collective-permute-start.21 = (bf16[64,896]{1,0:T(8,128)(2,1)S(1)}, bf16[64,896]{1,0:T(8,128)(2,1)S(1)}, u32[]{:S(2)}, u32[]{:S(2)}) collective-permute-start(bf16[64,896]{1,0:T(8,128)(2,1)S(1)} %get-tuple-element.121), channel_id=1, source_target_pairs={{0,2},{1,3},{2,0},{3,1},{4,6},{5,7},{6,4},{7,5},{8,10},{9,11},{10,... | collective-permute-start | bytes 344072 | tf_op jit(solution)/shard_map/ppermute | solution.py:63
  87.6 7.6 %collective-permute-start.27 = (bf16[64,896]{1,0:T(8,128)(2,1)S(1)}, bf16[64,896]{1,0:T(8,128)(2,1)S(1)}, u32[]{:S(2)}, u32[]{:S(2)}) collective-permute-start(bf16[64,896]{1,0:T(8,128)(2,1)S(1)} %get-tuple-element.112), channel_id=1, source_target_pairs={{0,1},{1,0},{2,3},{3,2},{4,5},{5,4},{6,7},{7,6},{8,9},{9,8},{10,11... | collective-permute-start | bytes 344072 | tf_op jit(solution)/shard_map/ppermute | solution.py:63
  88.2 8.4 %collective-permute-start.28 = (bf16[64,896]{1,0:T(8,128)(2,1)S(1)}, bf16[64,896]{1,0:T(8,128)(2,1)S(1)}, u32[]{:S(2)}, u32[]{:S(2)}) collective-permute-start(bf16[64,896]{1,0:T(8,128)(2,1)S(1)} %get-tuple-element.113), channel_id=1, source_target_pairs={{0,2},{1,3},{2,0},{3,1},{4,6},{5,7},{6,4},{7,5},{8,10},{9,11},{10,... | collective-permute-start | bytes 344072 | tf_op jit(solution)/shard_map/ppermute | solution.py:63
  89.7 7.7 %collective-permute-start.29 = (bf16[64,896]{1,0:T(8,128)(2,1)S(1)}, bf16[64,896]{1,0:T(8,128)(2,1)S(1)}, u32[]{:S(2)}, u32[]{:S(2)}) collective-permute-start(bf16[64,896]{1,0:T(8,128)(2,1)S(1)} %get-tuple-element.114), channel_id=1, source_target_pairs={{0,3},{1,2},{2,1},{3,0},{4,7},{5,6},{6,5},{7,4},{8,11},{9,10},{10,... | collective-permute-start | bytes 344072 | tf_op jit(solution)/shard_map/ppermute | solution.py:63
  91.1 9.2 %collective-permute-start.17 = (bf16[64,896]{1,0:T(8,128)(2,1)S(1)}, bf16[64,896]{1,0:T(8,128)(2,1)S(1)}, u32[]{:S(2)}, u32[]{:S(2)}) collective-permute-start(bf16[64,896]{1,0:T(8,128)(2,1)S(1)} %get-tuple-element.116), channel_id=1, source_target_pairs={{0,1},{1,0},{2,3},{3,2},{4,5},{5,4},{6,7},{7,6},{8,9},{9,8},{10,11... | collective-permute-start | bytes 344072 | tf_op jit(solution)/shard_map/ppermute | solution.py:63
  91.7 9.4 %collective-permute-start.18 = (bf16[64,896]{1,0:T(8,128)(2,1)S(1)}, bf16[64,896]{1,0:T(8,128)(2,1)S(1)}, u32[]{:S(2)}, u32[]{:S(2)}) collective-permute-start(bf16[64,896]{1,0:T(8,128)(2,1)S(1)} %get-tuple-element.117), channel_id=1, source_target_pairs={{0,2},{1,3},{2,0},{3,1},{4,6},{5,7},{6,4},{7,5},{8,10},{9,11},{10,... | collective-permute-start | bytes 344072 | tf_op jit(solution)/shard_map/ppermute | solution.py:63
  95.1 8.3 %collective-permute-start.19 = (bf16[64,896]{1,0:T(8,128)(2,1)S(1)}, bf16[64,896]{1,0:T(8,128)(2,1)S(1)}, u32[]{:S(2)}, u32[]{:S(2)}) collective-permute-start(bf16[64,896]{1,0:T(8,128)(2,1)S(1)} %get-tuple-element.118), channel_id=1, source_target_pairs={{0,3},{1,2},{2,1},{3,0},{4,7},{5,6},{6,5},{7,4},{8,11},{9,10},{10,... | collective-permute-start | bytes 344072 | tf_op jit(solution)/shard_map/ppermute | solution.py:63
  96.6 8.3 %collective-permute-start.24 = (bf16[64,896]{1,0:T(8,128)(2,1)S(1)}, bf16[64,896]{1,0:T(8,128)(2,1)S(1)}, u32[]{:S(2)}, u32[]{:S(2)}) collective-permute-start(bf16[64,896]{1,0:T(8,128)(2,1)S(1)} %get-tuple-element.124), channel_id=1, source_target_pairs={{0,1},{1,0},{2,3},{3,2},{4,5},{5,4},{6,7},{7,6},{8,9},{9,8},{10,11... | collective-permute-start | bytes 344072 | tf_op jit(solution)/shard_map/ppermute | solution.py:63
  97.4 7.4 %collective-permute-start.23 = (bf16[64,896]{1,0:T(8,128)(2,1)S(1)}, bf16[64,896]{1,0:T(8,128)(2,1)S(1)}, u32[]{:S(2)}, u32[]{:S(2)}) collective-permute-start(bf16[64,896]{1,0:T(8,128)(2,1)S(1)} %add_convert_fusion.3), channel_id=1, source_target_pairs={{0,4},{1,5},{2,6},{3,7},{4,0},{5,1},{6,2},{7,3},{8,12},{9,13},{10,... | collective-permute-start | bytes 344072 | tf_op jit(solution)/shard_map/ppermute | solution.py:63
  101.1 9.8 %collective-permute-start.26 = (bf16[64,896]{1,0:T(8,128)(2,1)S(1)}, bf16[64,896]{1,0:T(8,128)(2,1)S(1)}, u32[]{:S(2)}, u32[]{:S(2)}) collective-permute-start(bf16[64,896]{1,0:T(8,128)(2,1)S(1)} %get-tuple-element.126), channel_id=1, source_target_pairs={{0,3},{1,2},{2,1},{3,0},{4,7},{5,6},{6,5},{7,4},{8,11},{9,10},{10,... | collective-permute-start | bytes 344072 | tf_op jit(solution)/shard_map/ppermute | solution.py:63
  103.4 7.8 %collective-permute-start.30 = (bf16[64,896]{1,0:T(8,128)(2,1)S(1)}, bf16[64,896]{1,0:T(8,128)(2,1)S(1)}, u32[]{:S(2)}, u32[]{:S(2)}) collective-permute-start(bf16[64,896]{1,0:T(8,128)(2,1)S(1)} %add_convert_fusion.1), channel_id=1, source_target_pairs={{0,4},{1,5},{2,6},{3,7},{4,0},{5,1},{6,2},{7,3},{8,12},{9,13},{10,... | collective-permute-start | bytes 344072 | tf_op jit(solution)/shard_map/ppermute | solution.py:63
  (11 other events, 59.9 us)

commit v4 on v3

--- a/solution.py
+++ b/solution.py
@@ -112,6 +112,31 @@
         out_specs=pl.BlockSpec(memory_space=pltpu.VMEM),
         name="pack",
     )(tokens, expert_ids.T, combine_weights.T)
+
+
+def total_kernel(parts, *refs):
+    out = refs[-1]
+    count = (len(refs) - 1) // parts
+    columns = out.shape[1] // parts
+    for p in range(parts):
+        first, *others = refs[p * count : (p + 1) * count]
+        total = first[...]
+        for other in others:
+            total = total + other[...].astype(jnp.float32)
+        out[:, p * columns : (p + 1) * columns] = total.astype(out.dtype)
+
+
+def add_up(terms):
+    rows, columns = terms[0][0].shape
+    flat = [term for part in terms for term in part]
+    return pl.pallas_call(
+        functools.partial(total_kernel, len(terms)),
+        out_shape=jax.ShapeDtypeStruct((rows, columns * len(terms)), jnp.bfloat16),
+        in_specs=in_vmem(len(flat)),
+        out_specs=pl.BlockSpec(memory_space=pltpu.VMEM),
+        compiler_params=pltpu.CompilerParams(vmem_limit_bytes=8 * 2**20),
+        name="add_up",
+    )(*flat)
 
 
 def visiting(group):
@@ -532,17 +557,14 @@
     )
     done = []
     for partial, mine, received in zip(partials, own_parts, passing):
-        total = mine[0]
-        for near in nears:
-            total = total + swap(mine[near], "expert", near).astype(jnp.float32)
+        terms = [mine[0]] + [swap(mine[near], "expert", near) for near in nears]
         for far in fars:
             part = partial[far]
             for block in received[far]:
                 part = part + block.astype(jnp.float32)
-            part = swap(part.astype(jnp.bfloat16), "expert", far)
-            total = total + part.astype(jnp.float32)
-        done.append(total.astype(jnp.bfloat16))
-    return jnp.concatenate(done, axis=1)
+            terms.append(swap(part.astype(jnp.bfloat16), "expert", far))
+        done.append(terms)
+    return add_up(done)
 
 
 def fits(owners, group, tokens, expert_ids, w_gate):

time: 112 us -> 115 us (1.027)
  starting transfers between devices: 33.6 us -> 35.1 us
  waiting for transfers between devices: 24.1 us -> 25.4 us
    ppermute x31, starting transfers between devices: 33.6 us -> 35.1 us  [swap(): return lax.ppermute(value, axis, [(i, i ^ distance) for i in range(size)])]
    ppermute x31, waiting for transfers between devices: 24.1 us -> 25.4 us  [swap(): return lax.ppermute(value, axis, [(i, i ^ distance) for i in range(size)])]
  transfers between devices with their start and end apart: 31 -> 31, of which waited for: 14 -> 11; matrix products, arithmetic and copies ran while one was open for 0% -> 0% of each run, Pallas kernels for 33% -> 32%
where the time goes in v4:
time: 115 us
  Pallas kernels  48.7 us (42%)
  starting transfers between devices  35.1 us (31%)
  waiting for transfers between devices  25.4 us (22%)
  local copies, waits for them, and re-layouts  5.11 us (4%)
    ppermute x31, starting transfers between devices, swap(): return lax.ppermute(value, axis, [(i, i ^ distance) for i in range(size)])  35.1 us
    ppermute x31, waiting for transfers between devices, swap(): return lax.ppermute(value, axis, [(i, i ^ distance) for i in range(size)])  25.4 us
    pallas_call x4, Pallas kernels, load(): pl.pallas_call(functools.partial(load_kernel, starts, orders), out_shape=...  21.5 us
    pallas_call x2, Pallas kernels, project(): pl.pallas_call(functools.partial(project_kernel, top, group, rows, number...  16.8 us
    unnamed x8, local copies, waits for them, and re-layouts  5.11 us
    pallas_call x1, Pallas kernels, down(): pl.pallas_call(functools.partial(down_kernel, count), out_shape=jax.Shape...  3.62 us
    pallas_call x2, Pallas kernels, finish(): pl.pallas_call(functools.partial(finish_kernel, count, len(others) + 1, s...  3.53 us
  transfers between devices with their start and end apart: 31, of which 11 were waited for; matrix products, arithmetic and copies ran while one was open for 0% of the time, Pallas kernels for 32%

profile of v4, /device:TPU:0, one launch (start us, length us, event | category | flops | bytes accessed | tf_op | source)
XLA Modules:
  0.0 114.7 jit_solution(8948464137164762255)
XLA Ops:
  0.0 1.8 %pack.1.refs_1_.refs_0_ = bf16[64,1920]{1,0:T(8,128)(2,1)} custom-call(bf16[64,1792]{1,0:T(8,128)(2,1)} %tokens.1, s32[8,64]{1,0:T(8,128)} %bitcast.5, f32[8,64]{1,0:T(8,128)} %bitcast.6), custom_call_target="tpu_custom_call" | custom-call | tf_op jit(solution)/shard_map/pack/pallas_call | solution.py:108
  1.8 4.0 %collective-permute-start.3 = (bf16[64,1920]{1,0:T(8,128)(2,1)}, bf16[64,1920]{1,0:T(8,128)(2,1)S(1)}, u32[]{:S(2)}, u32[]{:S(2)}) collective-permute-start(bf16[64,1920]{1,0:T(8,128)(2,1)} %pack.1.refs_1_.refs_0_), channel_id=1, source_target_pairs={{0,4},{1,5},{2,6},{3,7},{4,0},{5,1},{6,2},{7,3},{8,12},{9,13},{10,... | collective-permute-start | bytes 737288 | tf_op jit(solution)/shard_map/ppermute | solution.py:63
  5.9 2.5 %collective-permute-start.2 = (bf16[64,1920]{1,0:T(8,128)(2,1)}, bf16[64,1920]{1,0:T(8,128)(2,1)S(1)}, u32[]{:S(2)}, u32[]{:S(2)}) collective-permute-start(bf16[64,1920]{1,0:T(8,128)(2,1)} %pack.1.refs_1_.refs_0_), channel_id=1, source_target_pairs={{0,3},{1,2},{2,1},{3,0},{4,7},{5,6},{6,5},{7,4},{8,11},{9,10},{10,... | collective-permute-start | bytes 737288 | tf_op jit(solution)/shard_map/ppermute | solution.py:63
  10.4 4.8 %load.4 = (bf16[3,1792,1024]{2,1,0:T(8,128)(2,1)S(1)}, f32[8,128]{1,0:T(8,128)S(1)}) custom-call(s32[3]{0:T(128)S(1)} %pad_add_fusion.1.place, bf16[8,1792,1024]{2,1,0:T(8,128)(2,1)} %refs_10_.3, bf16[64,1920]{1,0:T(8,128)(2,1)S(1)} %copy-done.2), custom_call_target="tpu_custom_call" | custom-call | bytes 11010048 | tf_op jit(solution)/shard_map/load/pallas_call | solution.py:176
  15.2 4.2 %copy-done = bf16[3,1792,1024]{2,1,0:T(8,128)(2,1)} copy-done((bf16[3,1792,1024]{2,1,0:T(8,128)(2,1)}, bf16[3,1792,1024]{2,1,0:T(8,128)(2,1)S(1)}, u32[]{:S(2)}) %copy-start) | copy-done | bytes 11010072
  19.4 2.5 %collective-permute-start.6 = (bf16[64,1920]{1,0:T(8,128)(2,1)S(1)}, bf16[64,1920]{1,0:T(8,128)(2,1)S(1)}, u32[]{:S(2)}, u32[]{:S(2)}) collective-permute-start(bf16[64,1920]{1,0:T(8,128)(2,1)S(1)} %collective-permute-done.3.refs_4_), channel_id=1, source_target_pairs={{0,3},{1,2},{2,1},{3,0},{4,7},{5,6},{6,5},{7,4},{8,11},{9,10},{10,... | collective-permute-start | bytes 737288 | tf_op jit(solution)/shard_map/ppermute | solution.py:63
  22.9 5.0 %load.5 = (bf16[3,1792,1024]{2,1,0:T(8,128)(2,1)S(1)}, f32[8,128]{1,0:T(8,128)S(1)}) custom-call(s32[3]{0:T(128)S(1)} %pad_add_fusion.1.place, bf16[8,1792,1024]{2,1,0:T(8,128)(2,1)} %refs_11_.3, f32[8,128]{1,0:T(8,128)S(1)} %get-tuple-element.69.refs_1_), custom_call_target="tpu_custom_call" | custom-call | bytes 11010048 | tf_op jit(solution)/shard_map/load/pallas_call | solution.py:176
  28.0 2.7 %collective-permute-done.6.refs_7_ = bf16[64,1920]{1,0:T(8,128)(2,1)S(1)} collective-permute-done((bf16[64,1920]{1,0:T(8,128)(2,1)S(1)}, bf16[64,1920]{1,0:T(8,128)(2,1)S(1)}, u32[]{:S(2)}, u32[]{:S(2)}) %collective-permute-start.6) | collective-permute-done | bytes 245792 | tf_op jit(solution)/shard_map/ppermute | solution.py:63
  30.6 3.8 %collective-permute-done.5.refs_6_ = bf16[64,1920]{1,0:T(8,128)(2,1)S(1)} collective-permute-done((bf16[64,1920]{1,0:T(8,128)(2,1)S(1)}, bf16[64,1920]{1,0:T(8,128)(2,1)S(1)}, u32[]{:S(2)}, u32[]{:S(2)}) %collective-permute-start.5) | collective-permute-done | bytes 245792 | tf_op jit(solution)/shard_map/ppermute | solution.py:63
  34.4 7.6 %project.2 = (bf16[2,80,2048]{2,1,0:T(8,128)(2,1)S(1)}, f32[80,2048]{1,0:T(8,128)S(1)}, f32[80,2048]{1,0:T(8,128)S(1)}, f32[80,128]{1,0:T(8,128)S(1)}, bf16[512,...) custom-call(s32[3]{0:T(128)S(1)} %pad_add_fusion.1.place, ...), custom_call_target="tpu_custom_call" | custom-call | flops 2348810240 | bytes 29360128 | tf_op jit(solution)/shard_map/project/pallas_call | solution.py:345
  42.1 9.2 %project.3 = (bf16[2,80,2048]{2,1,0:T(8,128)(2,1)S(1)}, f32[80,2048]{1,0:T(8,128)S(1)}, f32[80,2048]{1,0:T(8,128)S(1)}, f32[80,128]{1,0:T(8,128)S(1)}, bf16[512,320]{1,0:T(8,128)(2,1)S(1)}) custom-call(s32[3]{0:T(128)S(1)} %pad_add_fusion.place, bf16[64,1920]{1,0:T(8,128)(2,1)S(1)} %copy-done.3, bf16[64,1920]{1,0:T(8,128)(2,1)S(1)} %collective-permute-done.refs_1_, ...), custom_call_target="tpu_custom_call" | custom-call | flops 2348810240 | bytes 29360128 | tf_op jit(solution)/shard_map/project/pallas_call | solution.py:345
  51.8 1.6 %collective-permute-start.10 = (bf16[80,2048]{1,0:T(8,128)(2,1)S(1)}, bf16[80,2048]{1,0:T(8,128)(2,1)S(1)}, u32[]{:S(2)}, u32[]{:S(2)}) collective-permute-start(bf16[80,2048]{1,0:T(8,128)(2,1)S(1)} %get-tuple-element.84), channel_id=1, source_target_pairs={{0,16},{8,24},{16,0},{24,8},{1,17},{9,25},{17,1},{25,9},{2,18},{10... | collective-permute-start | bytes 983048 | tf_op jit(solution)/shard_map/ppermute | solution.py:63
  55.2 5.9 %load.6 = (bf16[4,1024,1792]{2,1,0:T(8,128)(2,1)S(1)}, f32[8,128]{1,0:T(8,128)S(1)}) custom-call(s32[3]{0:T(128)S(1)} %pad_add_fusion.1.place, bf16[8,1024,1792]{2,1,0:T(8,128)(2,1)} %refs_0_.7, bf16[80,2048]{1,0:T(8,128)(2,1)S(1)} %get-tuple-element.79.refs_1_), custom_call_target="tpu_custom_call" | custom-call | bytes 14680064 | tf_op jit(solution)/shard_map/load/pallas_call | solution.py:176
  62.5 1.7 %collective-permute-start.12 = (bf16[80,1024]{1,0:T(8,128)(2,1)S(1)}, bf16[80,1024]{1,0:T(8,128)(2,1)S(1)}, u32[]{:S(2)}, u32[]{:S(2)}) collective-permute-start(bf16[80,1024]{1,0:T(8,128)(2,1)S(1)} %activate.2.refs_1_.refs_0_), channel_id=1, source_target_pairs={{0,16},{8,24},{16,0},{24,8},{1,17},{9,25},{17,1},{25,9},{2,18},{10... | collective-permute-start | bytes 491528 | tf_op jit(solution)/shard_map/ppermute | solution.py:63
  64.2 5.9 %load.7 = (bf16[4,1024,1792]{2,1,0:T(8,128)(2,1)S(1)}, f32[8,128]{1,0:T(8,128)S(1)}) custom-call(s32[3]{0:T(128)S(1)} %pad_add_fusion.1.place, bf16[8,1024,1792]{2,1,0:T(8,128)(2,1)} %refs_0_.7, bf16[80,1024]{1,0:T(8,128)(2,1)S(1)} %activate.2.refs_1_.refs_0_), custom_call_target="tpu_custom_call" | custom-call | bytes 14680064 | tf_op jit(solution)/shard_map/load/pallas_call | solution.py:176
  70.1 2.2 %collective-permute-done.12.refs_2_ = bf16[80,1024]{1,0:T(8,128)(2,1)S(1)} collective-permute-done((bf16[80,1024]{1,0:T(8,128)(2,1)S(1)}, bf16[80,1024]{1,0:T(8,128)(2,1)S(1)}, u32[]{:S(2)}, u32[]{:S(2)}) %collective-permute-start.12) | collective-permute-done | bytes 163872 | tf_op jit(solution)/shard_map/ppermute | solution.py:63
  74.1 3.6 %down.1.refs_6_ = f32[512,1792]{1,0:T(8,128)S(1)} custom-call(bf16[80,1024]{1,0:T(8,128)(2,1)S(1)} %activate.2.refs_1_.refs_0_, bf16[80,1024]{1,0:T(8,128)(2,1)S(1)} %collective-permute-done.11.refs_1_, bf16[80,1024]{1,0:T(8,128)(2,1)S(1)} %collective-permute-done.12.refs_2_, bf16[80,1024]{1,0:T(8,128)(2,1)S(1)} %collective-permute-done.15.refs_3_, ...), custom_call_target="tpu_custom_call" | custom-call | flops 1761607680 | bytes 14680064 | tf_op jit(solution)/shard_map/down/pallas_call | solution.py:381
  80.5 1.8 %finish.3 = (f32[64,896]{1,0:T(8,128)S(1)}, bf16[64,896]{1,0:T(8,128)(2,1)S(1)}, bf16[64,896]{1,0:T(8,128)(2,1)S(1)}, bf16[64,896]{1,0:T(8,128)(2,1)S(1)}, f32[6...) custom-call(bf16[80,1024]{1,0:T(8,128)(2,1)S(1)} %activate.3.refs_0_,, ...), custom_call_target="tpu_custom_call" | custom-call | flops 880803840 | bytes 7340032 | tf_op jit(solution)/shard_map/finish/pallas_call | solution.py:426
  85.8 1.8 %finish.2 = (f32[64,896]{1,0:T(8,128)S(1)}, bf16[64,896]{1,0:T(8,128)(2,1)S(1)}, bf16[64,896]{1,0:T(8,128)(2,1)S(1)}, bf16[64,896]{1,0:T(8,128)(2,1)S(1)}, f32[6...) custom-call(bf16[80,1024]{1,0:T(8,128)(2,1)S(1)} %activate.3.refs_0_,, ...), custom_call_target="tpu_custom_call" | custom-call | flops 880803840 | bytes 7340032 | tf_op jit(solution)/shard_map/finish/pallas_call | solution.py:426
  93.3 3.9 %collective-permute-done.20 = bf16[64,896]{1,0:T(8,128)(2,1)S(1)} collective-permute-done((bf16[64,896]{1,0:T(8,128)(2,1)S(1)}, bf16[64,896]{1,0:T(8,128)(2,1)S(1)}, u32[]{:S(2)}, u32[]{:S(2)}) %collective-permute-start.20) | collective-permute-done | bytes 114720 | tf_op jit(solution)/shard_map/ppermute | solution.py:63
  100.7 1.6 %collective-permute-start.26 = (bf16[64,896]{1,0:T(8,128)(2,1)S(1)}, bf16[64,896]{1,0:T(8,128)(2,1)S(1)}, u32[]{:S(2)}, u32[]{:S(2)}) collective-permute-start(bf16[64,896]{1,0:T(8,128)(2,1)S(1)} %get-tuple-element.126), channel_id=1, source_target_pairs={{0,3},{1,2},{2,1},{3,0},{4,7},{5,6},{6,5},{7,4},{8,11},{9,10},{10,... | collective-permute-start | bytes 344072 | tf_op jit(solution)/shard_map/ppermute | solution.py:63
  105.5 3.3 %collective-permute-done.25.refs_7_ = bf16[64,896]{1,0:T(8,128)(2,1)S(1)} collective-permute-done((bf16[64,896]{1,0:T(8,128)(2,1)S(1)}, bf16[64,896]{1,0:T(8,128)(2,1)S(1)}, u32[]{:S(2)}, u32[]{:S(2)}) %collective-permute-start.25) | collective-permute-done | bytes 114720 | tf_op jit(solution)/shard_map/ppermute | solution.py:63
  108.8 2.8 %collective-permute-done.26.refs_8_ = bf16[64,896]{1,0:T(8,128)(2,1)S(1)} collective-permute-done((bf16[64,896]{1,0:T(8,128)(2,1)S(1)}, bf16[64,896]{1,0:T(8,128)(2,1)S(1)}, u32[]{:S(2)}, u32[]{:S(2)}) %collective-permute-start.26) | collective-permute-done | bytes 114720 | tf_op jit(solution)/shard_map/ppermute | solution.py:63
  111.7 2.2 %collective-permute-done.30.refs_9_ = bf16[64,896]{1,0:T(8,128)(2,1)S(1)} collective-permute-done((bf16[64,896]{1,0:T(8,128)(2,1)S(1)}, bf16[64,896]{1,0:T(8,128)(2,1)S(1)}, u32[]{:S(2)}, u32[]{:S(2)}) %collective-permute-start.30) | collective-permute-done | bytes 114720 | tf_op jit(solution)/shard_map/ppermute | solution.py:63
  (65 shorter events, 28.3 us)
Async XLA Ops:
  1.8 17.5 %collective-permute-start.3 = (bf16[64,1920]{1,0:T(8,128)(2,1)}, bf16[64,1920]{1,0:T(8,128)(2,1)S(1)}, u32[]{:S(2)}, u32[]{:S(2)}) collective-permute-start(bf16[64,1920]{1,0:T(8,128)(2,1)} %pack.1.refs_1_.refs_0_), channel_id=1, source_target_pairs={{0,4},{1,5},{2,6},{3,7},{4,0},{5,1},{6,2},{7,3},{8,12},{9,13},{10,... | collective-permute-start | bytes 737288 | tf_op jit(solution)/shard_map/ppermute | solution.py:63
  5.9 16.4 %collective-permute-start.2 = (bf16[64,1920]{1,0:T(8,128)(2,1)}, bf16[64,1920]{1,0:T(8,128)(2,1)S(1)}, u32[]{:S(2)}, u32[]{:S(2)}) collective-permute-start(bf16[64,1920]{1,0:T(8,128)(2,1)} %pack.1.refs_1_.refs_0_), channel_id=1, source_target_pairs={{0,3},{1,2},{2,1},{3,0},{4,7},{5,6},{6,5},{7,4},{8,11},{9,10},{10,... | collective-permute-start | bytes 737288 | tf_op jit(solution)/shard_map/ppermute | solution.py:63
  8.4 19.6 %collective-permute-start.1 = (bf16[64,1920]{1,0:T(8,128)(2,1)}, bf16[64,1920]{1,0:T(8,128)(2,1)S(1)}, u32[]{:S(2)}, u32[]{:S(2)}) collective-permute-start(bf16[64,1920]{1,0:T(8,128)(2,1)} %pack.1.refs_1_.refs_0_), channel_id=1, source_target_pairs={{0,2},{1,3},{2,0},{3,1},{4,6},{5,7},{6,4},{7,5},{8,10},{9,11},{10,... | collective-permute-start | bytes 737288 | tf_op jit(solution)/shard_map/ppermute | solution.py:63
  8.8 19.1 %collective-permute-start = (bf16[64,1920]{1,0:T(8,128)(2,1)}, bf16[64,1920]{1,0:T(8,128)(2,1)S(1)}, u32[]{:S(2)}, u32[]{:S(2)}) collective-permute-start(bf16[64,1920]{1,0:T(8,128)(2,1)} %pack.1.refs_1_.refs_0_), channel_id=1, source_target_pairs={{0,1},{1,0},{2,3},{3,2},{4,5},{5,4},{6,7},{7,6},{8,9},{9,8},{10,11... | collective-permute-start | bytes 737288 | tf_op jit(solution)/shard_map/ppermute | solution.py:63
  19.4 11.3 %collective-permute-start.6 = (bf16[64,1920]{1,0:T(8,128)(2,1)S(1)}, bf16[64,1920]{1,0:T(8,128)(2,1)S(1)}, u32[]{:S(2)}, u32[]{:S(2)}) collective-permute-start(bf16[64,1920]{1,0:T(8,128)(2,1)S(1)} %collective-permute-done.3.refs_4_), channel_id=1, source_target_pairs={{0,3},{1,2},{2,1},{3,0},{4,7},{5,6},{6,5},{7,4},{8,11},{9,10},{10,... | collective-permute-start | bytes 737288 | tf_op jit(solution)/shard_map/ppermute | solution.py:63
  21.9 12.6 %collective-permute-start.5 = (bf16[64,1920]{1,0:T(8,128)(2,1)S(1)}, bf16[64,1920]{1,0:T(8,128)(2,1)S(1)}, u32[]{:S(2)}, u32[]{:S(2)}) collective-permute-start(bf16[64,1920]{1,0:T(8,128)(2,1)S(1)} %collective-permute-done.3.refs_4_), channel_id=1, source_target_pairs={{0,2},{1,3},{2,0},{3,1},{4,6},{5,7},{6,4},{7,5},{8,10},{9,11},{10,... | collective-permute-start | bytes 737288 | tf_op jit(solution)/shard_map/ppermute | solution.py:63
  22.3 12.1 %collective-permute-start.4 = (bf16[64,1920]{1,0:T(8,128)(2,1)S(1)}, bf16[64,1920]{1,0:T(8,128)(2,1)S(1)}, u32[]{:S(2)}, u32[]{:S(2)}) collective-permute-start(bf16[64,1920]{1,0:T(8,128)(2,1)S(1)} %collective-permute-done.3.refs_4_), channel_id=1, source_target_pairs={{0,1},{1,0},{2,3},{3,2},{4,5},{5,4},{6,7},{7,6},{8,9},{9,8},{10,11... | collective-permute-start | bytes 737288 | tf_op jit(solution)/shard_map/ppermute | solution.py:63
  42.1 9.6 %collective-permute-start.9 = (bf16[2,80,2048]{2,1,0:T(8,128)(2,1)S(1)}, bf16[2,80,2048]{2,1,0:T(8,128)(2,1)S(1)}, u32[]{:S(2)}, u32[]{:S(2)}) collective-permute-start(bf16[2,80,2048]{2,1,0:T(8,128)(2,1)S(1)} %get-tuple-element.80), channel_id=1, source_target_pairs={{0,8},{8,0},{16,24},{24,16},{1,9},{9,1},{17,25},{25,17},{2,10},{10... | collective-permute-start | bytes 1966088 | tf_op jit(solution)/shard_map/ppermute | solution.py:63
  51.8 10.6 %collective-permute-start.10 = (bf16[80,2048]{1,0:T(8,128)(2,1)S(1)}, bf16[80,2048]{1,0:T(8,128)(2,1)S(1)}, u32[]{:S(2)}, u32[]{:S(2)}) collective-permute-start(bf16[80,2048]{1,0:T(8,128)(2,1)S(1)} %get-tuple-element.84), channel_id=1, source_target_pairs={{0,16},{8,24},{16,0},{24,8},{1,17},{9,25},{17,1},{25,9},{2,18},{10... | collective-permute-start | bytes 983048 | tf_op jit(solution)/shard_map/ppermute | solution.py:63
  53.6 16.5 %collective-permute-start.8 = (bf16[80,2048]{1,0:T(8,128)(2,1)S(1)}, bf16[80,2048]{1,0:T(8,128)(2,1)S(1)}, u32[]{:S(2)}, u32[]{:S(2)}) collective-permute-start(bf16[80,2048]{1,0:T(8,128)(2,1)S(1)} %get-tuple-element.79.refs_1_), channel_id=1, source_target_pairs={{0,16},{8,24},{16,0},{24,8},{1,17},{9,25},{17,1},{25,9},{2,18},{10... | collective-permute-start | bytes 983048 | tf_op jit(solution)/shard_map/ppermute | solution.py:63
  62.5 9.7 %collective-permute-start.12 = (bf16[80,1024]{1,0:T(8,128)(2,1)S(1)}, bf16[80,1024]{1,0:T(8,128)(2,1)S(1)}, u32[]{:S(2)}, u32[]{:S(2)}) collective-permute-start(bf16[80,1024]{1,0:T(8,128)(2,1)S(1)} %activate.2.refs_1_.refs_0_), channel_id=1, source_target_pairs={{0,16},{8,24},{16,0},{24,8},{1,17},{9,25},{17,1},{25,9},{2,18},{10... | collective-permute-start | bytes 491528 | tf_op jit(solution)/shard_map/ppermute | solution.py:63
  64.2 8.1 %collective-permute-start.11 = (bf16[80,1024]{1,0:T(8,128)(2,1)S(1)}, bf16[80,1024]{1,0:T(8,128)(2,1)S(1)}, u32[]{:S(2)}, u32[]{:S(2)}) collective-permute-start(bf16[80,1024]{1,0:T(8,128)(2,1)S(1)} %activate.2.refs_1_.refs_0_), channel_id=1, source_target_pairs={{0,8},{8,0},{16,24},{24,16},{1,9},{9,1},{17,25},{25,17},{2,10},{10... | collective-permute-start | bytes 491528 | tf_op jit(solution)/shard_map/ppermute | solution.py:63
  82.2 7.5 %collective-permute-start.27 = (bf16[64,896]{1,0:T(8,128)(2,1)S(1)}, bf16[64,896]{1,0:T(8,128)(2,1)S(1)}, u32[]{:S(2)}, u32[]{:S(2)}) collective-permute-start(bf16[64,896]{1,0:T(8,128)(2,1)S(1)} %get-tuple-element.112), channel_id=1, source_target_pairs={{0,1},{1,0},{2,3},{3,2},{4,5},{5,4},{6,7},{7,6},{8,9},{9,8},{10,11... | collective-permute-start | bytes 344072 | tf_op jit(solution)/shard_map/ppermute | solution.py:63
  82.9 7.3 %collective-permute-start.28 = (bf16[64,896]{1,0:T(8,128)(2,1)S(1)}, bf16[64,896]{1,0:T(8,128)(2,1)S(1)}, u32[]{:S(2)}, u32[]{:S(2)}) collective-permute-start(bf16[64,896]{1,0:T(8,128)(2,1)S(1)} %get-tuple-element.113), channel_id=1, source_target_pairs={{0,2},{1,3},{2,0},{3,1},{4,6},{5,7},{6,4},{7,5},{8,10},{9,11},{10,... | collective-permute-start | bytes 344072 | tf_op jit(solution)/shard_map/ppermute | solution.py:63
  84.4 7.3 %collective-permute-start.29 = (bf16[64,896]{1,0:T(8,128)(2,1)S(1)}, bf16[64,896]{1,0:T(8,128)(2,1)S(1)}, u32[]{:S(2)}, u32[]{:S(2)}) collective-permute-start(bf16[64,896]{1,0:T(8,128)(2,1)S(1)} %get-tuple-element.114), channel_id=1, source_target_pairs={{0,3},{1,2},{2,1},{3,0},{4,7},{5,6},{6,5},{7,4},{8,11},{9,10},{10,... | collective-permute-start | bytes 344072 | tf_op jit(solution)/shard_map/ppermute | solution.py:63
  87.6 13.1 %collective-permute-start.17 = (bf16[64,896]{1,0:T(8,128)(2,1)S(1)}, bf16[64,896]{1,0:T(8,128)(2,1)S(1)}, u32[]{:S(2)}, u32[]{:S(2)}) collective-permute-start(bf16[64,896]{1,0:T(8,128)(2,1)S(1)} %get-tuple-element.116), channel_id=1, source_target_pairs={{0,1},{1,0},{2,3},{3,2},{4,5},{5,4},{6,7},{7,6},{8,9},{9,8},{10,11... | collective-permute-start | bytes 344072 | tf_op jit(solution)/shard_map/ppermute | solution.py:63
  88.2 14.1 %collective-permute-start.18 = (bf16[64,896]{1,0:T(8,128)(2,1)S(1)}, bf16[64,896]{1,0:T(8,128)(2,1)S(1)}, u32[]{:S(2)}, u32[]{:S(2)}) collective-permute-start(bf16[64,896]{1,0:T(8,128)(2,1)S(1)} %get-tuple-element.117), channel_id=1, source_target_pairs={{0,2},{1,3},{2,0},{3,1},{4,6},{5,7},{6,4},{7,5},{8,10},{9,11},{10,... | collective-permute-start | bytes 344072 | tf_op jit(solution)/shard_map/ppermute | solution.py:63
  89.7 7.5 %collective-permute-start.20 = (bf16[64,896]{1,0:T(8,128)(2,1)S(1)}, bf16[64,896]{1,0:T(8,128)(2,1)S(1)}, u32[]{:S(2)}, u32[]{:S(2)}) collective-permute-start(bf16[64,896]{1,0:T(8,128)(2,1)S(1)} %get-tuple-element.120), channel_id=1, source_target_pairs={{0,1},{1,0},{2,3},{3,2},{4,5},{5,4},{6,7},{7,6},{8,9},{9,8},{10,11... | collective-permute-start | bytes 344072 | tf_op jit(solution)/shard_map/ppermute | solution.py:63
  90.2 8.4 %collective-permute-start.21 = (bf16[64,896]{1,0:T(8,128)(2,1)S(1)}, bf16[64,896]{1,0:T(8,128)(2,1)S(1)}, u32[]{:S(2)}, u32[]{:S(2)}) collective-permute-start(bf16[64,896]{1,0:T(8,128)(2,1)S(1)} %get-tuple-element.121), channel_id=1, source_target_pairs={{0,2},{1,3},{2,0},{3,1},{4,6},{5,7},{6,4},{7,5},{8,10},{9,11},{10,... | collective-permute-start | bytes 344072 | tf_op jit(solution)/shard_map/ppermute | solution.py:63
  91.7 7.5 %collective-permute-start.22 = (bf16[64,896]{1,0:T(8,128)(2,1)S(1)}, bf16[64,896]{1,0:T(8,128)(2,1)S(1)}, u32[]{:S(2)}, u32[]{:S(2)}) collective-permute-start(bf16[64,896]{1,0:T(8,128)(2,1)S(1)} %get-tuple-element.122), channel_id=1, source_target_pairs={{0,3},{1,2},{2,1},{3,0},{4,7},{5,6},{6,5},{7,4},{8,11},{9,10},{10,... | collective-permute-start | bytes 344072 | tf_op jit(solution)/shard_map/ppermute | solution.py:63
  99.2 9.7 %collective-permute-start.25 = (bf16[64,896]{1,0:T(8,128)(2,1)S(1)}, bf16[64,896]{1,0:T(8,128)(2,1)S(1)}, u32[]{:S(2)}, u32[]{:S(2)}) collective-permute-start(bf16[64,896]{1,0:T(8,128)(2,1)S(1)} %get-tuple-element.125), channel_id=1, source_target_pairs={{0,2},{1,3},{2,0},{3,1},{4,6},{5,7},{6,4},{7,5},{8,10},{9,11},{10,... | collective-permute-start | bytes 344072 | tf_op jit(solution)/shard_map/ppermute | solution.py:63
  100.7 11.0 %collective-permute-start.26 = (bf16[64,896]{1,0:T(8,128)(2,1)S(1)}, bf16[64,896]{1,0:T(8,128)(2,1)S(1)}, u32[]{:S(2)}, u32[]{:S(2)}) collective-permute-start(bf16[64,896]{1,0:T(8,128)(2,1)S(1)} %get-tuple-element.126), channel_id=1, source_target_pairs={{0,3},{1,2},{2,1},{3,0},{4,7},{5,6},{6,5},{7,4},{8,11},{9,10},{10,... | collective-permute-start | bytes 344072 | tf_op jit(solution)/shard_map/ppermute | solution.py:63
  102.3 9.4 %collective-permute-start.23 = (bf16[64,896]{1,0:T(8,128)(2,1)S(1)}, bf16[64,896]{1,0:T(8,128)(2,1)S(1)}, u32[]{:S(2)}, u32[]{:S(2)}) collective-permute-start(bf16[64,896]{1,0:T(8,128)(2,1)S(1)} %add_convert_fusion.1), channel_id=1, source_target_pairs={{0,4},{1,5},{2,6},{3,7},{4,0},{5,1},{6,2},{7,3},{8,12},{9,13},{10,... | collective-permute-start | bytes 344072 | tf_op jit(solution)/shard_map/ppermute | solution.py:63
  104.1 9.8 %collective-permute-start.30 = (bf16[64,896]{1,0:T(8,128)(2,1)S(1)}, bf16[64,896]{1,0:T(8,128)(2,1)S(1)}, u32[]{:S(2)}, u32[]{:S(2)}) collective-permute-start(bf16[64,896]{1,0:T(8,128)(2,1)S(1)} %add_convert_fusion), channel_id=1, source_target_pairs={{0,4},{1,5},{2,6},{3,7},{4,0},{5,1},{6,2},{7,3},{8,12},{9,13},{10,... | collective-permute-start | bytes 344072 | tf_op jit(solution)/shard_map/ppermute | solution.py:63
  (11 other events, 59.2 us)
